TPU v7x, 32 devices: a whole 2x2x4 slice. The times are simulated.
32 devices in a mesh: dp: 4 (over y, x), tp: 8 (over z, core).
Axes of the slice: x: 2, y: 2, z: 4, core: 2. Of those that a mesh axis runs over, the one named last changes fastest.
Arguments:
- hidden: bfloat16 [768, 2880], P(('dp', 'tp')), parts along dimension 0, may hold values from -6 to 6
- attn_gain: float32 [2880], replicated, may hold values from 0.1 to 1.9
- w_query: bfloat16 [2880, 4096], P(None, 'tp'), may hold values from -0.109375 to 0.109375
- w_keyval: bfloat16 [2880, 1024], P(None, 'tp'), may hold values from -0.109375 to 0.109375
- w_out: bfloat16 [4096, 2880], P('tp'), may hold values from -0.09375 to 0.09375
- cache_keys: bfloat16 [32, 2048, 512], P(('dp', 'tp')), parts along dimension 0, may hold values from -70 to 70
- cache_values: bfloat16 [32, 2048, 512], P(('dp', 'tp')), parts along dimension 0, may hold values from -6 to 6
- cache_lens: int32 [32], P(('dp', 'tp')), parts along dimension 0, may hold values from 256 to 2048, as said below
- parents: int32 [32, 24], P(('dp', 'tp')), parts along dimension 0, may hold values from 0 to 23, as said below
- accepted: int32 [32], P(('dp', 'tp')), parts along dimension 0, may hold values from 0 to 23, as said below
- moe_gain: float32 [2880], replicated, may hold values from 0.1 to 1.9
- w_router: bfloat16 [2880, 32], replicated, may hold values from -0.109375 to 0.109375
- routes: int32 [768, 4], P('dp'), parts along dimension 0, may hold values from 0 to 31, all different within a row; in each aligned block of 192 rows (0 to 191, 192 to 383, ...) at most 48 rows name the same one
- w_gate: bfloat16 [11520, 2880], P('tp'), may hold values from -0.109375 to 0.109375
- w_up: bfloat16 [11520, 2880], P('tp'), may hold values from -0.109375 to 0.109375
- w_down: bfloat16 [11520, 2880], P('tp'), may hold values from -0.109375 to 0.109375
Outputs:
- layer_out: bfloat16 [768, 2880], P(('dp', 'tp')), parts along dimension 0
- accepted_kv: bfloat16 [32, 8, 1024], P(('dp', 'tp')), parts along dimension 0
There are 4 independent parts, one for each index of `dp`. A program takes and returns all parts, laid end to end along the dimension named above; an argument that names none is the same for every part. Nothing has to cross between parts.
Inputs may be any that keep to these rules, and one draw needn't show every extreme that they name: `cache_lens`: 2048 for at least one request of every part. `parents`: node 0 names itself; every other node names a node of smaller index; no path from node 0 holds more than 8 nodes, and every tree has one of exactly 8. The path from node 0 to the accepted node holds at most 8 nodes, exactly 8 for at least one request of every part. `routes`: each token names 4 different experts; at most 48 tokens of a part name any one expert, a bound that some block reaches.
All inputs are finite; a program needn't handle non-finite values.
Results may differ from a plain program's by a relative error of at most 0.012.
The roundings to bfloat16 on the way count: a program that leaves them out, or rounds other values in their place, can miss the bound.
Values may be sent and summed in bfloat16 or wider, within the bound.
No kernel may reach another device: no remote copies, remote signals or barrier semaphores. Data moves between devices by JAX's collectives and lax.ppermute only.
A program may use at most 128 MiB of HBM per device.

v0:
```python
import math

import jax
import jax.numpy as jnp
from jax import lax
from jax.sharding import PartitionSpec as P

HEADS = 64
HEAD_DIM = 64
EXPERT_HID = 2880
DEPTH = 8


THETA = 150000.0
SWIGLU_ALPHA = 1.702
EPSILON = 1e-05


def rms_norm(values, gain):
    floats = values.astype(jnp.float32)
    mean_sq = jnp.mean(floats * floats, axis=-1, keepdims=True)
    return (floats * lax.rsqrt(mean_sq + EPSILON) * gain).astype(jnp.bfloat16)


def tree_paths(parent_row, depth_limit):
    count = parent_row.shape[0]
    identity = jnp.eye(count, dtype=jnp.bool_)
    ancestry = identity
    for level in range(depth_limit):
        ancestry = identity | jnp.take(ancestry, parent_row, axis=0)
    depths = jnp.sum(ancestry.astype(jnp.int32), axis=1) - 1
    return (ancestry, depths)


def rotate(values, positions):
    half = values.shape[-1] // 2
    steps_f = jnp.arange(half).astype(jnp.float32)
    inverse = jnp.exp(steps_f * (-2.0 * math.log(THETA) / values.shape[-1]))
    angles = positions[:, None] * inverse[None, :]
    cosine = jnp.cos(angles)[:, None, :]
    sine = jnp.sin(angles)[:, None, :]
    first = values[..., :half].astype(jnp.float32)
    second = values[..., half:].astype(jnp.float32)
    turned = jnp.concatenate(
        [first * cosine - second * sine, second * cosine + first * sine], axis=-1
    )
    return turned.astype(jnp.bfloat16)


def prepare(query, keyval, length, parent_row, depth_limit):
    draft, heads, head_dim = query.shape
    kv_width = keyval.shape[1] // 2
    kv_heads = kv_width // head_dim
    ancestry, depths = tree_paths(parent_row, depth_limit)
    positions = (length + depths).astype(jnp.float32)
    query_rot = rotate(query, positions)
    new_keys = rotate(keyval[:, :kv_width].reshape(draft, kv_heads, head_dim), positions)
    new_values = keyval[:, kv_width:].reshape(draft, kv_heads, head_dim)
    grouped = query_rot.reshape(draft, kv_heads, heads // kv_heads, head_dim)
    draft_scores = jnp.einsum(
        "jgqd,kgd->gqjk", grouped, new_keys, preferred_element_type=jnp.float32
    ) * (1.0 / math.sqrt(head_dim))
    draft_scores = jnp.where(ancestry[None, None], draft_scores, -jnp.inf)
    return (grouped, new_keys, new_values, ancestry, depths, draft_scores)


def accept_rows(new_keys, new_values, ancestry, depths, leaf, depth_limit):
    draft = depths.shape[0]
    selector = ancestry[leaf][None, :] & (depths[None, :] == jnp.arange(depth_limit)[:, None])
    new_rows = jnp.concatenate([new_keys.reshape(draft, -1), new_values.reshape(draft, -1)], axis=1)
    return jnp.dot(
        selector.astype(jnp.bfloat16), new_rows, preferred_element_type=jnp.float32
    ).astype(jnp.bfloat16)


def finish(weighted, total, draft):
    return (
        (weighted / jnp.transpose(total, (2, 0, 1))[..., None])
        .astype(jnp.bfloat16)
        .reshape(draft, -1)
    )


def attend_padded(query, keyval, keys_cache, values_cache, length, parent_row, leaf, depth_limit):
    draft, heads, head_dim = query.shape
    grouped, new_keys, new_values, ancestry, depths, draft_scores = prepare(
        query, keyval, length, parent_row, depth_limit
    )
    slots = keys_cache.shape[0]
    kv_heads = new_keys.shape[1]
    cache_k = keys_cache.reshape(slots, kv_heads, head_dim)
    cache_v = values_cache.reshape(slots, kv_heads, head_dim)
    cache_scores = jnp.einsum(
        "jgqd,pgd->gqjp", grouped, cache_k, preferred_element_type=jnp.float32
    ) * (1.0 / math.sqrt(head_dim))
    live = jnp.arange(slots) < length
    cache_scores = jnp.where(live[None, None, None], cache_scores, -jnp.inf)
    top = jnp.maximum(jnp.max(draft_scores, axis=-1), jnp.max(cache_scores, axis=-1))
    draft_exp = jnp.exp(draft_scores - top[..., None])
    cache_exp = jnp.exp(cache_scores - top[..., None])
    total = jnp.sum(draft_exp, axis=-1) + jnp.sum(cache_exp, axis=-1)
    weighted = jnp.einsum(
        "gqjk,kgd->jgqd",
        draft_exp.astype(jnp.bfloat16),
        new_values,
        preferred_element_type=jnp.float32,
    )
    weighted = weighted + jnp.einsum(
        "gqjp,pgd->jgqd",
        cache_exp.astype(jnp.bfloat16),
        cache_v,
        preferred_element_type=jnp.float32,
    )
    return (
        finish(weighted, total, draft),
        accept_rows(new_keys, new_values, ancestry, depths, leaf, depth_limit),
    )


def gate_weights(inputs, router, routes):
    logits = jnp.dot(inputs, router, preferred_element_type=jnp.float32)
    onehot = routes[:, :, None] == jnp.arange(router.shape[1])[None, None, :]
    picked = jnp.sum(jnp.where(onehot, logits[:, None, :], 0.0), axis=2)
    return jax.nn.softmax(picked, axis=1).astype(jnp.bfloat16)


def expert_slots(inputs, weights, routes, expert, gate_rows, up_rows, down_rows, capacity):
    count = inputs.shape[0]
    match = routes == expert
    hits = jnp.any(match, axis=1)
    gate_of = jnp.sum(jnp.where(match, weights.astype(jnp.float32), 0.0), axis=1)
    slot_ids = jnp.cumsum(hits.astype(jnp.int32)) - 1
    target = jnp.where(hits, slot_ids, capacity)
    index = jnp.full((capacity,), count, jnp.int32).at[target].set(jnp.arange(count), mode="drop")
    valid = index < count
    safe = jnp.minimum(index, count - 1)
    picked = inputs[safe]
    gate_val = lax.dot_general(
        picked, gate_rows, (((1,), (1,)), ((), ())), preferred_element_type=jnp.float32
    )
    up_val = lax.dot_general(
        picked, up_rows, (((1,), (1,)), ((), ())), preferred_element_type=jnp.float32
    )
    active = (gate_val * jax.nn.sigmoid(SWIGLU_ALPHA * gate_val) * (up_val + 1.0)).astype(
        jnp.bfloat16
    )
    result = jnp.dot(active, down_rows, preferred_element_type=jnp.float32)
    scale_rows = jnp.where(valid, gate_of[safe], 0.0)
    return (result * scale_rows[:, None], index)


def local(
    hidden,
    attn_gain,
    w_query,
    w_keyval,
    w_out,
    cache_keys,
    cache_values,
    cache_lens,
    parents,
    accepted,
    moe_gain,
    w_router,
    routes,
    w_gate,
    w_up,
    w_down,
):
    devices = lax.axis_size("tp")
    index_me = lax.axis_index("tp")
    rows = hidden.shape[0]
    normed = rms_norm(hidden, attn_gain)
    local_query = w_query.shape[1]
    both_weights = jnp.concatenate([w_query, w_keyval], axis=1)
    projected = jnp.dot(
        lax.all_gather(normed, "tp", axis=0, tiled=True),
        both_weights,
        preferred_element_type=jnp.float32,
    ).astype(jnp.bfloat16)
    width = projected.shape[1]
    gathered_cols = lax.all_to_all(projected, "tp", split_axis=0, concat_axis=1, tiled=True)
    gathered_cols = gathered_cols.reshape(rows, devices, width)
    requests = cache_lens.shape[0]
    draft = parents.shape[1]
    query = gathered_cols[:, :, :local_query].reshape(requests, draft, HEADS, HEAD_DIM)
    keyval = gathered_cols[:, :, local_query:].reshape(
        requests, draft, devices * (width - local_query)
    )

    def per_request(items):
        return attend_padded(*items, DEPTH)

    attended, accepted_kv = lax.map(
        per_request, (query, keyval, cache_keys, cache_values, cache_lens, parents, accepted)
    )
    attended = attended.reshape(rows, HEADS * HEAD_DIM)
    head_cols = lax.all_to_all(attended, "tp", split_axis=1, concat_axis=0, tiled=True)
    attn_sum = lax.psum_scatter(
        jnp.dot(head_cols, w_out, preferred_element_type=jnp.float32),
        "tp",
        scatter_dimension=0,
        tiled=True,
    )
    middle = (hidden.astype(jnp.float32) + attn_sum).astype(jnp.bfloat16)
    moe_in = rms_norm(middle, moe_gain)
    all_inputs = lax.all_gather(moe_in, "tp", axis=0, tiled=True)
    all_weights = gate_weights(all_inputs, w_router, routes)
    units = w_down.shape[0]
    expert = index_me * units // EXPERT_HID
    count = all_inputs.shape[0]
    capacity = 2 * count * routes.shape[1] // w_router.shape[1]
    slot_rows, slot_index = expert_slots(
        all_inputs, all_weights, routes, expert, w_gate, w_up, w_down, capacity
    )
    term = (
        jnp.zeros((count, all_inputs.shape[1]), jnp.float32)
        .at[slot_index]
        .add(slot_rows, mode="drop")
    )
    mixed = lax.psum_scatter(
        term.astype(jnp.bfloat16), "tp", scatter_dimension=0, tiled=True
    ).astype(jnp.float32)
    layer_out = (middle.astype(jnp.float32) + mixed).astype(jnp.bfloat16)
    return (layer_out, accepted_kv)


def solution(mesh):
    return jax.shard_map(
        local,
        mesh=mesh,
        in_specs=(
            P(("dp", "tp"), None),
            P(),
            P(None, "tp"),
            P(None, "tp"),
            P("tp", None),
            P(("dp", "tp"), None, None),
            P(("dp", "tp"), None, None),
            P(("dp", "tp")),
            P(("dp", "tp"), None),
            P(("dp", "tp")),
            P(),
            P(),
            P("dp", None),
            P("tp", None),
            P("tp", None),
            P("tp", None),
        ),
        out_specs=(P(("dp", "tp"), None), P(("dp", "tp"), None, None)),
        check_vma=False,
    )
```

profile of v0, /device:TPU:0, one launch (start us, length us, event | category | flops | bytes accessed | tf_op | source)
XLA Modules:
  0.0 235.1 jit_solution(12628495440118553622)
XLA Ops:
  7.2 1.2 fusion.39
  8.4 1.7 fusion.41
  17.3 4.0 %copy.137 = bf16[1,2048,512]{1,2,0:T(8,128)(2,1)} copy(bf16[1,2048,512]{2,1,0:T(8,128)(2,1)} %param.23) | data formatting | bytes 4194304 | tf_op args[5]
  22.2 4.0 %copy.143 = bf16[1,2048,512]{1,2,0:T(8,128)(2,1)} copy(bf16[1,2048,512]{2,1,0:T(8,128)(2,1)} %param.24) | data formatting | bytes 4194304 | tf_op args[6]
  26.1 9.3 %all-gather.3.cloned.1.call-done = bf16[192,2880]{1,0:T(8,128)(2,1)} async-done(((bf16[24,2880]{1,0:T(8,128)(2,1)}), bf16[192,2880]{1,0:T(8,128)(2,1)}) %all-gather.3.cloned.1.call-update) | async-done | bytes 1105936 | tf_op jit(solution)/shard_map/all_gather | solution.py:177
  35.5 4.1 %fusion.17 = bf16[192,640]{1,0:T(8,128)(2,1)} fusion(bf16[192,2880]{1,0:T(8,128)(2,1)} %all-gather.3.cloned.1.call-done, bf16[2880,128]{1,0:T(8,128)(2,1)} %param.21, bf16[2880,512]{1,0:T(8,128)(2,1)} %param.20), kind=kOutput, calls=%fused_computation.35 | convolution fusion | flops 715284480 | bytes 5038080 | tf_op jit(solution)/shard_map/dot_general | solution.py:176
  39.6 3.4 %all-to-all-start = ((bf16[8,24,640]{2,1,0:T(8,128)(2,1)}), bf16[8,24,640]{2,1,0:T(8,128)(2,1)S(1)}, u32[]{:S(2)}, u32[]{:S(2)}) async-start(bf16[8,24,640]{2,1,0:T(8,128)(2,1)} %bitcast), calls=%async_computation | async-start | bytes 491520 | tf_op jit(solution)/shard_map/all_to_all | solution.py:182
  44.3 8.0 %all-to-all-done = bf16[8,24,640]{2,1,0:T(8,128)(2,1)S(1)} async-done(((bf16[8,24,640]{2,1,0:T(8,128)(2,1)}), bf16[8,24,640]{2,1,0:T(8,128)(2,1)S(1)}, u32[]{:S(2)}, u32[]{:S(2)}) %all-to-all-start) | async-done | bytes 245792 | tf_op jit(solution)/shard_map/all_to_all | solution.py:182
  54.3 1.2 copy.162
  55.5 1.2 copy.163
  56.7 1.6 fusion.26
  58.3 1.9 copy.157
  61.2 1.3 pad_maximum_fusion
  62.5 8.0 %bitcast_reduce_fusion = (f32[8,8,24]{1,2,0:T(8,128)S(1)}, f32[8,24,8,2048]{3,2,1,0:T(8,128)}) fusion(pred[2048]{0:T(1024)(128)(4,1)S(1)} %iota_compare_fusion.2, bf16[2048,8,64,1]{0,2,3,1:T(8,128)(2,1)} %bitcast.95, bf16[24,8,8,64]{3,0,2,1:T(8,128)(2,1)S(1)} %pad_maximum_fusion), kind=kOutput, calls=%fused_computation.13 | convolution fusion | flops 412088832 | bytes 14884864 | tf_op jit(solution)/shard_map/while/body/eval_jaxpr/jgqd,pgd->gqjp/dot_general | solution.py:93
  71.0 1.7 fusion.83
  72.8 6.3 %fusion.1 = f32[8,8,24]{1,2,0:T(8,128)S(1)} fusion(f32[8,24,8,2048]{3,2,1,0:T(8,128)} %get-tuple-element.58, f32[8,8,24]{1,2,0:T(8,128)S(1)} %copy.142, pred[2048]{0:T(1024)(128)(4,1)S(1)} %iota_compare_fusion.2), kind=kLoop, calls=%fused_computation.16 | loop fusion | flops 12581376 | bytes 12597248 | tf_op jit(solution)/shard_map/while/body/eval_jaxpr/reduce_sum | solution.py:101
  79.2 1.4 fusion.23
  80.5 8.3 %fusion.3 = f32[8,8,24,64]{3,1,2,0:T(8,128)} fusion(bf16[2048,8,64,1]{0,2,3,1:T(8,128)(2,1)} %bitcast.96, f32[8,24,8,2048]{3,2,1,0:T(8,128)} %get-tuple-element.58, f32[8,8,24]{1,2,0:T(8,128)S(1)} %copy.142, pred[2048]{0:T(1024)(128)(4,1)S(1)} %iota_compare_fusion.2), kind=kOutput, calls=%fused_computation.18 | convolution fusion | flops 415236096 | bytes 15081472 | tf_op jit(solution)/shard_map/while/body/eval_jaxpr/gqjp,pgd->jgqd/dot_general | solution.py:108
  89.0 1.8 fusion.16
  91.1 10.7 %all_to_all.35 = bf16[24,8,512]{2,0,1:T(8,128)(2,1)S(1)} all-to-all(bf16[24,8,512]{2,0,1:T(8,128)(2,1)S(1)} %reshape.300), channel_id=1, replica_groups=mesh['dp'=4,'tp'=8] {'tp'}, dimensions={1} | all-to-all | bytes 393216 | tf_op jit(solution)/shard_map/all_to_all | solution.py:198
  101.9 2.5 %fusion.84 = f32[192,2880]{1,0:T(8,128)} fusion(bf16[192,512]{1,0:T(8,128)(2,1)S(1)} %bitcast.101, bf16[512,2880]{0,1:T(8,128)(2,1)S(1)} %copy-done), kind=kOutput, calls=%fused_computation.146 | convolution fusion | flops 566231040 | bytes 5357568 | tf_op jit(solution)/shard_map/dot_general | solution.py:200
  104.5 35.1 %reduce-scatter.7.cloned.1.call-done = f32[24,2880]{1,0:T(8,128)} async-done(((f32[192,2880]{1,0:T(8,128)}), f32[24,2880]{1,0:T(8,128)}) %reduce-scatter.7.cloned.1.call-update) | async-done | bytes 276496
  141.6 21.9 %all-gather.5.cloned.1.call-done = bf16[192,2880]{1,0:T(8,128)(2,1)} async-done(((bf16[24,2880]{1,0:T(8,128)(2,1)}), bf16[192,2880]{1,0:T(8,128)(2,1)}) %all-gather.5.cloned.1.call-update) | async-done | bytes 1105936 | tf_op jit(solution)/shard_map/all_gather | solution.py:207
  163.5 1.7 fusion.86
  166.0 1.2 scatter_custom_fusion
  168.0 2.4 %gather_fusion = bf16[48,2880]{1,0:T(8,128)(2,1)S(1)} fusion(bf16[192,2880]{1,0:T(8,128)(2,1)} %all-gather.5.cloned.1.call-done, s32[1024]{0:T(1024)S(1)} %pad_clamp_fusion), kind=kCustom, calls=%fused_computation.8 | custom fusion | bytes 553152 | tf_op jit(solution)/shard_map/gather | solution.py:137
  170.4 6.6 %fusion.85 = f32[48,1440]{1,0:T(8,128)} fusion(bf16[48,2880]{1,0:T(8,128)(2,1)S(1)} %gather_fusion, bf16[1440,2880]{1,0:T(8,128)(2,1)} %param.31), kind=kOutput, calls=%fused_computation.147 | convolution fusion | flops 398131200 | bytes 8847360 | tf_op jit(solution)/shard_map/dot_general | solution.py:138
  177.0 10.7 %convolution_multiply_fusion = f32[48,2880]{1,0:T(8,128)} fusion(bf16[1440,2880]{1,0:T(8,128)(2,1)} %param.33, bf16[48,2880]{1,0:T(8,128)(2,1)S(1)} %gather_fusion, bf16[1440,2880]{1,0:T(8,128)(2,1)} %param.32, f32[48,1440]{1,0:T(8,128)} %fusion.85, f32[48]{0:T(128)S(1)} %compare_select_fusion.4), kind=kOutput, calls=%fused_computation.24 | convolution fusion | flops 796953600 | bytes 17694912 | tf_op jit(solution)/shard_map/dot_general | solution.py:147
  187.7 3.4 %scatter_custom_fusion.1 = f32[192,2880]{1,0:T(8,128)} fusion(s32[48]{0:T(128)S(1)} %get-tuple-element.54, f32[48,2880]{1,0:T(8,128)} %convolution_multiply_fusion, f32[]{:T(128)} %constant.30.clone.1), kind=kCustom, calls=%fused_computation.36 | custom fusion | flops 138240 | bytes 2212352 | tf_op jit(solution)/shard_map/scatter-add | solution.py:219
  191.1 2.8 %convert_element_type.125 = bf16[192,2880]{1,0:T(8,128)(2,1)} convert(f32[192,2880]{1,0:T(8,128)} %scatter_custom_fusion.1) | non-fusion elementwise | flops 552960 | bytes 3317760 | tf_op jit(solution)/shard_map/convert_element_type | solution.py:222
  196.1 30.9 %reduce-scatter.9.cloned.1.call-done = bf16[24,2880]{1,0:T(8,128)(2,1)} async-done(((bf16[192,2880]{1,0:T(8,128)(2,1)}), bf16[24,2880]{1,0:T(8,128)(2,1)}) %reduce-scatter.9.cloned.1.call-update) | async-done | bytes 138256
  227.0 1.6 fusion.46
  (103 shorter events, 17.9 us)
Async XLA Ops:
  7.2 94.7 %copy-start = (bf16[512,2880]{0,1:T(8,128)(2,1)S(1)}, bf16[512,2880]{0,1:T(8,128)(2,1)}, u32[]{:S(2)}) copy-start(bf16[512,2880]{0,1:T(8,128)(2,1)} %param.22) | copy-start | bytes 8847364
  7.2 28.3 %all-gather.3.cloned.1.call-start = ((), (), s32[]{:S(2)}) async-start(), calls=%async_computation.4 | async-start | bytes 1271808 | tf_op jit(solution)/shard_map/all_gather | solution.py:177
  21.5 18.1 %copy-start.10 = (pred[24,24]{1,0:T(8,128)(4,1)}, pred[24,24]{1,0:T(8,128)(4,1)S(1)}, u32[]{:S(2)}) copy-start(pred[24,24]{1,0:T(8,128)(4,1)S(1)} %get-tuple-element.28) | copy-start | bytes 1732
  39.6 12.7 %all-to-all-start = ((bf16[8,24,640]{2,1,0:T(8,128)(2,1)}), bf16[8,24,640]{2,1,0:T(8,128)(2,1)S(1)}, u32[]{:S(2)}, u32[]{:S(2)}) async-start(bf16[8,24,640]{2,1,0:T(8,128)(2,1)} %bitcast), calls=%async_computation | async-start | bytes 491520 | tf_op jit(solution)/shard_map/all_to_all | solution.py:182
  43.0 96.6 %reduce-scatter.7.cloned.1.call-start = ((), (), s32[]{:S(2)}) async-start(), calls=%async_computation.6 | async-start | bytes 2543616
  62.5 8.1 %copy-start.4 = (bf16[24,1024]{1,0:T(8,128)(2,1)S(1)}, bf16[24,1024]{1,0:T(8,128)(2,1)}, u32[]{:S(2)}) copy-start(bf16[24,1024]{1,0:T(8,128)(2,1)} %copy_bitcast_fusion) | copy-start | bytes 147460
  62.5 8.3 %copy-start.5 = (f32[24,32]{1,0:T(8,128)S(1)}, f32[24,32]{1,0:T(8,128)}, u32[]{:S(2)}) copy-start(f32[24,32]{1,0:T(8,128)} %get-tuple-element.50) | copy-start | bytes 9220
  62.5 8.5 %copy-start.11 = (pred[24,24]{0,1:T(8,128)(4,1)S(1)}, pred[24,24]{0,1:T(8,128)(4,1)}, u32[]{:S(2)}) copy-start(pred[24,24]{0,1:T(8,128)(4,1)} %copy.127) | copy-start | bytes 1732
  70.6 18.3 %copy-start.6 = (bf16[24,512]{1,0:T(8,128)(2,1)}, bf16[24,512]{1,0:T(8,128)(2,1)S(1)}, u32[]{:S(2)}) copy-start(bf16[24,512]{1,0:T(8,128)(2,1)S(1)} %get-tuple-element.45) | copy-start | bytes 73732
  71.0 1.7 copy-start.2
  101.9 37.7 %copy-start.1 = (bf16[24,2880]{1,0:T(8,128)(2,1)S(1)}, bf16[24,2880]{1,0:T(8,128)(2,1)}, u32[]{:S(2)}) copy-start(bf16[24,2880]{1,0:T(8,128)(2,1)} %param.18) | copy-start | bytes 414724
  101.9 38.8 %copy-start.9 = (f32[2880]{0:T(1024)S(1)}, f32[2880]{0:T(1024)}, u32[]{:S(2)}) copy-start(f32[2880]{0:T(1024)} %param.28) | copy-start | bytes 34564
  101.9 63.3 %copy-start.8 = (s32[192,4]{0,1:T(4,128)S(1)}, s32[192,4]{0,1:T(4,128)}, u32[]{:S(2)}) copy-start(s32[192,4]{0,1:T(4,128)} %param.30) | copy-start | bytes 9220
  104.5 59.0 %all-gather.5.cloned.1.call-start = ((), (), s32[]{:S(2)}) async-start(), calls=%async_computation.5 | async-start | bytes 1271808 | tf_op jit(solution)/shard_map/all_gather | solution.py:207
  141.5 85.5 %reduce-scatter.9.cloned.1.call-start = ((), (), s32[]{:S(2)}) async-start(), calls=%async_computation.7 | async-start | bytes 1271808
  187.7 7.5 %copy-start.3 = (bf16[24,8,64]{2,0,1:T(8,128)(2,1)S(1)}, bf16[24,8,64]{2,0,1:T(8,128)(2,1)}, u32[]{:S(2)}) copy-start(bf16[24,8,64]{2,0,1:T(8,128)(2,1)} %copy-done.2) | copy-start | bytes 73732
  187.7 7.6 %copy-start.7 = (bf16[24,512]{1,0:T(8,128)(2,1)S(1)}, bf16[24,512]{1,0:T(8,128)(2,1)}, u32[]{:S(2)}) copy-start(bf16[24,512]{1,0:T(8,128)(2,1)} %copy-done.6) | copy-start | bytes 73732
  187.7 7.6 %copy-start.12 = (s32[24]{0:T(128)S(1)}, s32[24]{0:T(128)}, u32[]{:S(2)}) copy-start(s32[24]{0:T(128)} %get-tuple-element.51) | copy-start | bytes 292
Sparse Core Ops, SparseCore 0:
  10.3 25.1 all-gather.2
  104.6 34.9 reduce-scatter.6
  141.8 21.6 all-gather.4
  194.0 32.9 reduce-scatter.8
where the time goes:
time: 236 us; the launch traced here: 235 us
  waiting for transfers between devices  105 us (44%)
  matrix products  46.2 us (20%)
  other arithmetic  27.2 us (12%)
  local copies, waits for them, and re-layouts  26.7 us (11%)
  between operations  15.4 us (7%)
  blocking collectives  10.7 us (5%)
  starting transfers between devices  3.57 us (2%)
    unnamed x6, waiting for transfers between devices  66.1 us
    all_gather x1, waiting for transfers between devices, local(): all_inputs = lax.all_gather(moe_in, 'tp', axis=0, tiled=True)  21.9 us
    all_to_all x1, blocking collectives, local(): lax.all_to_all(attended, 'tp', split_axis=1, concat_axis=0, tiled=True)  10.7 us
    dot_general x1, matrix products, expert_slots(): result = jnp.dot(active, down_rows, preferred_element_type=jnp.float32)  10.7 us
    unnamed x30, local copies, waits for them, and re-layouts  10.4 us
    all_gather x1, waiting for transfers between devices, local(): lax.all_gather(normed, 'tp', axis=0, tiled=True)  9.32 us
    dot_general x1, matrix products, attend_padded(): jnp.einsum('gqjp,pgd->jgqd', cache_exp.astype(jnp.bfloat16), cache_v, pre...  8.35 us
    dot_general x1, matrix products, attend_padded(): jnp.einsum('jgqd,pgd->gqjp', grouped, cache_k, preferred_element_type=jnp...  8 us
  transfers between devices with their start and end apart: 5, of which 5 were waited for; matrix products, arithmetic and copies ran while one was open for 8% of the time, Pallas kernels for 0%

commit v1 on v0

--- a/solution.py
+++ b/solution.py
@@ -3,6 +3,8 @@
 import jax
 import jax.numpy as jnp
 from jax import lax
+from jax.experimental import pallas as pl
+from jax.experimental.pallas import tpu as pltpu
 from jax.sharding import PartitionSpec as P
 
 HEADS = 64
@@ -149,7 +151,7 @@
     return (result * scale_rows[:, None], index)
 
 
-def local(
+def local_general(
     hidden,
     attn_gain,
     w_query,
@@ -225,6 +227,414 @@
     return (layer_out, accepted_kv)
 
 
+NEGATIVE = -1e30
+VMEM_LIMIT = 60 * 1024 * 1024
+VM = pl.BlockSpec(memory_space=pltpu.VMEM)
+SM = pl.BlockSpec(memory_space=pltpu.SMEM)
+
+
+def run(kernel, outs, args, scalars=1, scratch=(), flops=0, moved=0):
+    return pl.pallas_call(
+        kernel,
+        out_shape=tuple(jax.ShapeDtypeStruct(s, t) for s, t in outs),
+        in_specs=[SM] * scalars + [VM] * (len(args) - scalars),
+        out_specs=tuple(VM for _ in outs),
+        scratch_shapes=list(scratch),
+        compiler_params=pltpu.CompilerParams(vmem_limit_bytes=VMEM_LIMIT),
+        cost_estimate=pl.CostEstimate(flops=flops, bytes_accessed=moved, transcendentals=0),
+    )(*args)
+
+
+def dot_nt(left, right):
+    return lax.dot_general(
+        left, right, (((1,), (1,)), ((), ())), preferred_element_type=jnp.float32
+    )
+
+
+def dot_tn(left, right):
+    return lax.dot_general(
+        left, right, (((0,), (0,)), ((), ())), preferred_element_type=jnp.float32
+    )
+
+
+def dot_nn(left, right):
+    return jnp.dot(left, right, preferred_element_type=jnp.float32)
+
+
+def iota(shape, dim):
+    return lax.broadcasted_iota(jnp.int32, shape, dim)
+
+
+def tree_kernel(lens, accepted, parents, cos_out, sin_out, bias_out, pick_out):
+    wide = parents.shape[1]
+    draft, lanes = cos_out.shape
+    rows, cols = iota((wide, wide), 0), iota((wide, wide), 1)
+    identity = (rows == cols).astype(jnp.bfloat16)
+    step = jnp.maximum((parents[...] == rows).astype(jnp.bfloat16), identity)
+    span = 1
+    while span < DEPTH:
+        step = (dot_nn(step, step) > 0.5).astype(jnp.bfloat16)
+        span = span * 2
+    ancestry = dot_tn(step, identity)
+    depth_row = jnp.sum(step.astype(jnp.float32), axis=0, keepdims=True) - 1.0
+    depth_col = jnp.sum(ancestry, axis=1, keepdims=True) - 1.0
+    positions = depth_col[:draft] + lens[0].astype(jnp.float32)
+    lane = iota((1, lanes), 1)
+    powers = jnp.bitwise_and(lane, HEAD_DIM // 2 - 1).astype(jnp.float32)
+    inverse = jnp.exp(powers * (-2.0 * math.log(THETA) / HEAD_DIM))
+    angles = positions * inverse
+    cos_out[...] = jnp.cos(angles)
+    low = jnp.bitwise_and(lane, HEAD_DIM - 1) < HEAD_DIM // 2
+    sine = jnp.sin(angles)
+    sin_out[...] = jnp.where(low, -sine, sine)
+    bias_out[...] = jnp.where(ancestry[:draft] > 0.5, 0.0, NEGATIVE)
+    leaf_row = jnp.sum(jnp.where(rows == accepted[0], ancestry, 0.0), axis=0, keepdims=True)
+    depths = iota(pick_out.shape, 0).astype(jnp.float32)
+    pick_out[...] = jnp.where((depth_row == depths) & (leaf_row > 0.5), 1.0, 0.0)
+
+
+def project_kernel(*refs):
+    pieces, (gain, w_query, w_keyval), rest = refs[:8], refs[8:11], refs[11:]
+    outs, normed = rest[:4], rest[4]
+    count = pieces[0].shape[0]
+    for k, piece in enumerate(pieces):
+        floats = piece[...].astype(jnp.float32)
+        mean_sq = jnp.mean(floats * floats, axis=-1, keepdims=True)
+        normed[k * count : (k + 1) * count, :] = floats * lax.rsqrt(mean_sq + EPSILON) * gain[...]
+    rows = normed[...].astype(jnp.bfloat16)
+    query = dot_nn(rows, w_query[...]).astype(jnp.bfloat16)
+    keyval = dot_nn(rows, w_keyval[...]).astype(jnp.bfloat16)
+    split = w_query.shape[1]
+    for i, out in enumerate(outs):
+        out[:, :split] = query[2 * count * i : 2 * count * (i + 1)]
+        out[:, split:] = keyval[2 * count * i : 2 * count * (i + 1)]
+
+
+def attend_kernel(*refs):
+    me, lens = refs[0][0], refs[1][0]
+    straight, crossed = refs[2:6], refs[6:10]
+    cos, sin, bias, pick, keys, values = refs[10:16]
+    outs, accepted_out = refs[16:20], refs[20]
+    blocks, queries, new_keys, new_values, attended = refs[21:]
+    draft = cos.shape[0]
+    lanes = 2 * HEAD_DIM
+    for i in range(4):
+        blocks[me ^ (2 * i)] = straight[i][:draft, :].astype(jnp.float32)
+        blocks[me ^ (2 * i + 1)] = crossed[i][draft:, :].astype(jnp.float32)
+    lane = iota((draft, lanes), 1)
+    low = jnp.bitwise_and(lane, HEAD_DIM - 1) < HEAD_DIM // 2
+    left = lane < HEAD_DIM
+    cosine, sine, mask = cos[...], sin[...], bias[...]
+    slots = keys.shape[0]
+    live = jnp.where(iota((1, slots), 1) < lens, 0.0, NEGATIVE)
+
+    def rope(tile):
+        half = HEAD_DIM // 2
+        partner = jnp.where(low, pltpu.roll(tile, lanes - half, 1), pltpu.roll(tile, half, 1))
+        return (tile * cosine + partner * sine).astype(jnp.bfloat16).astype(jnp.float32)
+
+    new_keys[...] = jnp.zeros_like(new_keys)
+    new_values[...] = jnp.zeros_like(new_values)
+    q_cols = blocks.shape[2] - lanes
+    heads = q_cols // HEAD_DIM
+    for pair in range(4):
+        new_keys[:draft, :] = rope(blocks[pair, :, q_cols:])
+        new_values[:draft, :] = blocks[4 + pair, :, q_cols:]
+        fresh_k = new_keys[...].astype(jnp.bfloat16)
+        fresh_v = new_values[...].astype(jnp.bfloat16)
+        picked = pick[...].astype(jnp.bfloat16)
+        span = slice(pair * lanes, (pair + 1) * lanes)
+        accepted_out[:, span] = dot_nn(picked, fresh_k).astype(jnp.bfloat16)
+        accepted_out[:, slice(4 * lanes + pair * lanes, 4 * lanes + (pair + 1) * lanes)] = dot_nn(
+            picked, fresh_v
+        ).astype(jnp.bfloat16)
+        for p in range(2):
+            for t in range(heads // 2):
+                tile = rope(blocks[2 * pair + p, :, t * lanes : (t + 1) * lanes]) * 0.125
+                turned = pltpu.roll(tile, HEAD_DIM, 1)
+                first, second = (tile, turned) if p == 0 else (turned, tile)
+                keep = left if p == 0 else ~left
+                at = (p * heads + 2 * t) * draft
+                queries[at : at + draft, :] = jnp.where(keep, first, 0.0)
+                queries[at + draft : at + 2 * draft, :] = jnp.where(keep, second, 0.0)
+        group = queries[...].astype(jnp.bfloat16)
+        scores = dot_nt(group, keys[:, span]) + live
+        fresh = dot_nt(group, fresh_k)
+        fresh = (fresh.reshape(2 * heads, draft, lanes) + mask[None]).reshape(fresh.shape)
+        top = jnp.maximum(
+            jnp.max(scores, axis=1, keepdims=True), jnp.max(fresh, axis=1, keepdims=True)
+        )
+        weights = jnp.exp(scores - top)
+        fresh = jnp.exp(fresh - top)
+        total = jnp.sum(weights, axis=1, keepdims=True) + jnp.sum(fresh, axis=1, keepdims=True)
+        mixed = dot_nn(weights.astype(jnp.bfloat16), values[:, span])
+        mixed = (mixed + dot_nn(fresh.astype(jnp.bfloat16), fresh_v)) / total
+        for p in range(2):
+            for t in range(heads // 2):
+                at = (p * heads + 2 * t) * draft
+                first, second = mixed[at : at + draft], mixed[at + draft : at + 2 * draft]
+                if p == 0:
+                    tile = jnp.where(left, first, pltpu.roll(second, HEAD_DIM, 1))
+                else:
+                    tile = jnp.where(left, pltpu.roll(first, HEAD_DIM, 1), second)
+                col = p * q_cols + t * lanes
+                attended[pair, :, col : col + lanes] = tile
+    for i, out in enumerate(outs):
+        out[...] = attended[(me // 2) ^ i].astype(jnp.bfloat16)
+
+
+def named_slots(routes, expert, first, count):
+    tokens = routes.shape[1]
+    hits = jnp.max((routes[...] == expert).astype(jnp.float32), axis=0, keepdims=True)
+    upper = (iota((tokens, tokens), 0) <= iota((tokens, tokens), 1)).astype(jnp.bfloat16)
+    wide = jnp.broadcast_to(hits, (16, tokens)).astype(jnp.bfloat16)
+    order = dot_nn(wide, upper)[:1]
+    place = iota((count, tokens), 0).astype(jnp.float32) + (first + 1).astype(jnp.float32)
+    return jnp.where((order == place) & (hits > 0.5), 1.0, 0.0)
+
+
+def residual_kernel(*refs):
+    me, pieces, routes, out, rows = refs[0][0], refs[1:9], refs[9], refs[10], refs[11]
+    count = pieces[0].shape[0]
+    for k, piece in enumerate(pieces):
+        rows[pl.ds(pl.multiple_of((me ^ k) * count, 8), count), :] = piece[...].astype(jnp.float32)
+    half = out.shape[0]
+    chosen = named_slots(routes, me // 2, (me % 2) * half, half).astype(jnp.bfloat16)
+    out[...] = dot_nn(chosen, rows[...].astype(jnp.bfloat16))
+
+
+def outproj_kernel(*refs):
+    me, pieces = refs[0][0], refs[1:9]
+    w_own, w_other, routes, residual = refs[9:13]
+    own, sends = refs[13], refs[14:17]
+    rows, chosen = refs[17:]
+    count = pieces[0].shape[0]
+    half = own.shape[0]
+    core = me % 2
+    for k, piece in enumerate(pieces):
+        rows[pl.ds(pl.multiple_of((me ^ k) * count, 8), count), :] = piece[...].astype(jnp.float32)
+    for i in range(4):
+        chosen[i * half : (i + 1) * half, :] = named_slots(routes, (me // 2) ^ i, core * half, half)
+    picked = dot_nn(chosen[...].astype(jnp.bfloat16), rows[...].astype(jnp.bfloat16))
+    width = w_own.shape[1]
+    low, high = picked[:, :width], picked[:, width:]
+    first = jnp.where(core == 0, low, high).astype(jnp.bfloat16)
+    second = jnp.where(core == 0, high, low).astype(jnp.bfloat16)
+    summed = dot_nt(first, w_own[...]) + dot_nt(second, w_other[...])
+    own[...] = summed[:half] + residual[...]
+    for i, out in enumerate(sends):
+        out[...] = summed[(i + 1) * half : (i + 2) * half].astype(jnp.bfloat16)
+
+
+def token_kernel(*refs):
+    me, pieces, (w_own, w_other, out, rows) = refs[0][0], refs[1:5], refs[5:]
+    count = pieces[0].shape[0]
+    core = me % 2
+    for i, piece in enumerate(pieces):
+        rows[i * count : (i + 1) * count, :] = piece[...].astype(jnp.float32)
+    width = w_own.shape[1]
+    low, high = rows[:, :width], rows[:, width:]
+    first = jnp.where(core == 0, low, high).astype(jnp.bfloat16)
+    second = jnp.where(core == 0, high, low).astype(jnp.bfloat16)
+    out[...] = dot_nt(first, w_own[...]) + dot_nt(second, w_other[...])
+
+
+def expert_kernel(me_ref, mine, theirs, gain, router, routes, w_gate, w_up, w_down, out, rows, active):
+    me = me_ref[0]
+    core, expert = me % 2, me // 2
+    half = mine.shape[0]
+    rows[pl.ds(pl.multiple_of(core * half, 8), half), :] = mine[...].astype(jnp.float32)
+    rows[pl.ds(pl.multiple_of((1 - core) * half, 8), half), :] = theirs[...].astype(jnp.float32)
+    floats = rows[...]
+    mean_sq = jnp.mean(floats * floats, axis=-1, keepdims=True)
+    inputs = (floats * lax.rsqrt(mean_sq + EPSILON) * gain[...]).astype(jnp.bfloat16)
+    experts, tokens = router.shape[0], routes.shape[1]
+    logits = dot_nt(inputs, router[...])
+    chosen = named_slots(routes, expert, expert * 0, 2 * half).astype(jnp.bfloat16)
+    named = jnp.zeros((experts, tokens), jnp.float32)
+    for i in range(routes.shape[0]):
+        named = jnp.maximum(
+            named, (iota((experts, tokens), 0) == routes[i : i + 1, :]).astype(jnp.float32)
+        )
+    named = dot_nt(chosen, named.astype(jnp.bfloat16)) > 0.5
+    logits = jnp.where(named, logits, NEGATIVE)
+    odds = jnp.exp(logits - jnp.max(logits, axis=1, keepdims=True))
+    here = named & (iota(logits.shape, 1) == expert)
+    share = jnp.sum(jnp.where(here, odds, 0.0), axis=1, keepdims=True)
+    share = (share / jnp.sum(odds, axis=1, keepdims=True)).astype(jnp.bfloat16).astype(jnp.float32)
+    gate_val = dot_nt(inputs, w_gate[...])
+    up_val = dot_nt(inputs, w_up[...])
+    act = gate_val * jax.nn.sigmoid(SWIGLU_ALPHA * gate_val) * (up_val + 1.0)
+    active[...] = act.astype(jnp.bfloat16)
+    out[...] = (dot_nn(active[...], w_down[...]) * share).astype(jnp.bfloat16)
+
+
+def combine_kernel(*refs):
+    me, mine, theirs, routes, sums, hidden = refs[0][0], *refs[1:6]
+    own, sends, rows = refs[6], refs[7:10], refs[10]
+    count = hidden.shape[0]
+    total = (mine[...].astype(jnp.float32) + theirs[...].astype(jnp.float32)).astype(jnp.bfloat16)
+    expert = me // 2
+    chosen = named_slots(routes, expert, expert * 0, total.shape[0]).astype(jnp.bfloat16)
+    rows[...] = dot_tn(chosen, total)
+
+    def of(i):
+        start = pl.multiple_of((me ^ (2 * i)) * count, 8)
+        return rows[pl.ds(start, count), :] + sums[i * count : (i + 1) * count, :]
+
+    own[...] = of(0) + hidden[...].astype(jnp.float32)
+    for i, out in enumerate(sends):
+        out[...] = of(i + 1).astype(jnp.bfloat16)
+
+
+def local_paired(
+    hidden,
+    attn_gain,
+    w_query,
+    w_keyval,
+    w_out,
+    cache_keys,
+    cache_values,
+    cache_lens,
+    parents,
+    accepted,
+    moe_gain,
+    w_router,
+    routes,
+    w_gate,
+    w_up,
+    w_down,
+):
+    devices = lax.axis_size("tp")
+    me = lax.axis_index("tp").astype(jnp.int32).reshape(1)
+    bf16, f32 = jnp.bfloat16, jnp.float32
+
+    def swap(values, offset):
+        return lax.ppermute(values, "tp", [(i, i ^ offset) for i in range(devices)])
+
+    rows, width = hidden.shape
+    tokens = routes.shape[0]
+    draft = parents.shape[1]
+    capacity = 2 * tokens * routes.shape[1] // w_router.shape[1]
+    half = capacity // 2
+    routes_t = routes.T
+    router_t = w_router.T
+    w_out_t = w_out.T
+    gain_row = attn_gain.reshape(1, width)
+    moe_row = moe_gain.reshape(1, width)
+
+    line = {s: swap(hidden, s) for s in (6, 4, 2)}
+    line[0] = hidden
+    across = {s: swap(line[s], 1) for s in (0, 2, 4, 6)}
+    pieces = [piece for s in (0, 2, 4, 6) for piece in (line[s], across[s])]
+    w_other_t = swap(w_out, 1).T
+
+    lanes = 128
+    tree = run(
+        tree_kernel,
+        [((draft, lanes), f32), ((draft, lanes), f32), ((draft, lanes), f32), ((DEPTH, lanes), f32)],
+        [cache_lens, accepted, jnp.pad(parents, ((0, 0), (0, lanes - draft)))],
+        scalars=2,
+    )
+
+    queries, keyvals = w_query.shape[1], w_keyval.shape[1]
+    columns = queries + keyvals
+    projected = run(
+        project_kernel,
+        [((2 * rows, columns), bf16)] * 4,
+        [*pieces, gain_row, w_query, w_keyval],
+        scalars=0,
+        scratch=[pltpu.VMEM((tokens, width), f32)],
+        flops=2 * tokens * width * columns,
+        moved=width * columns * 2,
+    )
+    straight = [projected[0]] + [swap(projected[i], 2 * i) for i in (1, 2, 3)]
+    crossed = [swap(block, 1) for block in straight]
+    residual = run(
+        residual_kernel,
+        [((half, width), f32)],
+        [me, *pieces, routes_t],
+        scratch=[pltpu.VMEM((tokens, width), f32)],
+        flops=2 * half * tokens * width,
+        moved=tokens * width * 4,
+    )[0]
+    slots, kv_cols = cache_keys.shape[1:]
+    attended = run(
+        attend_kernel,
+        [((rows, 2 * queries), bf16)] * 4 + [((DEPTH, 2 * kv_cols), bf16)],
+        [me, cache_lens, *straight, *crossed, *tree, cache_keys[0], cache_values[0]],
+        scalars=2,
+        scratch=[
+            pltpu.VMEM((devices, rows, columns), f32),
+            pltpu.VMEM((rows * queries * 2 // HEAD_DIM, lanes), f32),
+            pltpu.VMEM((lanes, lanes), f32),
+            pltpu.VMEM((lanes, lanes), f32),
+            pltpu.VMEM((devices // 2, rows, 2 * queries), f32),
+        ],
+        flops=4 * rows * HEADS * slots * HEAD_DIM,
+        moved=4 * slots * kv_cols,
+    )
+    accepted_kv = attended[4][None]
+    straight = [attended[0]] + [swap(attended[i], 2 * i) for i in (1, 2, 3)]
+    crossed = [swap(block, 1) for block in straight]
+    pieces = [piece for pair in zip(straight, crossed) for piece in pair]
+    out_flops = 2 * 4 * half * 2 * queries * width
+    dispatched = run(
+        outproj_kernel,
+        [((half, width), f32)] + [((half, width), bf16)] * 3,
+        [me, *pieces, w_out_t, w_other_t, routes_t, residual],
+        scratch=[pltpu.VMEM((tokens, 2 * queries), f32), pltpu.VMEM((4 * half, tokens), f32)],
+        flops=out_flops,
+        moved=4 * queries * width,
+    )
+    arrived = [swap(dispatched[i], 2 * i) for i in (1, 2, 3)]
+    sums = run(
+        token_kernel,
+        [((4 * rows, width), f32)],
+        [me, *straight, w_out_t, w_other_t],
+        scratch=[pltpu.VMEM((4 * rows, 2 * queries), f32)],
+        flops=out_flops,
+        moved=4 * queries * width,
+    )[0]
+    middle = dispatched[0]
+    for block in arrived:
+        middle = middle + block.astype(f32)
+    middle = middle.astype(bf16)
+    expert_rows = run(
+        expert_kernel,
+        [((capacity, width), bf16)],
+        [me, middle, swap(middle, 1), moe_row, router_t, routes_t, w_gate, w_up, w_down],
+        scratch=[pltpu.VMEM((capacity, width), f32), pltpu.VMEM((capacity, w_down.shape[0]), bf16)],
+        flops=6 * capacity * width * w_down.shape[0],
+        moved=6 * width * w_down.shape[0],
+    )[0]
+    combined = run(
+        combine_kernel,
+        [((rows, width), f32)] + [((rows, width), bf16)] * 3,
+        [me, expert_rows, swap(expert_rows, 1), routes_t, sums, hidden],
+        scratch=[pltpu.VMEM((tokens, width), f32)],
+        flops=2 * capacity * tokens * width,
+        moved=tokens * width * 4,
+    )
+    layer_out = combined[0]
+    for i in (1, 2, 3):
+        layer_out = layer_out + swap(combined[i], 2 * i).astype(f32)
+    return (layer_out.astype(bf16), accepted_kv)
+
+
+def local(hidden, attn_gain, w_query, w_keyval, *rest):
+    devices = lax.axis_size("tp")
+    parents, units = rest[4], rest[11].shape[0]
+    paired = (
+        devices == 8
+        and parents.shape[0] == 1
+        and units * 2 == EXPERT_HID
+        and w_query.shape[1] * devices == HEADS * HEAD_DIM
+        and w_keyval.shape[1] == 2 * HEAD_DIM
+    )
+    return (local_paired if paired else local_general)(hidden, attn_gain, w_query, w_keyval, *rest)
+
+
 def solution(mesh):
     return jax.shard_map(
         local,

time: 236 us -> 129 us (0.55)
  waiting for transfers between devices: 105 us -> 42.7 us
  Pallas kernels: 0 us -> 48.5 us
  matrix products: 46.2 us -> 0 us
  other arithmetic: 27.2 us -> 2.72 us
  starting transfers between devices: 3.57 us -> 25.6 us
  local copies, waits for them, and re-layouts: 26.7 us -> 7.38 us
  between operations: 15.4 us -> 2.25 us
  blocking collectives: 10.7 us -> 0 us
    unnamed x6 -> x0, waiting for transfers between devices: 66.1 us -> none
    pallas_call x0 -> x8, Pallas kernels: none -> 48.5 us  [run(): pl.pallas_call(kernel, out_shape=tuple((jax.ShapeDtypeStruct(s, t) for s,...]
    dot_general x10 -> x0, matrix products: 46.2 us -> none  [the longest x1 10.7 us: expert_slots(): result = jnp.dot(active, down_rows, preferred_element_type=jnp.float32)]
    ppermute x0 -> x30, waiting for transfers between devices: none -> 42.7 us  [swap(): return lax.ppermute(values, 'tp', [(i, i ^ offset) for i in range(devices)])]
    all_gather x2 -> x0, waiting for transfers between devices: 31.2 us -> none  [the longest x1 21.9 us: local(): all_inputs = lax.all_gather(moe_in, 'tp', axis=0, tiled=True)]
    ppermute x0 -> x30, starting transfers between devices: none -> 25.6 us  [swap(): return lax.ppermute(values, 'tp', [(i, i ^ offset) for i in range(devices)])]
    all_to_all x1 -> x0, blocking collectives: 10.7 us -> none  [local(): lax.all_to_all(attended, 'tp', split_axis=1, concat_axis=0, tiled=True)]
    reduce_sum x8 -> x0, other arithmetic: 10.3 us -> none  [the longest x2 7.7 us: attend_padded(): total = jnp.sum(draft_exp, axis=-1) + jnp.sum(cache_exp, axis=-1)]
  transfers between devices with their start and end apart: 5 -> 30, of which waited for: 5 -> 11; matrix products, arithmetic and copies ran while one was open for 8% -> 2% of each run, Pallas kernels for 0% -> 19%
where the time goes in v1:
time: 129 us
  Pallas kernels  48.5 us (38%)
  waiting for transfers between devices  42.7 us (33%)
  starting transfers between devices  25.6 us (20%)
  local copies, waits for them, and re-layouts  7.38 us (6%)
  other arithmetic  2.72 us (2%)
  between operations  2.25 us (2%)
    pallas_call x8, Pallas kernels, run(): pl.pallas_call(kernel, out_shape=tuple((jax.ShapeDtypeStruct(s, t) for s,...  48.5 us
    ppermute x30, waiting for transfers between devices, swap(): return lax.ppermute(values, 'tp', [(i, i ^ offset) for i in range(devices)])  42.7 us
    ppermute x30, starting transfers between devices, swap(): return lax.ppermute(values, 'tp', [(i, i ^ offset) for i in range(devices)])  25.6 us
    unnamed x54, local copies, waits for them, and re-layouts  4.94 us
  transfers between devices with their start and end apart: 30, of which 11 were waited for; matrix products, arithmetic and copies ran while one was open for 2% of the time, Pallas kernels for 19%

profile of v1, /device:TPU:0, one launch (start us, length us, event | category | flops | bytes accessed | tf_op | source)
XLA Modules:
  0.0 129.1 jit_solution(14813070899128159321)
XLA Ops:
  1.2 2.7 %collective-permute-start.1 = (bf16[24,2880]{1,0:T(8,128)(2,1)}, bf16[24,2880]{1,0:T(8,128)(2,1)S(1)}, u32[]{:S(2)}, u32[]{:S(2)}) collective-permute-start(bf16[24,2880]{1,0:T(8,128)(2,1)} %refs_5_.1), channel_id=1, source_target_pairs={{0,2},{1,3},{2,0},{3,1},{4,6},{5,7},{6,4},{7,5},{8,10},{9,11},{10,... | collective-permute-start | bytes 414728 | tf_op jit(solution)/shard_map/ppermute | solution.py:513
  3.8 2.6 %collective-permute-start.3 = (bf16[24,2880]{1,0:T(8,128)(2,1)}, bf16[24,2880]{1,0:T(8,128)(2,1)S(1)}, u32[]{:S(2)}, u32[]{:S(2)}) collective-permute-start(bf16[24,2880]{1,0:T(8,128)(2,1)} %refs_5_.1), channel_id=1, source_target_pairs={{0,4},{1,5},{2,6},{3,7},{4,0},{5,1},{6,2},{7,3},{8,12},{9,13},{10,... | collective-permute-start | bytes 414728 | tf_op jit(solution)/shard_map/ppermute | solution.py:513
  6.4 4.4 %collective-permute-done.1.refs_2_.refs_3_ = bf16[24,2880]{1,0:T(8,128)(2,1)S(1)} collective-permute-done((bf16[24,2880]{1,0:T(8,128)(2,1)}, bf16[24,2880]{1,0:T(8,128)(2,1)S(1)}, u32[]{:S(2)}, u32[]{:S(2)}) %collective-permute-start.1) | collective-permute-done | bytes 138272 | tf_op jit(solution)/shard_map/ppermute | solution.py:513
  10.8 6.8 %collective-permute-done.3.refs_4_.refs_5_ = bf16[24,2880]{1,0:T(8,128)(2,1)S(1)} collective-permute-done((bf16[24,2880]{1,0:T(8,128)(2,1)}, bf16[24,2880]{1,0:T(8,128)(2,1)S(1)}, u32[]{:S(2)}, u32[]{:S(2)}) %collective-permute-start.3) | collective-permute-done | bytes 138272 | tf_op jit(solution)/shard_map/ppermute | solution.py:513
  18.1 1.3 %reshape.14.refs_8_ = f32[1,2880]{1,0:T(1,128)} reshape(f32[2880]{0:T(1024)} %param.17) | data formatting | bytes 23040 | tf_op jit(solution)/shard_map/reshape | solution.py:523
  20.8 4.5 %shard_map.167 = (bf16[48,640]{1,0:T(8,128)(2,1)}, bf16[48,640]{1,0:T(8,128)(2,1)}, bf16[48,640]{1,0:T(8,128)(2,1)}, bf16[48,640]{1,0:T(8,128)(2,1)}) custom-call(bf16[24,2880]{1,0:T(8,128)(2,1)} %refs_5_.1, bf16[24,2880]{1,0:T(8,128)(2,1)} %copy-done.5, bf16[24,2880]{1,0:T(8,128)(2,1)} %copy-done.2, bf16[24,2880]{1,0:T(8,128)(2,1)} %copy-done.6, ...), custom_call_target="tpu_custom_call" | custom-call | flops 707788800 | bytes 3686400 | tf_op jit(solution)/shard_map/pallas_call | solution.py:237
  25.4 2.3 %collective-permute-start.7 = (bf16[48,640]{1,0:T(8,128)(2,1)}, bf16[48,640]{1,0:T(8,128)(2,1)S(1)}, u32[]{:S(2)}, u32[]{:S(2)}) collective-permute-start(bf16[48,640]{1,0:T(8,128)(2,1)} %get-tuple-element.24), channel_id=1, source_target_pairs={{0,2},{1,3},{2,0},{3,1},{4,6},{5,7},{6,4},{7,5},{8,10},{9,11},{10,... | collective-permute-start | bytes 184328 | tf_op jit(solution)/shard_map/ppermute | solution.py:513
  27.7 1.1 collective-permute-start.8
  28.8 1.4 %collective-permute-start.9 = (bf16[48,640]{1,0:T(8,128)(2,1)}, bf16[48,640]{1,0:T(8,128)(2,1)S(1)}, u32[]{:S(2)}, u32[]{:S(2)}) collective-permute-start(bf16[48,640]{1,0:T(8,128)(2,1)} %get-tuple-element.26), channel_id=1, source_target_pairs={{0,6},{1,7},{2,4},{3,5},{4,2},{5,3},{6,0},{7,1},{8,14},{9,15},{10,... | collective-permute-start | bytes 184328 | tf_op jit(solution)/shard_map/ppermute | solution.py:513
  30.7 5.4 %collective-permute-done.8.refs_4_ = bf16[48,640]{1,0:T(8,128)(2,1)S(1)} collective-permute-done((bf16[48,640]{1,0:T(8,128)(2,1)}, bf16[48,640]{1,0:T(8,128)(2,1)S(1)}, u32[]{:S(2)}, u32[]{:S(2)}) %collective-permute-start.8) | collective-permute-done | bytes 61472 | tf_op jit(solution)/shard_map/ppermute | solution.py:513
  38.4 2.0 %shard_map.168 = (f32[24,128]{1,0:T(8,128)}, f32[24,128]{1,0:T(8,128)}, f32[24,128]{1,0:T(8,128)}, f32[8,128]{1,0:T(8,128)}) custom-call(s32[1]{0:T(128)S(6)} %copy.18.lens.refs_1_, s32[1]{0:T(128)S(6)} %copy.19.accepted, s32[1,128]{1,0:T(1,128)} %pad.4.parents), custom_call_target="tpu_custom_call" | custom-call | tf_op jit(solution)/shard_map/pallas_call | solution.py:237
  41.1 9.3 %shard_map.169 = (bf16[24,1024]{1,0:T(8,128)(2,1)}, bf16[24,1024]{1,0:T(8,128)(2,1)}, bf16[24,1024]{1,0:T(8,128)(2,1)}, bf16[24,1024]{1,0:T(8,128)(2,1)}, bf16[8,1024]{1,0:T(8,128)(2,1)}) custom-call(s32[1]{0:T(128)} %bitcast.refs_0_.me_ref, s32[1]{0:T(128)S(6)} %copy.18.lens.refs_1_, bf16[48,640]{1,0:T(8,128)(2,1)} %get-tuple-element.23.refs_2_, ...), custom_call_target="tpu_custom_call" | custom-call | flops 805306368 | bytes 4194304 | tf_op jit(solution)/shard_map/pallas_call | solution.py:237
  50.4 1.0 collective-permute-start.15
  51.4 1.7 %collective-permute-start.17 = (bf16[24,1024]{1,0:T(8,128)(2,1)}, bf16[24,1024]{1,0:T(8,128)(2,1)S(1)}, u32[]{:S(2)}, u32[]{:S(2)}) collective-permute-start(bf16[24,1024]{1,0:T(8,128)(2,1)} %get-tuple-element.33), channel_id=1, source_target_pairs={{0,4},{1,5},{2,6},{3,7},{4,0},{5,1},{6,2},{7,3},{8,12},{9,13},{10,... | collective-permute-start | bytes 147464 | tf_op jit(solution)/shard_map/ppermute | solution.py:513
  53.1 1.7 %collective-permute-start.19 = (bf16[24,1024]{1,0:T(8,128)(2,1)}, bf16[24,1024]{1,0:T(8,128)(2,1)S(1)}, u32[]{:S(2)}, u32[]{:S(2)}) collective-permute-start(bf16[24,1024]{1,0:T(8,128)(2,1)} %get-tuple-element.34), channel_id=1, source_target_pairs={{0,6},{1,7},{2,4},{3,5},{4,2},{5,3},{6,0},{7,1},{8,14},{9,15},{10,... | collective-permute-start | bytes 147464 | tf_op jit(solution)/shard_map/ppermute | solution.py:513
  55.3 3.0 %collective-permute-done.17.refs_5_.refs_3_ = bf16[24,1024]{1,0:T(8,128)(2,1)S(1)} collective-permute-done((bf16[24,1024]{1,0:T(8,128)(2,1)}, bf16[24,1024]{1,0:T(8,128)(2,1)S(1)}, u32[]{:S(2)}, u32[]{:S(2)}) %collective-permute-start.17) | collective-permute-done | bytes 49184 | tf_op jit(solution)/shard_map/ppermute | solution.py:513
  59.3 2.5 %shard_map.170.refs_12_ = f32[24,2880]{1,0:T(8,128)} custom-call(s32[1]{0:T(128)} %bitcast.refs_0_.me_ref, bf16[24,2880]{1,0:T(8,128)(2,1)} %refs_5_.1, bf16[24,2880]{1,0:T(8,128)(2,1)} %copy-done.5, bf16[24,2880]{1,0:T(8,128)(2,1)} %copy-done.2, bf16[24,2880]{1,0:T(8,128)(2,1)} %copy-done.6, bf16[24,2880]{1,0:T(8,128)(2,1)} %copy-done.3, ...), custom_call_target="tpu_custom_call" | custom-call | flops 26542080 | bytes 2211840 | tf_op jit(solution)/shard_map/pallas_call | solution.py:237
  62.5 1.0 copy-done
  63.5 5.9 %shard_map.171 = (f32[24,2880]{1,0:T(8,128)}, bf16[24,2880]{1,0:T(8,128)(2,1)}, bf16[24,2880]{1,0:T(8,128)(2,1)}, bf16[24,2880]{1,0:T(8,128)(2,1)}) custom-call(s32[1]{0:T(128)} %bitcast.refs_0_.me_ref, bf16[24,1024]{1,0:T(8,128)(2,1)} %get-tuple-element.31.refs_1_, bf16[24,1024]{1,0:T(8,128)(2,1)} %copy-done.21, bf16[24,1024]{1,0:T(8,128)(2,1)} %copy-done.10, ...), custom_call_target="tpu_custom_call" | custom-call | flops 566231040 | bytes 5898240 | tf_op jit(solution)/shard_map/pallas_call | solution.py:237
  69.4 1.7 %collective-permute-start.24 = (bf16[24,2880]{1,0:T(8,128)(2,1)}, bf16[24,2880]{1,0:T(8,128)(2,1)S(1)}, u32[]{:S(2)}, u32[]{:S(2)}) collective-permute-start(bf16[24,2880]{1,0:T(8,128)(2,1)} %get-tuple-element.38), channel_id=1, source_target_pairs={{0,6},{1,7},{2,4},{3,5},{4,2},{5,3},{6,0},{7,1},{8,14},{9,15},{10,... | collective-permute-start | bytes 414728 | tf_op jit(solution)/shard_map/ppermute | solution.py:513
  71.7 2.1 %collective-permute-start.22 = (bf16[24,2880]{1,0:T(8,128)(2,1)}, bf16[24,2880]{1,0:T(8,128)(2,1)S(1)}, u32[]{:S(2)}, u32[]{:S(2)}) collective-permute-start(bf16[24,2880]{1,0:T(8,128)(2,1)} %get-tuple-element.36), channel_id=1, source_target_pairs={{0,2},{1,3},{2,0},{3,1},{4,6},{5,7},{6,4},{7,5},{8,10},{9,11},{10,... | collective-permute-start | bytes 414728 | tf_op jit(solution)/shard_map/ppermute | solution.py:513
  73.8 4.3 %collective-permute-done.24 = bf16[24,2880]{1,0:T(8,128)(2,1)S(1)} collective-permute-done((bf16[24,2880]{1,0:T(8,128)(2,1)}, bf16[24,2880]{1,0:T(8,128)(2,1)S(1)}, u32[]{:S(2)}, u32[]{:S(2)}) %collective-permute-start.24) | collective-permute-done | bytes 138272 | tf_op jit(solution)/shard_map/ppermute | solution.py:513
  78.1 7.0 %collective-permute-done.23 = bf16[24,2880]{1,0:T(8,128)(2,1)S(1)} collective-permute-done((bf16[24,2880]{1,0:T(8,128)(2,1)}, bf16[24,2880]{1,0:T(8,128)(2,1)S(1)}, u32[]{:S(2)}, u32[]{:S(2)}) %collective-permute-start.23) | collective-permute-done | bytes 138272 | tf_op jit(solution)/shard_map/ppermute | solution.py:513
  85.0 1.0 add_convert_fusion.1.mine
  88.2 15.5 %shard_map.172.refs_1_ = bf16[48,2880]{1,0:T(8,128)(2,1)} custom-call(s32[1]{0:T(128)} %bitcast.refs_0_.me_ref, bf16[24,2880]{1,0:T(8,128)(2,1)} %copy-done.1, bf16[24,2880]{1,0:T(8,128)(2,1)} %copy-done.13, f32[1,2880]{1,0:T(1,128)} %reshape.15.gain, bf16[32,2880]{1,0:T(8,128)(2,1)} %bitcast.14, s32[4,192]{1,0:T(4,128)} %bitcast.17, ...), custom_call_target="tpu_custom_call" | custom-call | flops 1194393600 | bytes 24883200 | tf_op jit(solution)/shard_map/pallas_call | solution.py:237
  103.8 5.7 %shard_map.173.refs_4_ = f32[96,2880]{1,0:T(8,128)} custom-call(s32[1]{0:T(128)} %bitcast.refs_0_.me_ref, bf16[24,1024]{1,0:T(8,128)(2,1)} %get-tuple-element.31.refs_1_, bf16[24,1024]{1,0:T(8,128)(2,1)} %copy-done.10, bf16[24,1024]{1,0:T(8,128)(2,1)} %copy-done.11, bf16[24,1024]{1,0:T(8,128)(2,1)} %copy-done.12, bf16[2880,512]{1,0:T(8,128)(2,1)} %bitcast.9, ...), custom_call_target="tpu_custom_call" | custom-call | flops 566231040 | bytes 5898240 | tf_op jit(solution)/shard_map/pallas_call | solution.py:237
  110.3 3.0 %shard_map.174 = (f32[24,2880]{1,0:T(8,128)}, bf16[24,2880]{1,0:T(8,128)(2,1)}, bf16[24,2880]{1,0:T(8,128)(2,1)}, bf16[24,2880]{1,0:T(8,128)(2,1)}) custom-call(s32[1]{0:T(128)} %bitcast.refs_0_.me_ref, bf16[48,2880]{1,0:T(8,128)(2,1)} %shard_map.172.refs_1_, bf16[48,2880]{1,0:T(8,128)(2,1)} %copy-done.9, s32[4,192]{1,0:T(4,128)} %bitcast.18, ...), custom_call_target="tpu_custom_call" | custom-call | flops 53084160 | bytes 2211840 | tf_op jit(solution)/shard_map/pallas_call | solution.py:237
  113.3 2.2 %collective-permute-start.29 = (bf16[24,2880]{1,0:T(8,128)(2,1)}, bf16[24,2880]{1,0:T(8,128)(2,1)S(1)}, u32[]{:S(2)}, u32[]{:S(2)}) collective-permute-start(bf16[24,2880]{1,0:T(8,128)(2,1)} %get-tuple-element.42), channel_id=1, source_target_pairs={{0,6},{1,7},{2,4},{3,5},{4,2},{5,3},{6,0},{7,1},{8,14},{9,15},{10,... | collective-permute-start | bytes 414728 | tf_op jit(solution)/shard_map/ppermute | solution.py:513
  115.5 2.2 %collective-permute-start.27 = (bf16[24,2880]{1,0:T(8,128)(2,1)}, bf16[24,2880]{1,0:T(8,128)(2,1)S(1)}, u32[]{:S(2)}, u32[]{:S(2)}) collective-permute-start(bf16[24,2880]{1,0:T(8,128)(2,1)} %get-tuple-element.40), channel_id=1, source_target_pairs={{0,2},{1,3},{2,0},{3,1},{4,6},{5,7},{6,4},{7,5},{8,10},{9,11},{10,... | collective-permute-start | bytes 414728 | tf_op jit(solution)/shard_map/ppermute | solution.py:513
  117.7 4.3 %collective-permute-done.29 = bf16[24,2880]{1,0:T(8,128)(2,1)S(1)} collective-permute-done((bf16[24,2880]{1,0:T(8,128)(2,1)}, bf16[24,2880]{1,0:T(8,128)(2,1)S(1)}, u32[]{:S(2)}, u32[]{:S(2)}) %collective-permute-start.29) | collective-permute-done | bytes 138272 | tf_op jit(solution)/shard_map/ppermute | solution.py:513
  122.0 5.5 %collective-permute-done.28 = bf16[24,2880]{1,0:T(8,128)(2,1)S(1)} collective-permute-done((bf16[24,2880]{1,0:T(8,128)(2,1)}, bf16[24,2880]{1,0:T(8,128)(2,1)S(1)}, u32[]{:S(2)}, u32[]{:S(2)}) %collective-permute-start.28) | collective-permute-done | bytes 138272 | tf_op jit(solution)/shard_map/ppermute | solution.py:513
  127.4 1.7 %add_convert_fusion = bf16[24,2880]{1,0:T(8,128)(2,1)} fusion(bf16[24,2880]{1,0:T(8,128)(2,1)S(1)} %collective-permute-done.29, bf16[24,2880]{1,0:T(8,128)(2,1)S(1)} %collective-permute-done.28, f32[24,2880]{1,0:T(8,128)} %get-tuple-element.39, bf16[24,2880]{1,0:T(8,128)(2,1)S(1)} %collective-permute-done.27), kind=kLoop, calls=%fused_computation | loop fusion | flops 483840 | bytes 829440 | tf_op jit(solution)/shard_map/convert_element_type | solution.py:622
  (95 shorter events, 10.1 us)
Async XLA Ops:
  0.6 37.2 %copy-start.26 = (s32[1,24]{1,0:T(1,128)S(1)}, s32[1,24]{1,0:T(1,128)}, u32[]{:S(2)}) copy-start(s32[1,24]{1,0:T(1,128)} %param.24) | copy-start | bytes 292
  0.6 61.2 %collective-permute-start.21 = (bf16[512,2880]{0,1:T(8,128)(2,1)}, bf16[512,2880]{0,1:T(8,128)(2,1)S(1)}, u32[]{:S(2)}, u32[]{:S(2)}) collective-permute-start(bf16[512,2880]{0,1:T(8,128)(2,1)} %param.20), channel_id=1, source_target_pairs={{0,1},{1,0},{2,3},{3,2},{4,5},{5,4},{6,7},{7,6},{8,9},{9,8},{10,11... | collective-permute-start | bytes 8847368 | tf_op jit(solution)/shard_map/ppermute | solution.py:513
  1.2 9.7 %collective-permute-start.1 = (bf16[24,2880]{1,0:T(8,128)(2,1)}, bf16[24,2880]{1,0:T(8,128)(2,1)S(1)}, u32[]{:S(2)}, u32[]{:S(2)}) collective-permute-start(bf16[24,2880]{1,0:T(8,128)(2,1)} %refs_5_.1), channel_id=1, source_target_pairs={{0,2},{1,3},{2,0},{3,1},{4,6},{5,7},{6,4},{7,5},{8,10},{9,11},{10,... | collective-permute-start | bytes 414728 | tf_op jit(solution)/shard_map/ppermute | solution.py:513
  3.8 13.8 %collective-permute-start.3 = (bf16[24,2880]{1,0:T(8,128)(2,1)}, bf16[24,2880]{1,0:T(8,128)(2,1)S(1)}, u32[]{:S(2)}, u32[]{:S(2)}) collective-permute-start(bf16[24,2880]{1,0:T(8,128)(2,1)} %refs_5_.1), channel_id=1, source_target_pairs={{0,4},{1,5},{2,6},{3,7},{4,0},{5,1},{6,2},{7,3},{8,12},{9,13},{10,... | collective-permute-start | bytes 414728 | tf_op jit(solution)/shard_map/ppermute | solution.py:513
  6.4 11.2 %collective-permute-start.5 = (bf16[24,2880]{1,0:T(8,128)(2,1)}, bf16[24,2880]{1,0:T(8,128)(2,1)S(1)}, u32[]{:S(2)}, u32[]{:S(2)}) collective-permute-start(bf16[24,2880]{1,0:T(8,128)(2,1)} %refs_5_.1), channel_id=1, source_target_pairs={{0,6},{1,7},{2,4},{3,5},{4,2},{5,3},{6,0},{7,1},{8,14},{9,15},{10,... | collective-permute-start | bytes 414728 | tf_op jit(solution)/shard_map/ppermute | solution.py:513
  6.4 13.0 %collective-permute-start = (bf16[24,2880]{1,0:T(8,128)(2,1)}, bf16[24,2880]{1,0:T(8,128)(2,1)S(1)}, u32[]{:S(2)}, u32[]{:S(2)}) collective-permute-start(bf16[24,2880]{1,0:T(8,128)(2,1)} %refs_5_.1), channel_id=1, source_target_pairs={{0,1},{1,0},{2,3},{3,2},{4,5},{5,4},{6,7},{7,6},{8,9},{9,8},{10,11... | collective-permute-start | bytes 414728 | tf_op jit(solution)/shard_map/ppermute | solution.py:513
  10.8 8.6 %collective-permute-start.2 = (bf16[24,2880]{1,0:T(8,128)(2,1)S(1)}, bf16[24,2880]{1,0:T(8,128)(2,1)S(1)}, u32[]{:S(2)}, u32[]{:S(2)}) collective-permute-start(bf16[24,2880]{1,0:T(8,128)(2,1)S(1)} %collective-permute-done.1.refs_2_.refs_3_), channel_id=1, source_target_pairs={{0,1},{1,0},{2,3},{3,2},{4,5},{5,4},{6,7},{7,6},{8,9},{9,8},{10,11... | collective-permute-start | bytes 414728 | tf_op jit(solution)/shard_map/ppermute | solution.py:513
  17.6 1.9 %collective-permute-start.4 = (bf16[24,2880]{1,0:T(8,128)(2,1)S(1)}, bf16[24,2880]{1,0:T(8,128)(2,1)S(1)}, u32[]{:S(2)}, u32[]{:S(2)}) collective-permute-start(bf16[24,2880]{1,0:T(8,128)(2,1)S(1)} %collective-permute-done.3.refs_4_.refs_5_), channel_id=1, source_target_pairs={{0,1},{1,0},{2,3},{3,2},{4,5},{5,4},{6,7},{7,6},{8,9},{9,8},{10,11... | collective-permute-start | bytes 414728 | tf_op jit(solution)/shard_map/ppermute | solution.py:513
  17.6 1.9 %collective-permute-start.6 = (bf16[24,2880]{1,0:T(8,128)(2,1)S(1)}, bf16[24,2880]{1,0:T(8,128)(2,1)S(1)}, u32[]{:S(2)}, u32[]{:S(2)}) collective-permute-start(bf16[24,2880]{1,0:T(8,128)(2,1)S(1)} %collective-permute-done.5.refs_6_.refs_7_), channel_id=1, source_target_pairs={{0,1},{1,0},{2,3},{3,2},{4,5},{5,4},{6,7},{7,6},{8,9},{9,8},{10,11... | collective-permute-start | bytes 414728 | tf_op jit(solution)/shard_map/ppermute | solution.py:513
  25.4 5.2 %collective-permute-start.7 = (bf16[48,640]{1,0:T(8,128)(2,1)}, bf16[48,640]{1,0:T(8,128)(2,1)S(1)}, u32[]{:S(2)}, u32[]{:S(2)}) collective-permute-start(bf16[48,640]{1,0:T(8,128)(2,1)} %get-tuple-element.24), channel_id=1, source_target_pairs={{0,2},{1,3},{2,0},{3,1},{4,6},{5,7},{6,4},{7,5},{8,10},{9,11},{10,... | collective-permute-start | bytes 184328 | tf_op jit(solution)/shard_map/ppermute | solution.py:513
  27.7 8.3 %collective-permute-start.8 = (bf16[48,640]{1,0:T(8,128)(2,1)}, bf16[48,640]{1,0:T(8,128)(2,1)S(1)}, u32[]{:S(2)}, u32[]{:S(2)}) collective-permute-start(bf16[48,640]{1,0:T(8,128)(2,1)} %get-tuple-element.25), channel_id=1, source_target_pairs={{0,4},{1,5},{2,6},{3,7},{4,0},{5,1},{6,2},{7,3},{8,12},{9,13},{10,... | collective-permute-start | bytes 184328 | tf_op jit(solution)/shard_map/ppermute | solution.py:513
  28.8 7.3 %collective-permute-start.9 = (bf16[48,640]{1,0:T(8,128)(2,1)}, bf16[48,640]{1,0:T(8,128)(2,1)S(1)}, u32[]{:S(2)}, u32[]{:S(2)}) collective-permute-start(bf16[48,640]{1,0:T(8,128)(2,1)} %get-tuple-element.26), channel_id=1, source_target_pairs={{0,6},{1,7},{2,4},{3,5},{4,2},{5,3},{6,0},{7,1},{8,14},{9,15},{10,... | collective-permute-start | bytes 184328 | tf_op jit(solution)/shard_map/ppermute | solution.py:513
  30.2 10.2 %collective-permute-start.10 = (bf16[48,640]{1,0:T(8,128)(2,1)}, bf16[48,640]{1,0:T(8,128)(2,1)S(1)}, u32[]{:S(2)}, u32[]{:S(2)}) collective-permute-start(bf16[48,640]{1,0:T(8,128)(2,1)} %get-tuple-element.23.refs_2_), channel_id=1, source_target_pairs={{0,1},{1,0},{2,3},{3,2},{4,5},{5,4},{6,7},{7,6},{8,9},{9,8},{10,11... | collective-permute-start | bytes 184328 | tf_op jit(solution)/shard_map/ppermute | solution.py:513
  30.6 9.8 %collective-permute-start.11 = (bf16[48,640]{1,0:T(8,128)(2,1)S(1)}, bf16[48,640]{1,0:T(8,128)(2,1)S(1)}, u32[]{:S(2)}, u32[]{:S(2)}) collective-permute-start(bf16[48,640]{1,0:T(8,128)(2,1)S(1)} %collective-permute-done.7.refs_3_), channel_id=1, source_target_pairs={{0,1},{1,0},{2,3},{3,2},{4,5},{5,4},{6,7},{7,6},{8,9},{9,8},{10,11... | collective-permute-start | bytes 184328 | tf_op jit(solution)/shard_map/ppermute | solution.py:513
  36.1 4.3 %collective-permute-start.12 = (bf16[48,640]{1,0:T(8,128)(2,1)S(1)}, bf16[48,640]{1,0:T(8,128)(2,1)S(1)}, u32[]{:S(2)}, u32[]{:S(2)}) collective-permute-start(bf16[48,640]{1,0:T(8,128)(2,1)S(1)} %collective-permute-done.8.refs_4_), channel_id=1, source_target_pairs={{0,1},{1,0},{2,3},{3,2},{4,5},{5,4},{6,7},{7,6},{8,9},{9,8},{10,11... | collective-permute-start | bytes 184328 | tf_op jit(solution)/shard_map/ppermute | solution.py:513
  36.1 4.3 %collective-permute-start.13 = (bf16[48,640]{1,0:T(8,128)(2,1)S(1)}, bf16[48,640]{1,0:T(8,128)(2,1)S(1)}, u32[]{:S(2)}, u32[]{:S(2)}) collective-permute-start(bf16[48,640]{1,0:T(8,128)(2,1)S(1)} %collective-permute-done.9.refs_5_), channel_id=1, source_target_pairs={{0,1},{1,0},{2,3},{3,2},{4,5},{5,4},{6,7},{7,6},{8,9},{9,8},{10,11... | collective-permute-start | bytes 184328 | tf_op jit(solution)/shard_map/ppermute | solution.py:513
  50.4 4.4 %collective-permute-start.15 = (bf16[24,1024]{1,0:T(8,128)(2,1)}, bf16[24,1024]{1,0:T(8,128)(2,1)S(1)}, u32[]{:S(2)}, u32[]{:S(2)}) collective-permute-start(bf16[24,1024]{1,0:T(8,128)(2,1)} %get-tuple-element.32), channel_id=1, source_target_pairs={{0,2},{1,3},{2,0},{3,1},{4,6},{5,7},{6,4},{7,5},{8,10},{9,11},{10,... | collective-permute-start | bytes 147464 | tf_op jit(solution)/shard_map/ppermute | solution.py:513
  51.4 7.0 %collective-permute-start.17 = (bf16[24,1024]{1,0:T(8,128)(2,1)}, bf16[24,1024]{1,0:T(8,128)(2,1)S(1)}, u32[]{:S(2)}, u32[]{:S(2)}) collective-permute-start(bf16[24,1024]{1,0:T(8,128)(2,1)} %get-tuple-element.33), channel_id=1, source_target_pairs={{0,4},{1,5},{2,6},{3,7},{4,0},{5,1},{6,2},{7,3},{8,12},{9,13},{10,... | collective-permute-start | bytes 147464 | tf_op jit(solution)/shard_map/ppermute | solution.py:513
  53.1 6.2 %collective-permute-start.19 = (bf16[24,1024]{1,0:T(8,128)(2,1)}, bf16[24,1024]{1,0:T(8,128)(2,1)S(1)}, u32[]{:S(2)}, u32[]{:S(2)}) collective-permute-start(bf16[24,1024]{1,0:T(8,128)(2,1)} %get-tuple-element.34), channel_id=1, source_target_pairs={{0,6},{1,7},{2,4},{3,5},{4,2},{5,3},{6,0},{7,1},{8,14},{9,15},{10,... | collective-permute-start | bytes 147464 | tf_op jit(solution)/shard_map/ppermute | solution.py:513
  54.8 7.0 %collective-permute-start.14 = (bf16[24,1024]{1,0:T(8,128)(2,1)}, bf16[24,1024]{1,0:T(8,128)(2,1)S(1)}, u32[]{:S(2)}, u32[]{:S(2)}) collective-permute-start(bf16[24,1024]{1,0:T(8,128)(2,1)} %get-tuple-element.31.refs_1_), channel_id=1, source_target_pairs={{0,1},{1,0},{2,3},{3,2},{4,5},{5,4},{6,7},{7,6},{8,9},{9,8},{10,11... | collective-permute-start | bytes 147464 | tf_op jit(solution)/shard_map/ppermute | solution.py:513
  54.8 7.0 %collective-permute-start.16 = (bf16[24,1024]{1,0:T(8,128)(2,1)S(1)}, bf16[24,1024]{1,0:T(8,128)(2,1)S(1)}, u32[]{:S(2)}, u32[]{:S(2)}) collective-permute-start(bf16[24,1024]{1,0:T(8,128)(2,1)S(1)} %collective-permute-done.15.refs_3_.refs_2_), channel_id=1, source_target_pairs={{0,1},{1,0},{2,3},{3,2},{4,5},{5,4},{6,7},{7,6},{8,9},{9,8},{10,11... | collective-permute-start | bytes 147464 | tf_op jit(solution)/shard_map/ppermute | solution.py:513
  58.3 3.5 %collective-permute-start.18 = (bf16[24,1024]{1,0:T(8,128)(2,1)S(1)}, bf16[24,1024]{1,0:T(8,128)(2,1)S(1)}, u32[]{:S(2)}, u32[]{:S(2)}) collective-permute-start(bf16[24,1024]{1,0:T(8,128)(2,1)S(1)} %collective-permute-done.17.refs_5_.refs_3_), channel_id=1, source_target_pairs={{0,1},{1,0},{2,3},{3,2},{4,5},{5,4},{6,7},{7,6},{8,9},{9,8},{10,11... | collective-permute-start | bytes 147464 | tf_op jit(solution)/shard_map/ppermute | solution.py:513
  59.3 2.6 %collective-permute-start.20 = (bf16[24,1024]{1,0:T(8,128)(2,1)S(1)}, bf16[24,1024]{1,0:T(8,128)(2,1)S(1)}, u32[]{:S(2)}, u32[]{:S(2)}) collective-permute-start(bf16[24,1024]{1,0:T(8,128)(2,1)S(1)} %collective-permute-done.19.refs_7_.refs_4_), channel_id=1, source_target_pairs={{0,1},{1,0},{2,3},{3,2},{4,5},{5,4},{6,7},{7,6},{8,9},{9,8},{10,11... | collective-permute-start | bytes 147464 | tf_op jit(solution)/shard_map/ppermute | solution.py:513
  63.5 22.7 %copy-start.25 = (f32[2880]{0:T(1024)S(1)}, f32[2880]{0:T(1024)}, u32[]{:S(2)}) copy-start(f32[2880]{0:T(1024)} %param.26) | copy-start | bytes 34564
  69.4 8.7 %collective-permute-start.24 = (bf16[24,2880]{1,0:T(8,128)(2,1)}, bf16[24,2880]{1,0:T(8,128)(2,1)S(1)}, u32[]{:S(2)}, u32[]{:S(2)}) collective-permute-start(bf16[24,2880]{1,0:T(8,128)(2,1)} %get-tuple-element.38), channel_id=1, source_target_pairs={{0,6},{1,7},{2,4},{3,5},{4,2},{5,3},{6,0},{7,1},{8,14},{9,15},{10,... | collective-permute-start | bytes 414728 | tf_op jit(solution)/shard_map/ppermute | solution.py:513
  71.1 13.9 %collective-permute-start.23 = (bf16[24,2880]{1,0:T(8,128)(2,1)}, bf16[24,2880]{1,0:T(8,128)(2,1)S(1)}, u32[]{:S(2)}, u32[]{:S(2)}) collective-permute-start(bf16[24,2880]{1,0:T(8,128)(2,1)} %get-tuple-element.37), channel_id=1, source_target_pairs={{0,4},{1,5},{2,6},{3,7},{4,0},{5,1},{6,2},{7,3},{8,12},{9,13},{10,... | collective-permute-start | bytes 414728 | tf_op jit(solution)/shard_map/ppermute | solution.py:513
  71.7 13.4 %collective-permute-start.22 = (bf16[24,2880]{1,0:T(8,128)(2,1)}, bf16[24,2880]{1,0:T(8,128)(2,1)S(1)}, u32[]{:S(2)}, u32[]{:S(2)}) collective-permute-start(bf16[24,2880]{1,0:T(8,128)(2,1)} %get-tuple-element.36), channel_id=1, source_target_pairs={{0,2},{1,3},{2,0},{3,1},{4,6},{5,7},{6,4},{7,5},{8,10},{9,11},{10,... | collective-permute-start | bytes 414728 | tf_op jit(solution)/shard_map/ppermute | solution.py:513
  86.1 1.4 %collective-permute-start.25 = (bf16[24,2880]{1,0:T(8,128)(2,1)S(1)}, bf16[24,2880]{1,0:T(8,128)(2,1)S(1)}, u32[]{:S(2)}, u32[]{:S(2)}) collective-permute-start(bf16[24,2880]{1,0:T(8,128)(2,1)S(1)} %add_convert_fusion.1.mine), channel_id=1, source_target_pairs={{0,1},{1,0},{2,3},{3,2},{4,5},{5,4},{6,7},{7,6},{8,9},{9,8},{10,11... | collective-permute-start | bytes 414728 | tf_op jit(solution)/shard_map/ppermute | solution.py:513
  103.7 5.9 %collective-permute-start.26 = (bf16[48,2880]{1,0:T(8,128)(2,1)}, bf16[48,2880]{1,0:T(8,128)(2,1)S(1)}, u32[]{:S(2)}, u32[]{:S(2)}) collective-permute-start(bf16[48,2880]{1,0:T(8,128)(2,1)} %shard_map.172.refs_1_), channel_id=1, source_target_pairs={{0,1},{1,0},{2,3},{3,2},{4,5},{5,4},{6,7},{7,6},{8,9},{9,8},{10,11... | collective-permute-start | bytes 829448 | tf_op jit(solution)/shard_map/ppermute | solution.py:513
  113.3 8.7 %collective-permute-start.29 = (bf16[24,2880]{1,0:T(8,128)(2,1)}, bf16[24,2880]{1,0:T(8,128)(2,1)S(1)}, u32[]{:S(2)}, u32[]{:S(2)}) collective-permute-start(bf16[24,2880]{1,0:T(8,128)(2,1)} %get-tuple-element.42), channel_id=1, source_target_pairs={{0,6},{1,7},{2,4},{3,5},{4,2},{5,3},{6,0},{7,1},{8,14},{9,15},{10,... | collective-permute-start | bytes 414728 | tf_op jit(solution)/shard_map/ppermute | solution.py:513
  115.5 12.0 %collective-permute-start.28 = (bf16[24,2880]{1,0:T(8,128)(2,1)}, bf16[24,2880]{1,0:T(8,128)(2,1)S(1)}, u32[]{:S(2)}, u32[]{:S(2)}) collective-permute-start(bf16[24,2880]{1,0:T(8,128)(2,1)} %get-tuple-element.41), channel_id=1, source_target_pairs={{0,4},{1,5},{2,6},{3,7},{4,0},{5,1},{6,2},{7,3},{8,12},{9,13},{10,... | collective-permute-start | bytes 414728 | tf_op jit(solution)/shard_map/ppermute | solution.py:513
  115.5 12.0 %collective-permute-start.27 = (bf16[24,2880]{1,0:T(8,128)(2,1)}, bf16[24,2880]{1,0:T(8,128)(2,1)S(1)}, u32[]{:S(2)}, u32[]{:S(2)}) collective-permute-start(bf16[24,2880]{1,0:T(8,128)(2,1)} %get-tuple-element.40), channel_id=1, source_target_pairs={{0,2},{1,3},{2,0},{3,1},{4,6},{5,7},{6,4},{7,5},{8,10},{9,11},{10,... | collective-permute-start | bytes 414728 | tf_op jit(solution)/shard_map/ppermute | solution.py:513
  (25 other events, 56.7 us)

commit v2 on v1

--- a/solution.py
+++ b/solution.py
@@ -228,21 +228,55 @@
 
 
 NEGATIVE = -1e30
-VMEM_LIMIT = 60 * 1024 * 1024
+MIB = 1024 * 1024
+VMEM_LIMIT = 24 * MIB
 VM = pl.BlockSpec(memory_space=pltpu.VMEM)
 SM = pl.BlockSpec(memory_space=pltpu.SMEM)
 
 
-def run(kernel, outs, args, scalars=1, scratch=(), flops=0, moved=0):
+def run(kernel, outs, args, scalars=1, scratch=(), flops=0, moved=0, limit=VMEM_LIMIT):
     return pl.pallas_call(
         kernel,
         out_shape=tuple(jax.ShapeDtypeStruct(s, t) for s, t in outs),
         in_specs=[SM] * scalars + [VM] * (len(args) - scalars),
         out_specs=tuple(VM for _ in outs),
         scratch_shapes=list(scratch),
-        compiler_params=pltpu.CompilerParams(vmem_limit_bytes=VMEM_LIMIT),
+        compiler_params=pltpu.CompilerParams(vmem_limit_bytes=limit),
         cost_estimate=pl.CostEstimate(flops=flops, bytes_accessed=moved, transcendentals=0),
     )(*args)
+
+
+def near(values):
+    return pltpu.with_memory_space_constraint(values, pltpu.VMEM)
+
+
+def far(values):
+    return pltpu.with_memory_space_constraint(values, pltpu.HBM)
+
+
+def load(*arrays):
+    def kernel(*refs):
+        count = len(arrays)
+        sources, targets, sems = refs[:count], refs[count : 2 * count], refs[2 * count]
+        copies = [
+            pltpu.make_async_copy(source, target, sems.at[i])
+            for i, (source, target) in enumerate(zip(sources, targets))
+        ]
+        for copy in copies:
+            copy.start()
+        for copy in copies:
+            copy.wait()
+
+    moved = sum(a.size * a.dtype.itemsize for a in arrays)
+    return pl.pallas_call(
+        kernel,
+        out_shape=tuple(pltpu.VMEM(a.shape, a.dtype) for a in arrays),
+        in_specs=[pl.BlockSpec(memory_space=pl.ANY)] * len(arrays),
+        out_specs=tuple(VM for _ in arrays),
+        scratch_shapes=[pltpu.SemaphoreType.DMA((len(arrays),))],
+        compiler_params=pltpu.CompilerParams(vmem_limit_bytes=MIB),
+        cost_estimate=pl.CostEstimate(flops=0, bytes_accessed=2 * moved, transcendentals=0),
+    )(*[far(a) for a in arrays])
 
 
 def dot_nt(left, right):
@@ -524,45 +558,53 @@
     moe_row = moe_gain.reshape(1, width)
 
     line = {s: swap(hidden, s) for s in (6, 4, 2)}
+    lanes = 128
+    parents = jnp.pad(parents, ((0, 0), (0, lanes - draft)))
+    early = (gain_row, moe_row, parents, load(w_query, w_keyval))
+    line, early = lax.optimization_barrier((line, early))
+    gain_row, moe_row, parents, (near_query, near_keyval) = early
     line[0] = hidden
     across = {s: swap(line[s], 1) for s in (0, 2, 4, 6)}
     pieces = [piece for s in (0, 2, 4, 6) for piece in (line[s], across[s])]
-    w_other_t = swap(w_out, 1).T
-
-    lanes = 128
-    tree = run(
-        tree_kernel,
-        [((draft, lanes), f32), ((draft, lanes), f32), ((draft, lanes), f32), ((DEPTH, lanes), f32)],
-        [cache_lens, accepted, jnp.pad(parents, ((0, 0), (0, lanes - draft)))],
-        scalars=2,
-    )
 
     queries, keyvals = w_query.shape[1], w_keyval.shape[1]
     columns = queries + keyvals
     projected = run(
         project_kernel,
         [((2 * rows, columns), bf16)] * 4,
-        [*pieces, gain_row, w_query, w_keyval],
+        [*pieces, gain_row, near(near_query), near(near_keyval)],
         scalars=0,
         scratch=[pltpu.VMEM((tokens, width), f32)],
         flops=2 * tokens * width * columns,
         moved=width * columns * 2,
     )
+    (keys, values, w_pair, lens, me_then), projected = lax.optimization_barrier(
+        ((cache_keys[0], cache_values[0], w_out, cache_lens, me), projected)
+    )
     straight = [projected[0]] + [swap(projected[i], 2 * i) for i in (1, 2, 3)]
-    crossed = [swap(block, 1) for block in straight]
+    tree = run(
+        tree_kernel,
+        [((draft, lanes), f32), ((draft, lanes), f32), ((draft, lanes), f32), ((DEPTH, lanes), f32)],
+        [lens, accepted, parents],
+        scalars=2,
+    )
     residual = run(
         residual_kernel,
         [((half, width), f32)],
-        [me, *pieces, routes_t],
+        [me_then, *pieces, routes_t],
         scratch=[pltpu.VMEM((tokens, width), f32)],
         flops=2 * half * tokens * width,
         moved=tokens * width * 4,
     )[0]
+    cached = load(keys, values)
+    straight, tree, residual, cached = lax.optimization_barrier((straight, tree, residual, cached))
+    crossed = [swap(block, 1) for block in straight]
+    w_other_t = swap(w_pair, 1).T
     slots, kv_cols = cache_keys.shape[1:]
     attended = run(
         attend_kernel,
         [((rows, 2 * queries), bf16)] * 4 + [((DEPTH, 2 * kv_cols), bf16)],
-        [me, cache_lens, *straight, *crossed, *tree, cache_keys[0], cache_values[0]],
+        [me, cache_lens, *straight, *crossed, *tree, near(cached[0]), near(cached[1])],
         scalars=2,
         scratch=[
             pltpu.VMEM((devices, rows, columns), f32),
@@ -575,36 +617,54 @@
         moved=4 * slots * kv_cols,
     )
     accepted_kv = attended[4][None]
+    w_out_t, attended = lax.optimization_barrier((w_out_t, attended))
     straight = [attended[0]] + [swap(attended[i], 2 * i) for i in (1, 2, 3)]
+    straight, (near_out,) = lax.optimization_barrier((straight, load(w_out_t)))
     crossed = [swap(block, 1) for block in straight]
     pieces = [piece for pair in zip(straight, crossed) for piece in pair]
     out_flops = 2 * 4 * half * 2 * queries * width
     dispatched = run(
         outproj_kernel,
         [((half, width), f32)] + [((half, width), bf16)] * 3,
-        [me, *pieces, w_out_t, w_other_t, routes_t, residual],
+        [me, *pieces, near(near_out), near(w_other_t), routes_t, residual],
         scratch=[pltpu.VMEM((tokens, 2 * queries), f32), pltpu.VMEM((4 * half, tokens), f32)],
         flops=out_flops,
         moved=4 * queries * width,
     )
     arrived = [swap(dispatched[i], 2 * i) for i in (1, 2, 3)]
+    me_after = lax.optimization_barrier((me, dispatched[1]))[0]
     sums = run(
         token_kernel,
         [((4 * rows, width), f32)],
-        [me, *straight, w_out_t, w_other_t],
+        [me_after, *straight, near(near_out), near(w_other_t)],
         scratch=[pltpu.VMEM((4 * rows, 2 * queries), f32)],
+        limit=6 * MIB,
         flops=out_flops,
         moved=4 * queries * width,
     )[0]
-    middle = dispatched[0]
+    experts, _ = lax.optimization_barrier(((w_gate, w_up, w_down), dispatched[1]))
+    near_gate, near_up, near_down = load(*experts)
+    near_weights = (near_gate, near_up, near_down)
+    middle, arrived, sums, near_weights = lax.optimization_barrier(
+        (dispatched[0], arrived, sums, near_weights)
+    )
     for block in arrived:
         middle = middle + block.astype(f32)
     middle = middle.astype(bf16)
     expert_rows = run(
         expert_kernel,
         [((capacity, width), bf16)],
-        [me, middle, swap(middle, 1), moe_row, router_t, routes_t, w_gate, w_up, w_down],
+        [
+            me,
+            middle,
+            swap(middle, 1),
+            moe_row,
+            router_t,
+            routes_t,
+            *map(near, near_weights),
+        ],
         scratch=[pltpu.VMEM((capacity, width), f32), pltpu.VMEM((capacity, w_down.shape[0]), bf16)],
+        limit=6 * MIB,
         flops=6 * capacity * width * w_down.shape[0],
         moved=6 * width * w_down.shape[0],
     )[0]

time: 129 us -> 96.3 us (0.75)
  waiting for transfers between devices: 42.7 us -> 25.9 us
  Pallas kernels: 48.5 us -> 37.3 us
  local copies, waits for them, and re-layouts: 7.38 us -> 4.09 us
  other arithmetic: 2.72 us -> 0.81 us
    pallas_call x8, Pallas kernels: 48.5 us -> 22.9 us  [run(): pl.pallas_call(kernel, out_shape=tuple((jax.ShapeDtypeStruct(s, t) for s,...]
    ppermute x30, waiting for transfers between devices: 42.7 us -> 25.9 us  [swap(): return lax.ppermute(values, 'tp', [(i, i ^ offset) for i in range(devices)])]
    pallas_call x0 -> x4, Pallas kernels: none -> 14.4 us  [load(): pl.pallas_call(kernel, out_shape=tuple((pltpu.VMEM(a.shape, a.dtype) for...]
    unnamed x54 -> x12, local copies, waits for them, and re-layouts: 4.94 us -> 2 us
  transfers between devices with their start and end apart: 30 -> 30, of which waited for: 11 -> 17; matrix products, arithmetic and copies ran while one was open for 2% -> 2% of each run, Pallas kernels for 19% -> 27%
where the time goes in v2:
time: 96.3 us; the launch traced here: 96 us
  Pallas kernels  37.3 us (39%)
  waiting for transfers between devices  25.9 us (27%)
  starting transfers between devices  25.7 us (27%)
  local copies, waits for them, and re-layouts  4.09 us (4%)
  between operations  2.16 us (2%)
    ppermute x30, waiting for transfers between devices, swap(): return lax.ppermute(values, 'tp', [(i, i ^ offset) for i in range(devices)])  25.9 us
    ppermute x30, starting transfers between devices, swap(): return lax.ppermute(values, 'tp', [(i, i ^ offset) for i in range(devices)])  25.7 us
    pallas_call x8, Pallas kernels, run(): pl.pallas_call(kernel, out_shape=tuple((jax.ShapeDtypeStruct(s, t) for s,...  22.9 us
    pallas_call x4, Pallas kernels, load(): pl.pallas_call(kernel, out_shape=tuple((pltpu.VMEM(a.shape, a.dtype) for...  14.4 us
    unnamed x12, local copies, waits for them, and re-layouts  2 us
  transfers between devices with their start and end apart: 30, of which 17 were waited for; matrix products, arithmetic and copies ran while one was open for 2% of the time, Pallas kernels for 27%

profile of v2, /device:TPU:0, one launch (start us, length us, event | category | flops | bytes accessed | tf_op | source)
XLA Modules:
  0.0 96.0 jit_solution(5918310752707412727)
XLA Ops:
  0.6 5.1 %collective-permute-start.3 = (bf16[24,2880]{1,0:T(8,128)(2,1)}, bf16[24,2880]{1,0:T(8,128)(2,1)S(1)}, u32[]{:S(2)}, u32[]{:S(2)}) collective-permute-start(bf16[24,2880]{1,0:T(8,128)(2,1)} %refs_5_.1), channel_id=1, source_target_pairs={{0,6},{1,7},{2,4},{3,5},{4,2},{5,3},{6,0},{7,1},{8,14},{9,15},{10,... | collective-permute-start | bytes 414728 | tf_op jit(solution)/shard_map/ppermute | solution.py:547
  8.5 2.0 %shard_map.167 = (bf16[2880,512]{1,0:T(8,128)(2,1)S(1)}, bf16[2880,128]{1,0:T(8,128)(2,1)S(1)}) custom-call(bf16[2880,512]{1,0:T(8,128)(2,1)} %refs_0_.2, bf16[2880,128]{1,0:T(8,128)(2,1)} %refs_1_.3), custom_call_target="tpu_custom_call" | custom-call | bytes 7372800 | tf_op jit(solution)/shard_map/pallas_call | solution.py:271
  10.5 0.9 copy-done.1
  11.4 6.5 %collective-permute-done.2.refs_4_.refs_5_ = bf16[24,2880]{1,0:T(8,128)(2,1)S(1)} collective-permute-done((bf16[24,2880]{1,0:T(8,128)(2,1)}, bf16[24,2880]{1,0:T(8,128)(2,1)S(1)}, u32[]{:S(2)}, u32[]{:S(2)}) %collective-permute-start.2) | collective-permute-done | bytes 138272 | tf_op jit(solution)/shard_map/ppermute | solution.py:547
  18.4 1.0 %collective-permute-done.4.refs_3_.refs_4_ = bf16[24,2880]{1,0:T(8,128)(2,1)} collective-permute-done((bf16[24,2880]{1,0:T(8,128)(2,1)S(1)}, bf16[24,2880]{1,0:T(8,128)(2,1)}, u32[]{:S(2)}, u32[]{:S(2)}) %collective-permute-start.4) | collective-permute-done | bytes 138272 | tf_op jit(solution)/shard_map/ppermute | solution.py:547
  19.9 1.1 %copy-done.2 = bf16[2880,128]{1,0:T(8,128)(2,1)S(1)} copy-done((bf16[2880,128]{1,0:T(8,128)(2,1)S(1)}, bf16[2880,128]{1,0:T(8,128)(2,1)}, u32[]{:S(2)}) %copy-start.2) | copy-done | bytes 737304
  21.0 2.6 %shard_map.168 = (bf16[48,640]{1,0:T(8,128)(2,1)S(1)}, bf16[48,640]{1,0:T(8,128)(2,1)S(1)}, bf16[48,640]{1,0:T(8,128)(2,1)S(1)}, bf16[48,640]{1,0:T(8,128)(2,1)S(1)}) custom-call(bf16[24,2880]{1,0:T(8,128)(2,1)S(1)} %copy-done, bf16[24,2880]{1,0:T(8,128)(2,1)} %collective-permute-done.refs_1_.refs_2_, ...), custom_call_target="tpu_custom_call" | custom-call | flops 707788800 | bytes 3686400 | tf_op jit(solution)/shard_map/pallas_call | solution.py:238
  24.0 3.1 %collective-permute-start.8 = (bf16[48,640]{1,0:T(8,128)(2,1)S(1)}, bf16[48,640]{1,0:T(8,128)(2,1)S(1)}, u32[]{:S(2)}, u32[]{:S(2)}) collective-permute-start(bf16[48,640]{1,0:T(8,128)(2,1)S(1)} %get-tuple-element.94), channel_id=1, source_target_pairs={{0,4},{1,5},{2,6},{3,7},{4,0},{5,1},{6,2},{7,3},{8,12},{9,13},{10,... | collective-permute-start | bytes 184328 | tf_op jit(solution)/shard_map/ppermute | solution.py:547
  27.1 1.3 %collective-permute-start.9 = (bf16[48,640]{1,0:T(8,128)(2,1)S(1)}, bf16[48,640]{1,0:T(8,128)(2,1)S(1)}, u32[]{:S(2)}, u32[]{:S(2)}) collective-permute-start(bf16[48,640]{1,0:T(8,128)(2,1)S(1)} %get-tuple-element.95), channel_id=1, source_target_pairs={{0,6},{1,7},{2,4},{3,5},{4,2},{5,3},{6,0},{7,1},{8,14},{9,15},{10,... | collective-permute-start | bytes 184328 | tf_op jit(solution)/shard_map/ppermute | solution.py:547
  30.4 2.2 %shard_map.171 = (bf16[2048,512]{1,0:T(8,128)(2,1)S(1)}, bf16[2048,512]{1,0:T(8,128)(2,1)S(1)}) custom-call(bf16[2048,512]{1,0:T(8,128)(2,1)} %bitcast.16, bf16[2048,512]{1,0:T(8,128)(2,1)} %bitcast.17), custom_call_target="tpu_custom_call" | custom-call | bytes 8388608 | tf_op jit(solution)/shard_map/pallas_call | solution.py:271
  32.6 1.6 %shard_map.170.refs_12_ = f32[24,2880]{1,0:T(8,128)S(1)} custom-call(s32[1]{0:T(128)} %bitcast.refs_0_.me_ref, bf16[24,2880]{1,0:T(8,128)(2,1)S(1)} %copy-done, bf16[24,2880]{1,0:T(8,128)(2,1)} %collective-permute-done.refs_1_.refs_2_, bf16[24,2880]{1,0:T(8,128)(2,1)S(1)} %collective-permute-done.1.refs_2_.refs_3_, ...), custom_call_target="tpu_custom_call" | custom-call | flops 26542080 | bytes 2211840 | tf_op jit(solution)/shard_map/pallas_call | solution.py:238
  36.3 6.8 %shard_map.172 = (bf16[24,1024]{1,0:T(8,128)(2,1)S(1)}, bf16[24,1024]{1,0:T(8,128)(2,1)S(1)}, bf16[24,1024]{1,0:T(8,128)(2,1)S(1)}, bf16[24,1024]{1,0:T(8,128)(2,1)S(1)}, bf16[8,1024]{1,0:T(8,128)(2,1)}) custom-call(s32[1]{0:T(128)} %bitcast.refs_0_.me_ref, s32[1]{0:T(128)S(6)} %copy.18.lens.refs_1_, bf16[48,640]{1,0:T(8,128)(2,1)S(1)} %get-tuple-element.107.refs_2_, ...), custom_call_target="tpu_custom_call" | custom-call | flops 805306368 | bytes 4194304 | tf_op jit(solution)/shard_map/pallas_call | solution.py:238
  43.1 3.1 %collective-permute-start.15 = (bf16[24,1024]{1,0:T(8,128)(2,1)S(1)}, bf16[24,1024]{1,0:T(8,128)(2,1)S(1)}, u32[]{:S(2)}, u32[]{:S(2)}) collective-permute-start(bf16[24,1024]{1,0:T(8,128)(2,1)S(1)} %get-tuple-element.124), channel_id=1, source_target_pairs={{0,4},{1,5},{2,6},{3,7},{4,0},{5,1},{6,2},{7,3},{8,12},{9,13},{10,... | collective-permute-start | bytes 147464 | tf_op jit(solution)/shard_map/ppermute | solution.py:547
  46.2 1.3 %collective-permute-start.16 = (bf16[24,1024]{1,0:T(8,128)(2,1)S(1)}, bf16[24,1024]{1,0:T(8,128)(2,1)S(1)}, u32[]{:S(2)}, u32[]{:S(2)}) collective-permute-start(bf16[24,1024]{1,0:T(8,128)(2,1)S(1)} %get-tuple-element.125), channel_id=1, source_target_pairs={{0,6},{1,7},{2,4},{3,5},{4,2},{5,3},{6,0},{7,1},{8,14},{9,15},{10,... | collective-permute-start | bytes 147464 | tf_op jit(solution)/shard_map/ppermute | solution.py:547
  47.5 1.8 %shard_map.173.refs_9_.refs_5_ = bf16[2880,512]{1,0:T(8,128)(2,1)S(1)} custom-call(bf16[2880,512]{1,0:T(8,128)(2,1)} %bitcast.15), custom_call_target="tpu_custom_call" | custom-call | bytes 5898240 | tf_op jit(solution)/shard_map/pallas_call | solution.py:271
  49.4 2.7 %collective-permute-done.16.refs_7_.refs_4_ = bf16[24,1024]{1,0:T(8,128)(2,1)S(1)} collective-permute-done((bf16[24,1024]{1,0:T(8,128)(2,1)S(1)}, bf16[24,1024]{1,0:T(8,128)(2,1)S(1)}, u32[]{:S(2)}, u32[]{:S(2)}) %collective-permute-start.16) | collective-permute-done | bytes 49184 | tf_op jit(solution)/shard_map/ppermute | solution.py:547
  54.0 2.2 %shard_map.174 = (f32[24,2880]{1,0:T(8,128)S(1)}, bf16[24,2880]{1,0:T(8,128)(2,1)S(1)}, bf16[24,2880]{1,0:T(8,128)(2,1)S(1)}, bf16[24,2880]{1,0:T(8,128)(2,1)S(1)}) custom-call(s32[1]{0:T(128)} %bitcast.refs_0_.me_ref, bf16[24,1024]{1,0:T(8,128)(2,1)S(1)} %get-tuple-element.127.refs_1_, bf16[24,1024]{1,0:T(8,128)(2,1)S(1)} %collective-permute-done.17.refs_2_, ...), custom_call_target="tpu_custom_call" | custom-call | flops 566231040 | bytes 5898240 | tf_op jit(solution)/shard_map/pallas_call | solution.py:238
  56.1 0.8 collective-permute-start.23
  56.9 0.8 collective-permute-start.24
  57.7 2.0 %collective-permute-start.22 = (bf16[24,2880]{1,0:T(8,128)(2,1)S(1)}, bf16[24,2880]{1,0:T(8,128)(2,1)S(1)}, u32[]{:S(2)}, u32[]{:S(2)}) collective-permute-start(bf16[24,2880]{1,0:T(8,128)(2,1)S(1)} %get-tuple-element.135), channel_id=1, source_target_pairs={{0,2},{1,3},{2,0},{3,1},{4,6},{5,7},{6,4},{7,5},{8,10},{9,11},{10,... | collective-permute-start | bytes 414728 | tf_op jit(solution)/shard_map/ppermute | solution.py:547
  59.7 8.3 %shard_map.176 = (bf16[1440,2880]{1,0:T(8,128)(2,1)S(1)}, bf16[1440,2880]{1,0:T(8,128)(2,1)S(1)}, bf16[1440,2880]{1,0:T(8,128)(2,1)S(1)}) custom-call(bf16[1440,2880]{1,0:T(8,128)(2,1)} %refs_0_.4, bf16[1440,2880]{1,0:T(8,128)(2,1)} %refs_1_.5, bf16[1440,2880]{1,0:T(8,128)(2,1)} %refs_2_), custom_call_target="tpu_custom_call" | custom-call | bytes 49766400 | tf_op jit(solution)/shard_map/pallas_call | solution.py:271
  68.0 2.1 %shard_map.175.refs_4_ = f32[96,2880]{1,0:T(8,128)S(1)} custom-call(s32[1]{0:T(128)} %bitcast.refs_0_.me_ref, bf16[24,1024]{1,0:T(8,128)(2,1)S(1)} %get-tuple-element.127.refs_1_, bf16[24,1024]{1,0:T(8,128)(2,1)S(1)} %collective-permute-done.14.refs_3_.refs_2_, bf16[24,1024]{1,0:T(8,128)(2,1)S(1)} %collective-permute-done.15.refs_5_.refs_3_, ...), custom_call_target="tpu_custom_call" | custom-call | flops 566231040 | bytes 5898240 | tf_op jit(solution)/shard_map/pallas_call | solution.py:238
  70.2 1.3 %collective-permute-done.25.theirs = bf16[24,2880]{1,0:T(8,128)(2,1)S(1)} collective-permute-done((bf16[24,2880]{1,0:T(8,128)(2,1)S(1)}, bf16[24,2880]{1,0:T(8,128)(2,1)S(1)}, u32[]{:S(2)}, u32[]{:S(2)}) %collective-permute-start.25) | collective-permute-done | bytes 138272 | tf_op jit(solution)/shard_map/ppermute | solution.py:547
  71.6 6.1 %shard_map.177.refs_1_ = bf16[48,2880]{1,0:T(8,128)(2,1)S(1)} custom-call(s32[1]{0:T(128)} %bitcast.refs_0_.me_ref, bf16[24,2880]{1,0:T(8,128)(2,1)S(1)} %add_convert_fusion.1.mine, bf16[24,2880]{1,0:T(8,128)(2,1)S(1)} %collective-permute-done.25.theirs, f32[1,2880]{1,0:T(1,128)S(1)} %reshape.15.gain, bf16[32,2880]{1,0:T(8,128)(2,1)S(1)} %bitcast.10, ...), custom_call_target="tpu_custom_call" | custom-call | flops 1194393600 | bytes 24883200 | tf_op jit(solution)/shard_map/pallas_call | solution.py:238
  77.9 1.4 %collective-permute-done.26.refs_2_ = bf16[48,2880]{1,0:T(8,128)(2,1)S(1)} collective-permute-done((bf16[48,2880]{1,0:T(8,128)(2,1)S(1)}, bf16[48,2880]{1,0:T(8,128)(2,1)S(1)}, u32[]{:S(2)}, u32[]{:S(2)}) %collective-permute-start.26) | collective-permute-done | bytes 276512 | tf_op jit(solution)/shard_map/ppermute | solution.py:547
  79.4 0.8 shard_map.178
  80.1 1.5 %collective-permute-start.27 = (bf16[24,2880]{1,0:T(8,128)(2,1)S(1)}, bf16[24,2880]{1,0:T(8,128)(2,1)S(1)}, u32[]{:S(2)}, u32[]{:S(2)}) collective-permute-start(bf16[24,2880]{1,0:T(8,128)(2,1)S(1)} %get-tuple-element.155), channel_id=1, source_target_pairs={{0,2},{1,3},{2,0},{3,1},{4,6},{5,7},{6,4},{7,5},{8,10},{9,11},{10,... | collective-permute-start | bytes 414728 | tf_op jit(solution)/shard_map/ppermute | solution.py:547
  81.7 1.3 %collective-permute-start.28 = (bf16[24,2880]{1,0:T(8,128)(2,1)S(1)}, bf16[24,2880]{1,0:T(8,128)(2,1)S(1)}, u32[]{:S(2)}, u32[]{:S(2)}) collective-permute-start(bf16[24,2880]{1,0:T(8,128)(2,1)S(1)} %get-tuple-element.156), channel_id=1, source_target_pairs={{0,4},{1,5},{2,6},{3,7},{4,0},{5,1},{6,2},{7,3},{8,12},{9,13},{10,... | collective-permute-start | bytes 414728 | tf_op jit(solution)/shard_map/ppermute | solution.py:547
  82.9 1.7 %collective-permute-start.29 = (bf16[24,2880]{1,0:T(8,128)(2,1)S(1)}, bf16[24,2880]{1,0:T(8,128)(2,1)S(1)}, u32[]{:S(2)}, u32[]{:S(2)}) collective-permute-start(bf16[24,2880]{1,0:T(8,128)(2,1)S(1)} %get-tuple-element.157), channel_id=1, source_target_pairs={{0,6},{1,7},{2,4},{3,5},{4,2},{5,3},{6,0},{7,1},{8,14},{9,15},{10,... | collective-permute-start | bytes 414728 | tf_op jit(solution)/shard_map/ppermute | solution.py:547
  84.6 3.7 %collective-permute-done.27 = bf16[24,2880]{1,0:T(8,128)(2,1)S(1)} collective-permute-done((bf16[24,2880]{1,0:T(8,128)(2,1)S(1)}, bf16[24,2880]{1,0:T(8,128)(2,1)S(1)}, u32[]{:S(2)}, u32[]{:S(2)}) %collective-permute-start.27) | collective-permute-done | bytes 138272 | tf_op jit(solution)/shard_map/ppermute | solution.py:547
  88.3 6.9 %collective-permute-done.28 = bf16[24,2880]{1,0:T(8,128)(2,1)S(1)} collective-permute-done((bf16[24,2880]{1,0:T(8,128)(2,1)S(1)}, bf16[24,2880]{1,0:T(8,128)(2,1)S(1)}, u32[]{:S(2)}, u32[]{:S(2)}) %collective-permute-start.28) | collective-permute-done | bytes 138272 | tf_op jit(solution)/shard_map/ppermute | solution.py:547
  95.2 0.7 add_convert_fusion
  (57 shorter events, 9.0 us)
Async XLA Ops:
  0.6 19.3 %copy-start = (bf16[24,2880]{1,0:T(8,128)(2,1)S(1)}, bf16[24,2880]{1,0:T(8,128)(2,1)}, u32[]{:S(2)}) copy-start(bf16[24,2880]{1,0:T(8,128)(2,1)} %refs_5_.1) | copy-start | bytes 414724
  0.6 10.8 %collective-permute-start.3 = (bf16[24,2880]{1,0:T(8,128)(2,1)}, bf16[24,2880]{1,0:T(8,128)(2,1)S(1)}, u32[]{:S(2)}, u32[]{:S(2)}) collective-permute-start(bf16[24,2880]{1,0:T(8,128)(2,1)} %refs_5_.1), channel_id=1, source_target_pairs={{0,6},{1,7},{2,4},{3,5},{4,2},{5,3},{6,0},{7,1},{8,14},{9,15},{10,... | collective-permute-start | bytes 414728 | tf_op jit(solution)/shard_map/ppermute | solution.py:547
  5.8 12.2 %collective-permute-start.2 = (bf16[24,2880]{1,0:T(8,128)(2,1)}, bf16[24,2880]{1,0:T(8,128)(2,1)S(1)}, u32[]{:S(2)}, u32[]{:S(2)}) collective-permute-start(bf16[24,2880]{1,0:T(8,128)(2,1)} %refs_5_.1), channel_id=1, source_target_pairs={{0,4},{1,5},{2,6},{3,7},{4,0},{5,1},{6,2},{7,3},{8,12},{9,13},{10,... | collective-permute-start | bytes 414728 | tf_op jit(solution)/shard_map/ppermute | solution.py:547
  5.8 12.2 %collective-permute-start.1 = (bf16[24,2880]{1,0:T(8,128)(2,1)}, bf16[24,2880]{1,0:T(8,128)(2,1)S(1)}, u32[]{:S(2)}, u32[]{:S(2)}) collective-permute-start(bf16[24,2880]{1,0:T(8,128)(2,1)} %refs_5_.1), channel_id=1, source_target_pairs={{0,2},{1,3},{2,0},{3,1},{4,6},{5,7},{6,4},{7,5},{8,10},{9,11},{10,... | collective-permute-start | bytes 414728 | tf_op jit(solution)/shard_map/ppermute | solution.py:547
  6.4 12.0 %collective-permute-start = (bf16[24,2880]{1,0:T(8,128)(2,1)}, bf16[24,2880]{1,0:T(8,128)(2,1)}, u32[]{:S(2)}, u32[]{:S(2)}) collective-permute-start(bf16[24,2880]{1,0:T(8,128)(2,1)} %refs_5_.1), channel_id=1, source_target_pairs={{0,1},{1,0},{2,3},{3,2},{4,5},{5,4},{6,7},{7,6},{8,9},{9,8},{10,11... | collective-permute-start | bytes 414728 | tf_op jit(solution)/shard_map/ppermute | solution.py:547
  17.9 1.5 %collective-permute-start.4 = (bf16[24,2880]{1,0:T(8,128)(2,1)S(1)}, bf16[24,2880]{1,0:T(8,128)(2,1)}, u32[]{:S(2)}, u32[]{:S(2)}) collective-permute-start(bf16[24,2880]{1,0:T(8,128)(2,1)S(1)} %collective-permute-done.1.refs_2_.refs_3_), channel_id=1, source_target_pairs={{0,1},{1,0},{2,3},{3,2},{4,5},{5,4},{6,7},{7,6},{8,9},{9,8},{10,11... | collective-permute-start | bytes 414728 | tf_op jit(solution)/shard_map/ppermute | solution.py:547
  17.9 1.7 %collective-permute-start.5 = (bf16[24,2880]{1,0:T(8,128)(2,1)S(1)}, bf16[24,2880]{1,0:T(8,128)(2,1)}, u32[]{:S(2)}, u32[]{:S(2)}) collective-permute-start(bf16[24,2880]{1,0:T(8,128)(2,1)S(1)} %collective-permute-done.2.refs_4_.refs_5_), channel_id=1, source_target_pairs={{0,1},{1,0},{2,3},{3,2},{4,5},{5,4},{6,7},{7,6},{8,9},{9,8},{10,11... | collective-permute-start | bytes 414728 | tf_op jit(solution)/shard_map/ppermute | solution.py:547
  18.4 1.5 %collective-permute-start.6 = (bf16[24,2880]{1,0:T(8,128)(2,1)S(1)}, bf16[24,2880]{1,0:T(8,128)(2,1)}, u32[]{:S(2)}, u32[]{:S(2)}) collective-permute-start(bf16[24,2880]{1,0:T(8,128)(2,1)S(1)} %collective-permute-done.3.refs_6_.refs_7_), channel_id=1, source_target_pairs={{0,1},{1,0},{2,3},{3,2},{4,5},{5,4},{6,7},{7,6},{8,9},{9,8},{10,11... | collective-permute-start | bytes 414728 | tf_op jit(solution)/shard_map/ppermute | solution.py:547
  23.7 8.9 %copy-start.4 = (s32[192,4]{0,1:T(4,128)S(1)}, s32[192,4]{0,1:T(4,128)}, u32[]{:S(2)}) copy-start(s32[192,4]{0,1:T(4,128)} %param.28) | copy-start | bytes 9220
  23.7 30.3 %collective-permute-start.21 = (bf16[512,2880]{0,1:T(8,128)(2,1)S(1)}, bf16[512,2880]{0,1:T(8,128)(2,1)S(1)}, u32[]{:S(2)}, u32[]{:S(2)}) collective-permute-start(bf16[512,2880]{0,1:T(8,128)(2,1)S(1)} %copy-done.5), channel_id=1, source_target_pairs={{0,1},{1,0},{2,3},{3,2},{4,5},{5,4},{6,7},{7,6},{8,9},{9,8},{10,11... | collective-permute-start | bytes 8847368 | tf_op jit(solution)/shard_map/ppermute | solution.py:547
  24.0 10.3 %collective-permute-start.7 = (bf16[48,640]{1,0:T(8,128)(2,1)S(1)}, bf16[48,640]{1,0:T(8,128)(2,1)S(1)}, u32[]{:S(2)}, u32[]{:S(2)}) collective-permute-start(bf16[48,640]{1,0:T(8,128)(2,1)S(1)} %get-tuple-element.93), channel_id=1, source_target_pairs={{0,2},{1,3},{2,0},{3,1},{4,6},{5,7},{6,4},{7,5},{8,10},{9,11},{10,... | collective-permute-start | bytes 184328 | tf_op jit(solution)/shard_map/ppermute | solution.py:547
  24.0 10.3 %collective-permute-start.8 = (bf16[48,640]{1,0:T(8,128)(2,1)S(1)}, bf16[48,640]{1,0:T(8,128)(2,1)S(1)}, u32[]{:S(2)}, u32[]{:S(2)}) collective-permute-start(bf16[48,640]{1,0:T(8,128)(2,1)S(1)} %get-tuple-element.94), channel_id=1, source_target_pairs={{0,4},{1,5},{2,6},{3,7},{4,0},{5,1},{6,2},{7,3},{8,12},{9,13},{10,... | collective-permute-start | bytes 184328 | tf_op jit(solution)/shard_map/ppermute | solution.py:547
  27.1 7.2 %collective-permute-start.9 = (bf16[48,640]{1,0:T(8,128)(2,1)S(1)}, bf16[48,640]{1,0:T(8,128)(2,1)S(1)}, u32[]{:S(2)}, u32[]{:S(2)}) collective-permute-start(bf16[48,640]{1,0:T(8,128)(2,1)S(1)} %get-tuple-element.95), channel_id=1, source_target_pairs={{0,6},{1,7},{2,4},{3,5},{4,2},{5,3},{6,0},{7,1},{8,14},{9,15},{10,... | collective-permute-start | bytes 184328 | tf_op jit(solution)/shard_map/ppermute | solution.py:547
  34.3 1.3 %collective-permute-start.10 = (bf16[48,640]{1,0:T(8,128)(2,1)S(1)}, bf16[48,640]{1,0:T(8,128)(2,1)S(1)}, u32[]{:S(2)}, u32[]{:S(2)}) collective-permute-start(bf16[48,640]{1,0:T(8,128)(2,1)S(1)} %get-tuple-element.107.refs_2_), channel_id=1, source_target_pairs={{0,1},{1,0},{2,3},{3,2},{4,5},{5,4},{6,7},{7,6},{8,9},{9,8},{10,11... | collective-permute-start | bytes 184328 | tf_op jit(solution)/shard_map/ppermute | solution.py:547
  34.4 1.4 %collective-permute-start.11 = (bf16[48,640]{1,0:T(8,128)(2,1)S(1)}, bf16[48,640]{1,0:T(8,128)(2,1)S(1)}, u32[]{:S(2)}, u32[]{:S(2)}) collective-permute-start(bf16[48,640]{1,0:T(8,128)(2,1)S(1)} %collective-permute-done.7.refs_3_), channel_id=1, source_target_pairs={{0,1},{1,0},{2,3},{3,2},{4,5},{5,4},{6,7},{7,6},{8,9},{9,8},{10,11... | collective-permute-start | bytes 184328 | tf_op jit(solution)/shard_map/ppermute | solution.py:547
  34.9 1.2 %collective-permute-start.12 = (bf16[48,640]{1,0:T(8,128)(2,1)S(1)}, bf16[48,640]{1,0:T(8,128)(2,1)S(1)}, u32[]{:S(2)}, u32[]{:S(2)}) collective-permute-start(bf16[48,640]{1,0:T(8,128)(2,1)S(1)} %collective-permute-done.8.refs_4_), channel_id=1, source_target_pairs={{0,1},{1,0},{2,3},{3,2},{4,5},{5,4},{6,7},{7,6},{8,9},{9,8},{10,11... | collective-permute-start | bytes 184328 | tf_op jit(solution)/shard_map/ppermute | solution.py:547
  34.9 1.3 %collective-permute-start.13 = (bf16[48,640]{1,0:T(8,128)(2,1)S(1)}, bf16[48,640]{1,0:T(8,128)(2,1)S(1)}, u32[]{:S(2)}, u32[]{:S(2)}) collective-permute-start(bf16[48,640]{1,0:T(8,128)(2,1)S(1)} %collective-permute-done.9.refs_5_), channel_id=1, source_target_pairs={{0,1},{1,0},{2,3},{3,2},{4,5},{5,4},{6,7},{7,6},{8,9},{9,8},{10,11... | collective-permute-start | bytes 184328 | tf_op jit(solution)/shard_map/ppermute | solution.py:547
  43.1 6.2 %collective-permute-start.14 = (bf16[24,1024]{1,0:T(8,128)(2,1)S(1)}, bf16[24,1024]{1,0:T(8,128)(2,1)S(1)}, u32[]{:S(2)}, u32[]{:S(2)}) collective-permute-start(bf16[24,1024]{1,0:T(8,128)(2,1)S(1)} %get-tuple-element.123), channel_id=1, source_target_pairs={{0,2},{1,3},{2,0},{3,1},{4,6},{5,7},{6,4},{7,5},{8,10},{9,11},{10,... | collective-permute-start | bytes 147464 | tf_op jit(solution)/shard_map/ppermute | solution.py:547
  43.1 6.2 %collective-permute-start.15 = (bf16[24,1024]{1,0:T(8,128)(2,1)S(1)}, bf16[24,1024]{1,0:T(8,128)(2,1)S(1)}, u32[]{:S(2)}, u32[]{:S(2)}) collective-permute-start(bf16[24,1024]{1,0:T(8,128)(2,1)S(1)} %get-tuple-element.124), channel_id=1, source_target_pairs={{0,4},{1,5},{2,6},{3,7},{4,0},{5,1},{6,2},{7,3},{8,12},{9,13},{10,... | collective-permute-start | bytes 147464 | tf_op jit(solution)/shard_map/ppermute | solution.py:547
  46.2 5.9 %collective-permute-start.16 = (bf16[24,1024]{1,0:T(8,128)(2,1)S(1)}, bf16[24,1024]{1,0:T(8,128)(2,1)S(1)}, u32[]{:S(2)}, u32[]{:S(2)}) collective-permute-start(bf16[24,1024]{1,0:T(8,128)(2,1)S(1)} %get-tuple-element.125), channel_id=1, source_target_pairs={{0,6},{1,7},{2,4},{3,5},{4,2},{5,3},{6,0},{7,1},{8,14},{9,15},{10,... | collective-permute-start | bytes 147464 | tf_op jit(solution)/shard_map/ppermute | solution.py:547
  52.1 1.2 %collective-permute-start.17 = (bf16[24,1024]{1,0:T(8,128)(2,1)S(1)}, bf16[24,1024]{1,0:T(8,128)(2,1)S(1)}, u32[]{:S(2)}, u32[]{:S(2)}) collective-permute-start(bf16[24,1024]{1,0:T(8,128)(2,1)S(1)} %get-tuple-element.127.refs_1_), channel_id=1, source_target_pairs={{0,1},{1,0},{2,3},{3,2},{4,5},{5,4},{6,7},{7,6},{8,9},{9,8},{10,11... | collective-permute-start | bytes 147464 | tf_op jit(solution)/shard_map/ppermute | solution.py:547
  52.1 1.4 %collective-permute-start.18 = (bf16[24,1024]{1,0:T(8,128)(2,1)S(1)}, bf16[24,1024]{1,0:T(8,128)(2,1)S(1)}, u32[]{:S(2)}, u32[]{:S(2)}) collective-permute-start(bf16[24,1024]{1,0:T(8,128)(2,1)S(1)} %collective-permute-done.14.refs_3_.refs_2_), channel_id=1, source_target_pairs={{0,1},{1,0},{2,3},{3,2},{4,5},{5,4},{6,7},{7,6},{8,9},{9,8},{10,11... | collective-permute-start | bytes 147464 | tf_op jit(solution)/shard_map/ppermute | solution.py:547
  52.6 1.2 %collective-permute-start.19 = (bf16[24,1024]{1,0:T(8,128)(2,1)S(1)}, bf16[24,1024]{1,0:T(8,128)(2,1)S(1)}, u32[]{:S(2)}, u32[]{:S(2)}) collective-permute-start(bf16[24,1024]{1,0:T(8,128)(2,1)S(1)} %collective-permute-done.15.refs_5_.refs_3_), channel_id=1, source_target_pairs={{0,1},{1,0},{2,3},{3,2},{4,5},{5,4},{6,7},{7,6},{8,9},{9,8},{10,11... | collective-permute-start | bytes 147464 | tf_op jit(solution)/shard_map/ppermute | solution.py:547
  52.6 1.4 %collective-permute-start.20 = (bf16[24,1024]{1,0:T(8,128)(2,1)S(1)}, bf16[24,1024]{1,0:T(8,128)(2,1)S(1)}, u32[]{:S(2)}, u32[]{:S(2)}) collective-permute-start(bf16[24,1024]{1,0:T(8,128)(2,1)S(1)} %collective-permute-done.16.refs_7_.refs_4_), channel_id=1, source_target_pairs={{0,1},{1,0},{2,3},{3,2},{4,5},{5,4},{6,7},{7,6},{8,9},{9,8},{10,11... | collective-permute-start | bytes 147464 | tf_op jit(solution)/shard_map/ppermute | solution.py:547
  56.1 13.9 %collective-permute-start.23 = (bf16[24,2880]{1,0:T(8,128)(2,1)S(1)}, bf16[24,2880]{1,0:T(8,128)(2,1)S(1)}, u32[]{:S(2)}, u32[]{:S(2)}) collective-permute-start(bf16[24,2880]{1,0:T(8,128)(2,1)S(1)} %get-tuple-element.136), channel_id=1, source_target_pairs={{0,4},{1,5},{2,6},{3,7},{4,0},{5,1},{6,2},{7,3},{8,12},{9,13},{10,... | collective-permute-start | bytes 414728 | tf_op jit(solution)/shard_map/ppermute | solution.py:547
  56.9 13.1 %collective-permute-start.24 = (bf16[24,2880]{1,0:T(8,128)(2,1)S(1)}, bf16[24,2880]{1,0:T(8,128)(2,1)S(1)}, u32[]{:S(2)}, u32[]{:S(2)}) collective-permute-start(bf16[24,2880]{1,0:T(8,128)(2,1)S(1)} %get-tuple-element.137), channel_id=1, source_target_pairs={{0,6},{1,7},{2,4},{3,5},{4,2},{5,3},{6,0},{7,1},{8,14},{9,15},{10,... | collective-permute-start | bytes 414728 | tf_op jit(solution)/shard_map/ppermute | solution.py:547
  57.7 12.4 %collective-permute-start.22 = (bf16[24,2880]{1,0:T(8,128)(2,1)S(1)}, bf16[24,2880]{1,0:T(8,128)(2,1)S(1)}, u32[]{:S(2)}, u32[]{:S(2)}) collective-permute-start(bf16[24,2880]{1,0:T(8,128)(2,1)S(1)} %get-tuple-element.135), channel_id=1, source_target_pairs={{0,2},{1,3},{2,0},{3,1},{4,6},{5,7},{6,4},{7,5},{8,10},{9,11},{10,... | collective-permute-start | bytes 414728 | tf_op jit(solution)/shard_map/ppermute | solution.py:547
  70.2 1.4 %collective-permute-start.25 = (bf16[24,2880]{1,0:T(8,128)(2,1)S(1)}, bf16[24,2880]{1,0:T(8,128)(2,1)S(1)}, u32[]{:S(2)}, u32[]{:S(2)}) collective-permute-start(bf16[24,2880]{1,0:T(8,128)(2,1)S(1)} %add_convert_fusion.1.mine), channel_id=1, source_target_pairs={{0,1},{1,0},{2,3},{3,2},{4,5},{5,4},{6,7},{7,6},{8,9},{9,8},{10,11... | collective-permute-start | bytes 414728 | tf_op jit(solution)/shard_map/ppermute | solution.py:547
  77.7 1.6 %collective-permute-start.26 = (bf16[48,2880]{1,0:T(8,128)(2,1)S(1)}, bf16[48,2880]{1,0:T(8,128)(2,1)S(1)}, u32[]{:S(2)}, u32[]{:S(2)}) collective-permute-start(bf16[48,2880]{1,0:T(8,128)(2,1)S(1)} %shard_map.177.refs_1_), channel_id=1, source_target_pairs={{0,1},{1,0},{2,3},{3,2},{4,5},{5,4},{6,7},{7,6},{8,9},{9,8},{10,11... | collective-permute-start | bytes 829448 | tf_op jit(solution)/shard_map/ppermute | solution.py:547
  80.1 8.2 %collective-permute-start.27 = (bf16[24,2880]{1,0:T(8,128)(2,1)S(1)}, bf16[24,2880]{1,0:T(8,128)(2,1)S(1)}, u32[]{:S(2)}, u32[]{:S(2)}) collective-permute-start(bf16[24,2880]{1,0:T(8,128)(2,1)S(1)} %get-tuple-element.155), channel_id=1, source_target_pairs={{0,2},{1,3},{2,0},{3,1},{4,6},{5,7},{6,4},{7,5},{8,10},{9,11},{10,... | collective-permute-start | bytes 414728 | tf_op jit(solution)/shard_map/ppermute | solution.py:547
  81.7 13.6 %collective-permute-start.28 = (bf16[24,2880]{1,0:T(8,128)(2,1)S(1)}, bf16[24,2880]{1,0:T(8,128)(2,1)S(1)}, u32[]{:S(2)}, u32[]{:S(2)}) collective-permute-start(bf16[24,2880]{1,0:T(8,128)(2,1)S(1)} %get-tuple-element.156), channel_id=1, source_target_pairs={{0,4},{1,5},{2,6},{3,7},{4,0},{5,1},{6,2},{7,3},{8,12},{9,13},{10,... | collective-permute-start | bytes 414728 | tf_op jit(solution)/shard_map/ppermute | solution.py:547
  82.9 12.3 %collective-permute-start.29 = (bf16[24,2880]{1,0:T(8,128)(2,1)S(1)}, bf16[24,2880]{1,0:T(8,128)(2,1)S(1)}, u32[]{:S(2)}, u32[]{:S(2)}) collective-permute-start(bf16[24,2880]{1,0:T(8,128)(2,1)S(1)} %get-tuple-element.157), channel_id=1, source_target_pairs={{0,6},{1,7},{2,4},{3,5},{4,2},{5,3},{6,0},{7,1},{8,14},{9,15},{10,... | collective-permute-start | bytes 414728 | tf_op jit(solution)/shard_map/ppermute | solution.py:547
  (4 other events, 8.3 us)

commit v3 on v2

--- a/solution.py
+++ b/solution.py
@@ -328,7 +328,7 @@
 
 
 def project_kernel(*refs):
-    pieces, (gain, w_query, w_keyval), rest = refs[:8], refs[8:11], refs[11:]
+    pieces, (gain, *weights), rest = refs[:4], refs[4:9], refs[9:]
     outs, normed = rest[:4], rest[4]
     count = pieces[0].shape[0]
     for k, piece in enumerate(pieces):
@@ -336,25 +336,27 @@
         mean_sq = jnp.mean(floats * floats, axis=-1, keepdims=True)
         normed[k * count : (k + 1) * count, :] = floats * lax.rsqrt(mean_sq + EPSILON) * gain[...]
     rows = normed[...].astype(jnp.bfloat16)
-    query = dot_nn(rows, w_query[...]).astype(jnp.bfloat16)
-    keyval = dot_nn(rows, w_keyval[...]).astype(jnp.bfloat16)
-    split = w_query.shape[1]
-    for i, out in enumerate(outs):
-        out[:, :split] = query[2 * count * i : 2 * count * (i + 1)]
-        out[:, split:] = keyval[2 * count * i : 2 * count * (i + 1)]
+    at = 0
+    for weight in weights:
+        result = dot_nn(rows, weight[...])
+        width = weight.shape[1]
+        for i, out in enumerate(outs):
+            out[:, at : at + width] = result[count * i : count * (i + 1)].astype(jnp.bfloat16)
+        at += width
 
 
 def attend_kernel(*refs):
     me, lens = refs[0][0], refs[1][0]
-    straight, crossed = refs[2:6], refs[6:10]
-    cos, sin, bias, pick, keys, values = refs[10:16]
-    outs, accepted_out = refs[16:20], refs[20]
-    blocks, queries, new_keys, new_values, attended = refs[21:]
+    arrived = refs[2:6]
+    cos, sin, bias, pick, keys, values = refs[6:12]
+    outs, accepted_out = refs[12:16], refs[16]
+    blocks, queries, new_keys, new_values, attended = refs[17:]
     draft = cos.shape[0]
     lanes = 2 * HEAD_DIM
     for i in range(4):
-        blocks[me ^ (2 * i)] = straight[i][:draft, :].astype(jnp.float32)
-        blocks[me ^ (2 * i + 1)] = crossed[i][draft:, :].astype(jnp.float32)
+        columns = blocks.shape[2]
+        blocks[me ^ (2 * i)] = arrived[i][:, :columns].astype(jnp.float32)
+        blocks[me ^ (2 * i + 1)] = arrived[i][:, columns:].astype(jnp.float32)
     lane = iota((draft, lanes), 1)
     low = jnp.bitwise_and(lane, HEAD_DIM - 1) < HEAD_DIM // 2
     left = lane < HEAD_DIM
@@ -439,9 +441,9 @@
 
 def outproj_kernel(*refs):
     me, pieces = refs[0][0], refs[1:9]
-    w_own, w_other, routes, residual = refs[9:13]
-    own, sends = refs[13], refs[14:17]
-    rows, chosen = refs[17:]
+    w_own, w_other, routes = refs[9:12]
+    own, sends = refs[12], refs[13:16]
+    rows, chosen = refs[16:]
     count = pieces[0].shape[0]
     half = own.shape[0]
     core = me % 2
@@ -455,7 +457,7 @@
     first = jnp.where(core == 0, low, high).astype(jnp.bfloat16)
     second = jnp.where(core == 0, high, low).astype(jnp.bfloat16)
     summed = dot_nt(first, w_own[...]) + dot_nt(second, w_other[...])
-    own[...] = summed[:half] + residual[...]
+    own[...] = summed[:half]
     for i, out in enumerate(sends):
         out[...] = summed[(i + 1) * half : (i + 2) * half].astype(jnp.bfloat16)
 
@@ -553,58 +555,58 @@
     half = capacity // 2
     routes_t = routes.T
     router_t = w_router.T
-    w_out_t = w_out.T
     gain_row = attn_gain.reshape(1, width)
     moe_row = moe_gain.reshape(1, width)
 
     line = {s: swap(hidden, s) for s in (6, 4, 2)}
+    other_query, other_keyval = swap(w_query, 1), swap(w_keyval, 1)
     lanes = 128
     parents = jnp.pad(parents, ((0, 0), (0, lanes - draft)))
     early = (gain_row, moe_row, parents, load(w_query, w_keyval))
     line, early = lax.optimization_barrier((line, early))
     gain_row, moe_row, parents, (near_query, near_keyval) = early
     line[0] = hidden
-    across = {s: swap(line[s], 1) for s in (0, 2, 4, 6)}
-    pieces = [piece for s in (0, 2, 4, 6) for piece in (line[s], across[s])]
 
     queries, keyvals = w_query.shape[1], w_keyval.shape[1]
     columns = queries + keyvals
     projected = run(
         project_kernel,
-        [((2 * rows, columns), bf16)] * 4,
-        [*pieces, gain_row, near(near_query), near(near_keyval)],
+        [((rows, 2 * columns), bf16)] * 4,
+        [
+            *(line[s] for s in (0, 2, 4, 6)),
+            gain_row,
+            near(near_query),
+            near(near_keyval),
+            near(other_query),
+            near(other_keyval),
+        ],
         scalars=0,
-        scratch=[pltpu.VMEM((tokens, width), f32)],
+        scratch=[pltpu.VMEM((4 * rows, width), f32)],
+        limit=10 * MIB,
         flops=2 * tokens * width * columns,
         moved=width * columns * 2,
     )
-    (keys, values, w_pair, lens, me_then), projected = lax.optimization_barrier(
-        ((cache_keys[0], cache_values[0], w_out, cache_lens, me), projected)
-    )
-    straight = [projected[0]] + [swap(projected[i], 2 * i) for i in (1, 2, 3)]
+    later = (line, w_out, cache_keys[0], cache_values[0], cache_lens)
+    later, projected = lax.optimization_barrier((later, projected))
+    line, w_pair, keys, values, lens = later
+    arrived = [projected[0]] + [swap(projected[i], 2 * i) for i in (1, 2, 3)]
     tree = run(
         tree_kernel,
         [((draft, lanes), f32), ((draft, lanes), f32), ((draft, lanes), f32), ((DEPTH, lanes), f32)],
         [lens, accepted, parents],
         scalars=2,
-    )
-    residual = run(
-        residual_kernel,
-        [((half, width), f32)],
-        [me_then, *pieces, routes_t],
-        scratch=[pltpu.VMEM((tokens, width), f32)],
-        flops=2 * half * tokens * width,
-        moved=tokens * width * 4,
-    )[0]
+        limit=4 * MIB,
+    )
     cached = load(keys, values)
-    straight, tree, residual, cached = lax.optimization_barrier((straight, tree, residual, cached))
-    crossed = [swap(block, 1) for block in straight]
-    w_other_t = swap(w_pair, 1).T
+    arrived, tree, cached = lax.optimization_barrier((arrived, tree, cached))
+    across = {s: swap(line[s], 1) for s in (0, 2, 4, 6)}
+    pieces = [piece for s in (0, 2, 4, 6) for piece in (line[s], across[s])]
+    w_other = swap(w_pair, 1)
     slots, kv_cols = cache_keys.shape[1:]
     attended = run(
         attend_kernel,
         [((rows, 2 * queries), bf16)] * 4 + [((DEPTH, 2 * kv_cols), bf16)],
-        [me, cache_lens, *straight, *crossed, *tree, near(cached[0]), near(cached[1])],
+        [me, cache_lens, *arrived, *tree, near(cached[0]), near(cached[1])],
         scalars=2,
         scratch=[
             pltpu.VMEM((devices, rows, columns), f32),
@@ -613,41 +615,54 @@
             pltpu.VMEM((lanes, lanes), f32),
             pltpu.VMEM((devices // 2, rows, 2 * queries), f32),
         ],
+        limit=14 * MIB,
         flops=4 * rows * HEADS * slots * HEAD_DIM,
         moved=4 * slots * kv_cols,
     )
     accepted_kv = attended[4][None]
-    w_out_t, attended = lax.optimization_barrier((w_out_t, attended))
+    (w_own, w_other), attended = lax.optimization_barrier(((w_out, w_other), attended))
     straight = [attended[0]] + [swap(attended[i], 2 * i) for i in (1, 2, 3)]
-    straight, (near_out,) = lax.optimization_barrier((straight, load(w_out_t)))
+    near_out = load(w_own.T, w_other.T)
+    straight, near_out = lax.optimization_barrier((straight, near_out))
     crossed = [swap(block, 1) for block in straight]
-    pieces = [piece for pair in zip(straight, crossed) for piece in pair]
+    blocks = [block for pair in zip(straight, crossed) for block in pair]
     out_flops = 2 * 4 * half * 2 * queries * width
     dispatched = run(
         outproj_kernel,
         [((half, width), f32)] + [((half, width), bf16)] * 3,
-        [me, *pieces, near(near_out), near(w_other_t), routes_t, residual],
+        [me, *blocks, *map(near, near_out), routes_t],
         scratch=[pltpu.VMEM((tokens, 2 * queries), f32), pltpu.VMEM((4 * half, tokens), f32)],
+        limit=10 * MIB,
         flops=out_flops,
         moved=4 * queries * width,
     )
     arrived = [swap(dispatched[i], 2 * i) for i in (1, 2, 3)]
-    me_after = lax.optimization_barrier((me, dispatched[1]))[0]
+    (me_then, experts), _ = lax.optimization_barrier(
+        ((me, (w_gate, w_up, w_down)), dispatched[1])
+    )
     sums = run(
         token_kernel,
         [((4 * rows, width), f32)],
-        [me_after, *straight, near(near_out), near(w_other_t)],
+        [me_then, *straight, *map(near, near_out)],
         scratch=[pltpu.VMEM((4 * rows, 2 * queries), f32)],
         limit=6 * MIB,
         flops=out_flops,
         moved=4 * queries * width,
     )[0]
-    experts, _ = lax.optimization_barrier(((w_gate, w_up, w_down), dispatched[1]))
-    near_gate, near_up, near_down = load(*experts)
-    near_weights = (near_gate, near_up, near_down)
-    middle, arrived, sums, near_weights = lax.optimization_barrier(
-        (dispatched[0], arrived, sums, near_weights)
-    )
+    residual = run(
+        residual_kernel,
+        [((half, width), f32)],
+        [me_then, *pieces, routes_t],
+        scratch=[pltpu.VMEM((tokens, width), f32)],
+        limit=6 * MIB,
+        flops=2 * half * tokens * width,
+        moved=tokens * width * 4,
+    )[0]
+    near_weights = load(*experts)
+    middle, arrived, sums, residual, near_weights = lax.optimization_barrier(
+        (dispatched[0], arrived, sums, residual, near_weights)
+    )
+    middle = middle + residual
     for block in arrived:
         middle = middle + block.astype(f32)
     middle = middle.astype(bf16)

time: 96.3 us -> 89.9 us (0.934)
  local copies, waits for them, and re-layouts: 4.09 us -> 0.05 us
  Pallas kernels: 37.3 us -> 35.9 us
    pallas_call x8, Pallas kernels: 22.9 us -> 20.6 us  [run(): pl.pallas_call(kernel, out_shape=tuple((jax.ShapeDtypeStruct(s, t) for s,...]
    unnamed x12, local copies, waits for them, and re-layouts: 2 us -> 0.02 us
    ppermute x30 -> x28, waiting for transfers between devices: 25.9 us -> 25.3 us  [swap(): return lax.ppermute(values, 'tp', [(i, i ^ offset) for i in range(devices)])]
    ppermute x30 -> x28, starting transfers between devices: 25.7 us -> 25.2 us  [swap(): return lax.ppermute(values, 'tp', [(i, i ^ offset) for i in range(devices)])]
  transfers between devices with their start and end apart: 30 -> 28, of which waited for: 17 -> 10; matrix products, arithmetic and copies ran while one was open for 2% -> 0% of each run, Pallas kernels for 27% -> 31%
where the time goes in v3:
time: 89.9 us; the launch traced here: 89.7 us
  Pallas kernels  35.9 us (40%)
  waiting for transfers between devices  25.3 us (28%)
  starting transfers between devices  25.2 us (28%)
  between operations  2.4 us (3%)
    ppermute x28, waiting for transfers between devices, swap(): return lax.ppermute(values, 'tp', [(i, i ^ offset) for i in range(devices)])  25.3 us
    ppermute x28, starting transfers between devices, swap(): return lax.ppermute(values, 'tp', [(i, i ^ offset) for i in range(devices)])  25.2 us
    pallas_call x8, Pallas kernels, run(): pl.pallas_call(kernel, out_shape=tuple((jax.ShapeDtypeStruct(s, t) for s,...  20.6 us
    pallas_call x4, Pallas kernels, load(): pl.pallas_call(kernel, out_shape=tuple((pltpu.VMEM(a.shape, a.dtype) for...  15.3 us
  transfers between devices with their start and end apart: 28, of which 10 were waited for; matrix products, arithmetic and copies ran while one was open for 0% of the time, Pallas kernels for 31%

profile of v3, /device:TPU:0, one launch (start us, length us, event | category | flops | bytes accessed | tf_op | source)
XLA Modules:
  0.0 89.7 jit_solution(5382352726933581106)
XLA Ops:
  0.7 0.5 collective-permute-start.3
  1.3 5.0 %collective-permute-start.2 = (bf16[24,2880]{1,0:T(8,128)(2,1)}, bf16[24,2880]{1,0:T(8,128)(2,1)S(1)}, u32[]{:S(2)}, u32[]{:S(2)}) collective-permute-start(bf16[24,2880]{1,0:T(8,128)(2,1)} %refs_5_.1), channel_id=1, source_target_pairs={{0,6},{1,7},{2,4},{3,5},{4,2},{5,3},{6,0},{7,1},{8,14},{9,15},{10,... | collective-permute-start | bytes 414728 | tf_op jit(solution)/shard_map/ppermute | solution.py:549
  6.3 0.6 collective-permute-start
  6.9 2.0 %shard_map.167 = (bf16[2880,512]{1,0:T(8,128)(2,1)S(1)}, bf16[2880,128]{1,0:T(8,128)(2,1)S(1)}) custom-call(bf16[2880,512]{1,0:T(8,128)(2,1)} %refs_0_.2, bf16[2880,128]{1,0:T(8,128)(2,1)} %refs_1_.2), custom_call_target="tpu_custom_call" | custom-call | bytes 7372800 | tf_op jit(solution)/shard_map/pallas_call | solution.py:271
  9.0 2.2 %collective-permute-done.2.refs_3_.refs_7_ = bf16[24,2880]{1,0:T(8,128)(2,1)S(1)} collective-permute-done((bf16[24,2880]{1,0:T(8,128)(2,1)}, bf16[24,2880]{1,0:T(8,128)(2,1)S(1)}, u32[]{:S(2)}, u32[]{:S(2)}) %collective-permute-start.2) | collective-permute-done | bytes 138272 | tf_op jit(solution)/shard_map/ppermute | solution.py:549
  11.1 7.6 %collective-permute-done.1.refs_2_.refs_5_ = bf16[24,2880]{1,0:T(8,128)(2,1)S(1)} collective-permute-done((bf16[24,2880]{1,0:T(8,128)(2,1)}, bf16[24,2880]{1,0:T(8,128)(2,1)S(1)}, u32[]{:S(2)}, u32[]{:S(2)}) %collective-permute-start.1) | collective-permute-done | bytes 138272 | tf_op jit(solution)/shard_map/ppermute | solution.py:549
  18.7 1.6 %shard_map.168 = (bf16[24,1280]{1,0:T(8,128)(2,1)S(1)}, bf16[24,1280]{1,0:T(8,128)(2,1)S(1)}, bf16[24,1280]{1,0:T(8,128)(2,1)S(1)}, bf16[24,1280]{1,0:T(8,128)(2,1)S(1)}) custom-call(bf16[24,2880]{1,0:T(8,128)(2,1)S(1)} %copy-done, bf16[24,2880]{1,0:T(8,128)(2,1)S(1)} %collective-permute-done.refs_1_.refs_3_, ...), custom_call_target="tpu_custom_call" | custom-call | flops 707788800 | bytes 3686400 | tf_op jit(solution)/shard_map/pallas_call | solution.py:238
  20.5 3.0 %collective-permute-start.7 = (bf16[24,1280]{1,0:T(8,128)(2,1)S(1)}, bf16[24,1280]{1,0:T(8,128)(2,1)S(1)}, u32[]{:S(2)}, u32[]{:S(2)}) collective-permute-start(bf16[24,1280]{1,0:T(8,128)(2,1)S(1)} %get-tuple-element.102), channel_id=1, source_target_pairs={{0,4},{1,5},{2,6},{3,7},{4,0},{5,1},{6,2},{7,3},{8,12},{9,13},{10,... | collective-permute-start | bytes 184328 | tf_op jit(solution)/shard_map/ppermute | solution.py:549
  23.5 1.3 %collective-permute-start.8 = (bf16[24,1280]{1,0:T(8,128)(2,1)S(1)}, bf16[24,1280]{1,0:T(8,128)(2,1)S(1)}, u32[]{:S(2)}, u32[]{:S(2)}) collective-permute-start(bf16[24,1280]{1,0:T(8,128)(2,1)S(1)} %get-tuple-element.103), channel_id=1, source_target_pairs={{0,6},{1,7},{2,4},{3,5},{4,2},{5,3},{6,0},{7,1},{8,14},{9,15},{10,... | collective-permute-start | bytes 184328 | tf_op jit(solution)/shard_map/ppermute | solution.py:549
  26.2 0.7 shard_map.169
  26.9 2.2 %shard_map.170 = (bf16[2048,512]{1,0:T(8,128)(2,1)S(1)}, bf16[2048,512]{1,0:T(8,128)(2,1)S(1)}) custom-call(bf16[2048,512]{1,0:T(8,128)(2,1)} %bitcast.13, bf16[2048,512]{1,0:T(8,128)(2,1)} %bitcast.14), custom_call_target="tpu_custom_call" | custom-call | bytes 8388608 | tf_op jit(solution)/shard_map/pallas_call | solution.py:271
  29.6 6.8 %shard_map.171 = (bf16[24,1024]{1,0:T(8,128)(2,1)S(1)}, bf16[24,1024]{1,0:T(8,128)(2,1)S(1)}, bf16[24,1024]{1,0:T(8,128)(2,1)S(1)}, bf16[24,1024]{1,0:T(8,128)(2,1)S(1)}, bf16[8,1024]{1,0:T(8,128)(2,1)}) custom-call(s32[1]{0:T(128)} %bitcast.refs_0_.me_ref, s32[1]{0:T(128)S(6)} %copy.18.lens.refs_1_, bf16[24,1280]{1,0:T(8,128)(2,1)S(1)} %get-tuple-element.114.refs_2_, ...), custom_call_target="tpu_custom_call" | custom-call | flops 805306368 | bytes 4194304 | tf_op jit(solution)/shard_map/pallas_call | solution.py:238
  36.4 0.8 collective-permute-start.9
  37.2 1.8 %collective-permute-start.10 = (bf16[24,1024]{1,0:T(8,128)(2,1)S(1)}, bf16[24,1024]{1,0:T(8,128)(2,1)S(1)}, u32[]{:S(2)}, u32[]{:S(2)}) collective-permute-start(bf16[24,1024]{1,0:T(8,128)(2,1)S(1)} %get-tuple-element.131), channel_id=1, source_target_pairs={{0,4},{1,5},{2,6},{3,7},{4,0},{5,1},{6,2},{7,3},{8,12},{9,13},{10,... | collective-permute-start | bytes 147464 | tf_op jit(solution)/shard_map/ppermute | solution.py:549
  39.1 1.8 %collective-permute-start.11 = (bf16[24,1024]{1,0:T(8,128)(2,1)S(1)}, bf16[24,1024]{1,0:T(8,128)(2,1)S(1)}, u32[]{:S(2)}, u32[]{:S(2)}) collective-permute-start(bf16[24,1024]{1,0:T(8,128)(2,1)S(1)} %get-tuple-element.132), channel_id=1, source_target_pairs={{0,6},{1,7},{2,4},{3,5},{4,2},{5,3},{6,0},{7,1},{8,14},{9,15},{10,... | collective-permute-start | bytes 147464 | tf_op jit(solution)/shard_map/ppermute | solution.py:549
  40.8 2.8 %shard_map.172 = (bf16[2880,512]{1,0:T(8,128)(2,1)S(1)}, bf16[2880,512]{1,0:T(8,128)(2,1)S(1)}) custom-call(bf16[2880,512]{1,0:T(8,128)(2,1)} %bitcast.3.refs_0_, bf16[2880,512]{1,0:T(8,128)(2,1)} %bitcast.4.refs_1_), custom_call_target="tpu_custom_call" | custom-call | bytes 11796480 | tf_op jit(solution)/shard_map/pallas_call | solution.py:271
  43.6 1.3 %collective-permute-done.11.refs_7_.refs_4_ = bf16[24,1024]{1,0:T(8,128)(2,1)S(1)} collective-permute-done((bf16[24,1024]{1,0:T(8,128)(2,1)S(1)}, bf16[24,1024]{1,0:T(8,128)(2,1)S(1)}, u32[]{:S(2)}, u32[]{:S(2)}) %collective-permute-start.11) | collective-permute-done | bytes 49184 | tf_op jit(solution)/shard_map/ppermute | solution.py:549
  47.4 2.2 %shard_map.173 = (f32[24,2880]{1,0:T(8,128)S(1)}, bf16[24,2880]{1,0:T(8,128)(2,1)S(1)}, bf16[24,2880]{1,0:T(8,128)(2,1)S(1)}, bf16[24,2880]{1,0:T(8,128)(2,1)S(1)}) custom-call(s32[1]{0:T(128)} %bitcast.refs_0_.me_ref, bf16[24,1024]{1,0:T(8,128)(2,1)S(1)} %get-tuple-element.137.refs_1_, bf16[24,1024]{1,0:T(8,128)(2,1)S(1)} %collective-permute-done.12.refs_2_, ...), custom_call_target="tpu_custom_call" | custom-call | flops 566231040 | bytes 5898240 | tf_op jit(solution)/shard_map/pallas_call | solution.py:238
  49.8 1.8 %collective-permute-start.18 = (bf16[24,2880]{1,0:T(8,128)(2,1)S(1)}, bf16[24,2880]{1,0:T(8,128)(2,1)S(1)}, u32[]{:S(2)}, u32[]{:S(2)}) collective-permute-start(bf16[24,2880]{1,0:T(8,128)(2,1)S(1)} %get-tuple-element.146), channel_id=1, source_target_pairs={{0,6},{1,7},{2,4},{3,5},{4,2},{5,3},{6,0},{7,1},{8,14},{9,15},{10,... | collective-permute-start | bytes 414728 | tf_op jit(solution)/shard_map/ppermute | solution.py:549
  51.6 1.6 %collective-permute-start.16 = (bf16[24,2880]{1,0:T(8,128)(2,1)S(1)}, bf16[24,2880]{1,0:T(8,128)(2,1)S(1)}, u32[]{:S(2)}, u32[]{:S(2)}) collective-permute-start(bf16[24,2880]{1,0:T(8,128)(2,1)S(1)} %get-tuple-element.144), channel_id=1, source_target_pairs={{0,2},{1,3},{2,0},{3,1},{4,6},{5,7},{6,4},{7,5},{8,10},{9,11},{10,... | collective-permute-start | bytes 414728 | tf_op jit(solution)/shard_map/ppermute | solution.py:549
  53.1 8.3 %shard_map.176 = (bf16[1440,2880]{1,0:T(8,128)(2,1)S(1)}, bf16[1440,2880]{1,0:T(8,128)(2,1)S(1)}, bf16[1440,2880]{1,0:T(8,128)(2,1)S(1)}) custom-call(bf16[1440,2880]{1,0:T(8,128)(2,1)} %refs_0_.4, bf16[1440,2880]{1,0:T(8,128)(2,1)} %refs_1_.4, bf16[1440,2880]{1,0:T(8,128)(2,1)} %refs_2_), custom_call_target="tpu_custom_call" | custom-call | bytes 49766400 | tf_op jit(solution)/shard_map/pallas_call | solution.py:271
  61.9 1.9 %shard_map.174.refs_4_ = f32[96,2880]{1,0:T(8,128)S(1)} custom-call(s32[1]{0:T(128)} %bitcast.refs_0_.me_ref, bf16[24,1024]{1,0:T(8,128)(2,1)S(1)} %get-tuple-element.137.refs_1_, bf16[24,1024]{1,0:T(8,128)(2,1)S(1)} %collective-permute-done.9.refs_3_.refs_2_, bf16[24,1024]{1,0:T(8,128)(2,1)S(1)} %collective-permute-done.10.refs_5_.refs_3_, ...), custom_call_target="tpu_custom_call" | custom-call | flops 566231040 | bytes 5898240 | tf_op jit(solution)/shard_map/pallas_call | solution.py:238
  64.2 1.3 %collective-permute-done.23.theirs = bf16[24,2880]{1,0:T(8,128)(2,1)S(1)} collective-permute-done((bf16[24,2880]{1,0:T(8,128)(2,1)S(1)}, bf16[24,2880]{1,0:T(8,128)(2,1)S(1)}, u32[]{:S(2)}, u32[]{:S(2)}) %collective-permute-start.23) | collective-permute-done | bytes 138272 | tf_op jit(solution)/shard_map/ppermute | solution.py:549
  65.6 6.1 %shard_map.177.refs_1_ = bf16[48,2880]{1,0:T(8,128)(2,1)S(1)} custom-call(s32[1]{0:T(128)} %bitcast.refs_0_.me_ref, bf16[24,2880]{1,0:T(8,128)(2,1)S(1)} %add_convert_fusion.1.mine, bf16[24,2880]{1,0:T(8,128)(2,1)S(1)} %collective-permute-done.23.theirs, f32[1,2880]{1,0:T(1,128)S(1)} %reshape.15.gain, bf16[32,2880]{1,0:T(8,128)(2,1)S(1)} %bitcast.8, ...), custom_call_target="tpu_custom_call" | custom-call | flops 1194393600 | bytes 24883200 | tf_op jit(solution)/shard_map/pallas_call | solution.py:238
  71.9 1.4 %collective-permute-done.24.refs_2_ = bf16[48,2880]{1,0:T(8,128)(2,1)S(1)} collective-permute-done((bf16[48,2880]{1,0:T(8,128)(2,1)S(1)}, bf16[48,2880]{1,0:T(8,128)(2,1)S(1)}, u32[]{:S(2)}, u32[]{:S(2)}) %collective-permute-start.24) | collective-permute-done | bytes 276512 | tf_op jit(solution)/shard_map/ppermute | solution.py:549
  73.3 0.8 shard_map.178
  74.1 1.3 %collective-permute-start.25 = (bf16[24,2880]{1,0:T(8,128)(2,1)S(1)}, bf16[24,2880]{1,0:T(8,128)(2,1)S(1)}, u32[]{:S(2)}, u32[]{:S(2)}) collective-permute-start(bf16[24,2880]{1,0:T(8,128)(2,1)S(1)} %get-tuple-element.169), channel_id=1, source_target_pairs={{0,2},{1,3},{2,0},{3,1},{4,6},{5,7},{6,4},{7,5},{8,10},{9,11},{10,... | collective-permute-start | bytes 414728 | tf_op jit(solution)/shard_map/ppermute | solution.py:549
  75.4 1.1 %collective-permute-start.26 = (bf16[24,2880]{1,0:T(8,128)(2,1)S(1)}, bf16[24,2880]{1,0:T(8,128)(2,1)S(1)}, u32[]{:S(2)}, u32[]{:S(2)}) collective-permute-start(bf16[24,2880]{1,0:T(8,128)(2,1)S(1)} %get-tuple-element.170), channel_id=1, source_target_pairs={{0,4},{1,5},{2,6},{3,7},{4,0},{5,1},{6,2},{7,3},{8,12},{9,13},{10,... | collective-permute-start | bytes 414728 | tf_op jit(solution)/shard_map/ppermute | solution.py:549
  76.5 2.1 %collective-permute-start.27 = (bf16[24,2880]{1,0:T(8,128)(2,1)S(1)}, bf16[24,2880]{1,0:T(8,128)(2,1)S(1)}, u32[]{:S(2)}, u32[]{:S(2)}) collective-permute-start(bf16[24,2880]{1,0:T(8,128)(2,1)S(1)} %get-tuple-element.171), channel_id=1, source_target_pairs={{0,6},{1,7},{2,4},{3,5},{4,2},{5,3},{6,0},{7,1},{8,14},{9,15},{10,... | collective-permute-start | bytes 414728 | tf_op jit(solution)/shard_map/ppermute | solution.py:549
  78.6 3.6 %collective-permute-done.25 = bf16[24,2880]{1,0:T(8,128)(2,1)S(1)} collective-permute-done((bf16[24,2880]{1,0:T(8,128)(2,1)S(1)}, bf16[24,2880]{1,0:T(8,128)(2,1)S(1)}, u32[]{:S(2)}, u32[]{:S(2)}) %collective-permute-start.25) | collective-permute-done | bytes 138272 | tf_op jit(solution)/shard_map/ppermute | solution.py:549
  82.2 6.8 %collective-permute-done.26 = bf16[24,2880]{1,0:T(8,128)(2,1)S(1)} collective-permute-done((bf16[24,2880]{1,0:T(8,128)(2,1)S(1)}, bf16[24,2880]{1,0:T(8,128)(2,1)S(1)}, u32[]{:S(2)}, u32[]{:S(2)}) %collective-permute-start.26) | collective-permute-done | bytes 138272 | tf_op jit(solution)/shard_map/ppermute | solution.py:549
  89.0 0.7 add_convert_fusion
  (53 shorter events, 4.3 us)
Async XLA Ops:
  0.6 18.1 %copy-start = (bf16[24,2880]{1,0:T(8,128)(2,1)S(1)}, bf16[24,2880]{1,0:T(8,128)(2,1)}, u32[]{:S(2)}) copy-start(bf16[24,2880]{1,0:T(8,128)(2,1)} %refs_5_.1) | copy-start | bytes 414724
  0.6 8.3 %copy-start.3 = (f32[2880]{0:T(1024)S(1)}, f32[2880]{0:T(1024)}, u32[]{:S(2)}) copy-start(f32[2880]{0:T(1024)} %param.17) | copy-start | bytes 34564
  0.7 8.3 %copy-start.4 = (f32[2880]{0:T(1024)S(1)}, f32[2880]{0:T(1024)}, u32[]{:S(2)}) copy-start(f32[2880]{0:T(1024)} %param.26) | copy-start | bytes 34564
  0.7 8.3 %copy-start.5 = (s32[1,24]{1,0:T(1,128)S(1)}, s32[1,24]{1,0:T(1,128)}, u32[]{:S(2)}) copy-start(s32[1,24]{1,0:T(1,128)} %param.24) | copy-start | bytes 292
  0.7 18.0 %collective-permute-start.3 = (bf16[2880,512]{1,0:T(8,128)(2,1)}, bf16[2880,512]{1,0:T(8,128)(2,1)S(1)}, u32[]{:S(2)}, u32[]{:S(2)}) collective-permute-start(bf16[2880,512]{1,0:T(8,128)(2,1)} %refs_0_.2), channel_id=1, source_target_pairs={{0,1},{1,0},{2,3},{3,2},{4,5},{5,4},{6,7},{7,6},{8,9},{9,8},{10,11... | collective-permute-start | bytes 8847368 | tf_op jit(solution)/shard_map/ppermute | solution.py:549
  1.2 17.5 %collective-permute-start.4 = (bf16[2880,128]{1,0:T(8,128)(2,1)}, bf16[2880,128]{1,0:T(8,128)(2,1)S(1)}, u32[]{:S(2)}, u32[]{:S(2)}) collective-permute-start(bf16[2880,128]{1,0:T(8,128)(2,1)} %refs_1_.2), channel_id=1, source_target_pairs={{0,1},{1,0},{2,3},{3,2},{4,5},{5,4},{6,7},{7,6},{8,9},{9,8},{10,11... | collective-permute-start | bytes 2211848 | tf_op jit(solution)/shard_map/ppermute | solution.py:549
  1.3 9.9 %collective-permute-start.2 = (bf16[24,2880]{1,0:T(8,128)(2,1)}, bf16[24,2880]{1,0:T(8,128)(2,1)S(1)}, u32[]{:S(2)}, u32[]{:S(2)}) collective-permute-start(bf16[24,2880]{1,0:T(8,128)(2,1)} %refs_5_.1), channel_id=1, source_target_pairs={{0,6},{1,7},{2,4},{3,5},{4,2},{5,3},{6,0},{7,1},{8,14},{9,15},{10,... | collective-permute-start | bytes 414728 | tf_op jit(solution)/shard_map/ppermute | solution.py:549
  6.3 12.4 %collective-permute-start.1 = (bf16[24,2880]{1,0:T(8,128)(2,1)}, bf16[24,2880]{1,0:T(8,128)(2,1)S(1)}, u32[]{:S(2)}, u32[]{:S(2)}) collective-permute-start(bf16[24,2880]{1,0:T(8,128)(2,1)} %refs_5_.1), channel_id=1, source_target_pairs={{0,4},{1,5},{2,6},{3,7},{4,0},{5,1},{6,2},{7,3},{8,12},{9,13},{10,... | collective-permute-start | bytes 414728 | tf_op jit(solution)/shard_map/ppermute | solution.py:549
  6.3 12.4 %collective-permute-start = (bf16[24,2880]{1,0:T(8,128)(2,1)}, bf16[24,2880]{1,0:T(8,128)(2,1)S(1)}, u32[]{:S(2)}, u32[]{:S(2)}) collective-permute-start(bf16[24,2880]{1,0:T(8,128)(2,1)} %refs_5_.1), channel_id=1, source_target_pairs={{0,2},{1,3},{2,0},{3,1},{4,6},{5,7},{6,4},{7,5},{8,10},{9,11},{10,... | collective-permute-start | bytes 414728 | tf_op jit(solution)/shard_map/ppermute | solution.py:549
  20.3 16.1 %collective-permute-start.5 = (bf16[512,2880]{0,1:T(8,128)(2,1)}, bf16[512,2880]{0,1:T(8,128)(2,1)}, u32[]{:S(2)}, u32[]{:S(2)}) collective-permute-start(bf16[512,2880]{0,1:T(8,128)(2,1)} %param.20), channel_id=1, source_target_pairs={{0,1},{1,0},{2,3},{3,2},{4,5},{5,4},{6,7},{7,6},{8,9},{9,8},{10,11... | collective-permute-start | bytes 8847368 | tf_op jit(solution)/shard_map/ppermute | solution.py:549
  20.4 8.7 %collective-permute-start.6 = (bf16[24,1280]{1,0:T(8,128)(2,1)S(1)}, bf16[24,1280]{1,0:T(8,128)(2,1)S(1)}, u32[]{:S(2)}, u32[]{:S(2)}) collective-permute-start(bf16[24,1280]{1,0:T(8,128)(2,1)S(1)} %get-tuple-element.101), channel_id=1, source_target_pairs={{0,2},{1,3},{2,0},{3,1},{4,6},{5,7},{6,4},{7,5},{8,10},{9,11},{10,... | collective-permute-start | bytes 184328 | tf_op jit(solution)/shard_map/ppermute | solution.py:549
  20.5 8.7 %collective-permute-start.7 = (bf16[24,1280]{1,0:T(8,128)(2,1)S(1)}, bf16[24,1280]{1,0:T(8,128)(2,1)S(1)}, u32[]{:S(2)}, u32[]{:S(2)}) collective-permute-start(bf16[24,1280]{1,0:T(8,128)(2,1)S(1)} %get-tuple-element.102), channel_id=1, source_target_pairs={{0,4},{1,5},{2,6},{3,7},{4,0},{5,1},{6,2},{7,3},{8,12},{9,13},{10,... | collective-permute-start | bytes 184328 | tf_op jit(solution)/shard_map/ppermute | solution.py:549
  23.5 6.1 %collective-permute-start.8 = (bf16[24,1280]{1,0:T(8,128)(2,1)S(1)}, bf16[24,1280]{1,0:T(8,128)(2,1)S(1)}, u32[]{:S(2)}, u32[]{:S(2)}) collective-permute-start(bf16[24,1280]{1,0:T(8,128)(2,1)S(1)} %get-tuple-element.103), channel_id=1, source_target_pairs={{0,6},{1,7},{2,4},{3,5},{4,2},{5,3},{6,0},{7,1},{8,14},{9,15},{10,... | collective-permute-start | bytes 184328 | tf_op jit(solution)/shard_map/ppermute | solution.py:549
  36.4 7.2 %collective-permute-start.9 = (bf16[24,1024]{1,0:T(8,128)(2,1)S(1)}, bf16[24,1024]{1,0:T(8,128)(2,1)S(1)}, u32[]{:S(2)}, u32[]{:S(2)}) collective-permute-start(bf16[24,1024]{1,0:T(8,128)(2,1)S(1)} %get-tuple-element.130), channel_id=1, source_target_pairs={{0,2},{1,3},{2,0},{3,1},{4,6},{5,7},{6,4},{7,5},{8,10},{9,11},{10,... | collective-permute-start | bytes 147464 | tf_op jit(solution)/shard_map/ppermute | solution.py:549
  37.2 6.4 %collective-permute-start.10 = (bf16[24,1024]{1,0:T(8,128)(2,1)S(1)}, bf16[24,1024]{1,0:T(8,128)(2,1)S(1)}, u32[]{:S(2)}, u32[]{:S(2)}) collective-permute-start(bf16[24,1024]{1,0:T(8,128)(2,1)S(1)} %get-tuple-element.131), channel_id=1, source_target_pairs={{0,4},{1,5},{2,6},{3,7},{4,0},{5,1},{6,2},{7,3},{8,12},{9,13},{10,... | collective-permute-start | bytes 147464 | tf_op jit(solution)/shard_map/ppermute | solution.py:549
  39.1 5.9 %collective-permute-start.11 = (bf16[24,1024]{1,0:T(8,128)(2,1)S(1)}, bf16[24,1024]{1,0:T(8,128)(2,1)S(1)}, u32[]{:S(2)}, u32[]{:S(2)}) collective-permute-start(bf16[24,1024]{1,0:T(8,128)(2,1)S(1)} %get-tuple-element.132), channel_id=1, source_target_pairs={{0,6},{1,7},{2,4},{3,5},{4,2},{5,3},{6,0},{7,1},{8,14},{9,15},{10,... | collective-permute-start | bytes 147464 | tf_op jit(solution)/shard_map/ppermute | solution.py:549
  44.9 1.2 %collective-permute-start.12 = (bf16[24,1024]{1,0:T(8,128)(2,1)S(1)}, bf16[24,1024]{1,0:T(8,128)(2,1)S(1)}, u32[]{:S(2)}, u32[]{:S(2)}) collective-permute-start(bf16[24,1024]{1,0:T(8,128)(2,1)S(1)} %get-tuple-element.137.refs_1_), channel_id=1, source_target_pairs={{0,1},{1,0},{2,3},{3,2},{4,5},{5,4},{6,7},{7,6},{8,9},{9,8},{10,11... | collective-permute-start | bytes 147464 | tf_op jit(solution)/shard_map/ppermute | solution.py:549
  44.9 4.9 %collective-permute-start.19 = (bf16[24,2880]{1,0:T(8,128)(2,1)S(1)}, bf16[24,2880]{1,0:T(8,128)(2,1)S(1)}, u32[]{:S(2)}, u32[]{:S(2)}) collective-permute-start(bf16[24,2880]{1,0:T(8,128)(2,1)S(1)} %copy-done), channel_id=1, source_target_pairs={{0,1},{1,0},{2,3},{3,2},{4,5},{5,4},{6,7},{7,6},{8,9},{9,8},{10,11... | collective-permute-start | bytes 414728 | tf_op jit(solution)/shard_map/ppermute | solution.py:549
  45.5 6.1 %collective-permute-start.20 = (bf16[24,2880]{1,0:T(8,128)(2,1)S(1)}, bf16[24,2880]{1,0:T(8,128)(2,1)S(1)}, u32[]{:S(2)}, u32[]{:S(2)}) collective-permute-start(bf16[24,2880]{1,0:T(8,128)(2,1)S(1)} %collective-permute-done.refs_1_.refs_3_), channel_id=1, source_target_pairs={{0,1},{1,0},{2,3},{3,2},{4,5},{5,4},{6,7},{7,6},{8,9},{9,8},{10,11... | collective-permute-start | bytes 414728 | tf_op jit(solution)/shard_map/ppermute | solution.py:549
  45.5 1.4 %collective-permute-start.13 = (bf16[24,1024]{1,0:T(8,128)(2,1)S(1)}, bf16[24,1024]{1,0:T(8,128)(2,1)S(1)}, u32[]{:S(2)}, u32[]{:S(2)}) collective-permute-start(bf16[24,1024]{1,0:T(8,128)(2,1)S(1)} %collective-permute-done.9.refs_3_.refs_2_), channel_id=1, source_target_pairs={{0,1},{1,0},{2,3},{3,2},{4,5},{5,4},{6,7},{7,6},{8,9},{9,8},{10,11... | collective-permute-start | bytes 147464 | tf_op jit(solution)/shard_map/ppermute | solution.py:549
  46.0 1.2 %collective-permute-start.14 = (bf16[24,1024]{1,0:T(8,128)(2,1)S(1)}, bf16[24,1024]{1,0:T(8,128)(2,1)S(1)}, u32[]{:S(2)}, u32[]{:S(2)}) collective-permute-start(bf16[24,1024]{1,0:T(8,128)(2,1)S(1)} %collective-permute-done.10.refs_5_.refs_3_), channel_id=1, source_target_pairs={{0,1},{1,0},{2,3},{3,2},{4,5},{5,4},{6,7},{7,6},{8,9},{9,8},{10,11... | collective-permute-start | bytes 147464 | tf_op jit(solution)/shard_map/ppermute | solution.py:549
  46.2 1.2 %collective-permute-start.15 = (bf16[24,1024]{1,0:T(8,128)(2,1)S(1)}, bf16[24,1024]{1,0:T(8,128)(2,1)S(1)}, u32[]{:S(2)}, u32[]{:S(2)}) collective-permute-start(bf16[24,1024]{1,0:T(8,128)(2,1)S(1)} %collective-permute-done.11.refs_7_.refs_4_), channel_id=1, source_target_pairs={{0,1},{1,0},{2,3},{3,2},{4,5},{5,4},{6,7},{7,6},{8,9},{9,8},{10,11... | collective-permute-start | bytes 147464 | tf_op jit(solution)/shard_map/ppermute | solution.py:549
  46.9 14.5 %collective-permute-start.21 = (bf16[24,2880]{1,0:T(8,128)(2,1)S(1)}, bf16[24,2880]{1,0:T(8,128)(2,1)S(1)}, u32[]{:S(2)}, u32[]{:S(2)}) collective-permute-start(bf16[24,2880]{1,0:T(8,128)(2,1)S(1)} %collective-permute-done.1.refs_2_.refs_5_), channel_id=1, source_target_pairs={{0,1},{1,0},{2,3},{3,2},{4,5},{5,4},{6,7},{7,6},{8,9},{9,8},{10,11... | collective-permute-start | bytes 414728 | tf_op jit(solution)/shard_map/ppermute | solution.py:549
  47.2 14.2 %collective-permute-start.22 = (bf16[24,2880]{1,0:T(8,128)(2,1)S(1)}, bf16[24,2880]{1,0:T(8,128)(2,1)S(1)}, u32[]{:S(2)}, u32[]{:S(2)}) collective-permute-start(bf16[24,2880]{1,0:T(8,128)(2,1)S(1)} %collective-permute-done.2.refs_3_.refs_7_), channel_id=1, source_target_pairs={{0,1},{1,0},{2,3},{3,2},{4,5},{5,4},{6,7},{7,6},{8,9},{9,8},{10,11... | collective-permute-start | bytes 414728 | tf_op jit(solution)/shard_map/ppermute | solution.py:549
  49.6 14.3 %collective-permute-start.17 = (bf16[24,2880]{1,0:T(8,128)(2,1)S(1)}, bf16[24,2880]{1,0:T(8,128)(2,1)S(1)}, u32[]{:S(2)}, u32[]{:S(2)}) collective-permute-start(bf16[24,2880]{1,0:T(8,128)(2,1)S(1)} %get-tuple-element.145), channel_id=1, source_target_pairs={{0,4},{1,5},{2,6},{3,7},{4,0},{5,1},{6,2},{7,3},{8,12},{9,13},{10,... | collective-permute-start | bytes 414728 | tf_op jit(solution)/shard_map/ppermute | solution.py:549
  49.8 14.2 %collective-permute-start.18 = (bf16[24,2880]{1,0:T(8,128)(2,1)S(1)}, bf16[24,2880]{1,0:T(8,128)(2,1)S(1)}, u32[]{:S(2)}, u32[]{:S(2)}) collective-permute-start(bf16[24,2880]{1,0:T(8,128)(2,1)S(1)} %get-tuple-element.146), channel_id=1, source_target_pairs={{0,6},{1,7},{2,4},{3,5},{4,2},{5,3},{6,0},{7,1},{8,14},{9,15},{10,... | collective-permute-start | bytes 414728 | tf_op jit(solution)/shard_map/ppermute | solution.py:549
  51.6 12.5 %collective-permute-start.16 = (bf16[24,2880]{1,0:T(8,128)(2,1)S(1)}, bf16[24,2880]{1,0:T(8,128)(2,1)S(1)}, u32[]{:S(2)}, u32[]{:S(2)}) collective-permute-start(bf16[24,2880]{1,0:T(8,128)(2,1)S(1)} %get-tuple-element.144), channel_id=1, source_target_pairs={{0,2},{1,3},{2,0},{3,1},{4,6},{5,7},{6,4},{7,5},{8,10},{9,11},{10,... | collective-permute-start | bytes 414728 | tf_op jit(solution)/shard_map/ppermute | solution.py:549
  64.1 1.4 %collective-permute-start.23 = (bf16[24,2880]{1,0:T(8,128)(2,1)S(1)}, bf16[24,2880]{1,0:T(8,128)(2,1)S(1)}, u32[]{:S(2)}, u32[]{:S(2)}) collective-permute-start(bf16[24,2880]{1,0:T(8,128)(2,1)S(1)} %add_convert_fusion.1.mine), channel_id=1, source_target_pairs={{0,1},{1,0},{2,3},{3,2},{4,5},{5,4},{6,7},{7,6},{8,9},{9,8},{10,11... | collective-permute-start | bytes 414728 | tf_op jit(solution)/shard_map/ppermute | solution.py:549
  71.7 1.6 %collective-permute-start.24 = (bf16[48,2880]{1,0:T(8,128)(2,1)S(1)}, bf16[48,2880]{1,0:T(8,128)(2,1)S(1)}, u32[]{:S(2)}, u32[]{:S(2)}) collective-permute-start(bf16[48,2880]{1,0:T(8,128)(2,1)S(1)} %shard_map.177.refs_1_), channel_id=1, source_target_pairs={{0,1},{1,0},{2,3},{3,2},{4,5},{5,4},{6,7},{7,6},{8,9},{9,8},{10,11... | collective-permute-start | bytes 829448 | tf_op jit(solution)/shard_map/ppermute | solution.py:549
  74.1 8.1 %collective-permute-start.25 = (bf16[24,2880]{1,0:T(8,128)(2,1)S(1)}, bf16[24,2880]{1,0:T(8,128)(2,1)S(1)}, u32[]{:S(2)}, u32[]{:S(2)}) collective-permute-start(bf16[24,2880]{1,0:T(8,128)(2,1)S(1)} %get-tuple-element.169), channel_id=1, source_target_pairs={{0,2},{1,3},{2,0},{3,1},{4,6},{5,7},{6,4},{7,5},{8,10},{9,11},{10,... | collective-permute-start | bytes 414728 | tf_op jit(solution)/shard_map/ppermute | solution.py:549
  75.4 13.6 %collective-permute-start.26 = (bf16[24,2880]{1,0:T(8,128)(2,1)S(1)}, bf16[24,2880]{1,0:T(8,128)(2,1)S(1)}, u32[]{:S(2)}, u32[]{:S(2)}) collective-permute-start(bf16[24,2880]{1,0:T(8,128)(2,1)S(1)} %get-tuple-element.170), channel_id=1, source_target_pairs={{0,4},{1,5},{2,6},{3,7},{4,0},{5,1},{6,2},{7,3},{8,12},{9,13},{10,... | collective-permute-start | bytes 414728 | tf_op jit(solution)/shard_map/ppermute | solution.py:549
  76.5 12.5 %collective-permute-start.27 = (bf16[24,2880]{1,0:T(8,128)(2,1)S(1)}, bf16[24,2880]{1,0:T(8,128)(2,1)S(1)}, u32[]{:S(2)}, u32[]{:S(2)}) collective-permute-start(bf16[24,2880]{1,0:T(8,128)(2,1)S(1)} %get-tuple-element.171), channel_id=1, source_target_pairs={{0,6},{1,7},{2,4},{3,5},{4,2},{5,3},{6,0},{7,1},{8,14},{9,15},{10,... | collective-permute-start | bytes 414728 | tf_op jit(solution)/shard_map/ppermute | solution.py:549
  (2 other events, 10.2 us)

commit v4 on v3

--- a/solution.py
+++ b/solution.py
@@ -1,3 +1,4 @@
+import functools
 import math
 
 import jax
@@ -230,6 +231,7 @@
 NEGATIVE = -1e30
 MIB = 1024 * 1024
 VMEM_LIMIT = 24 * MIB
+SCORE_STEP = 1024
 VM = pl.BlockSpec(memory_space=pltpu.VMEM)
 SM = pl.BlockSpec(memory_space=pltpu.SMEM)
 
@@ -331,10 +333,11 @@
     pieces, (gain, *weights), rest = refs[:4], refs[4:9], refs[9:]
     outs, normed = rest[:4], rest[4]
     count = pieces[0].shape[0]
+    scale = gain[...].reshape(1, gain.shape[0])
     for k, piece in enumerate(pieces):
         floats = piece[...].astype(jnp.float32)
         mean_sq = jnp.mean(floats * floats, axis=-1, keepdims=True)
-        normed[k * count : (k + 1) * count, :] = floats * lax.rsqrt(mean_sq + EPSILON) * gain[...]
+        normed[k * count : (k + 1) * count, :] = floats * lax.rsqrt(mean_sq + EPSILON) * scale
     rows = normed[...].astype(jnp.bfloat16)
     at = 0
     for weight in weights:
@@ -350,7 +353,7 @@
     arrived = refs[2:6]
     cos, sin, bias, pick, keys, values = refs[6:12]
     outs, accepted_out = refs[12:16], refs[16]
-    blocks, queries, new_keys, new_values, attended = refs[17:]
+    blocks, queries, new_keys, new_values, attended, held = refs[17:]
     draft = cos.shape[0]
     lanes = 2 * HEAD_DIM
     for i in range(4):
@@ -362,6 +365,7 @@
     left = lane < HEAD_DIM
     cosine, sine, mask = cos[...], sin[...], bias[...]
     slots = keys.shape[0]
+    step = SCORE_STEP
     live = jnp.where(iota((1, slots), 1) < lens, 0.0, NEGATIVE)
 
     def rope(tile):
@@ -373,38 +377,62 @@
     new_values[...] = jnp.zeros_like(new_values)
     q_cols = blocks.shape[2] - lanes
     heads = q_cols // HEAD_DIM
-    for pair in range(4):
-        new_keys[:draft, :] = rope(blocks[pair, :, q_cols:])
-        new_values[:draft, :] = blocks[4 + pair, :, q_cols:]
-        fresh_k = new_keys[...].astype(jnp.bfloat16)
-        fresh_v = new_values[...].astype(jnp.bfloat16)
-        picked = pick[...].astype(jnp.bfloat16)
-        span = slice(pair * lanes, (pair + 1) * lanes)
-        accepted_out[:, span] = dot_nn(picked, fresh_k).astype(jnp.bfloat16)
-        accepted_out[:, slice(4 * lanes + pair * lanes, 4 * lanes + (pair + 1) * lanes)] = dot_nn(
-            picked, fresh_v
-        ).astype(jnp.bfloat16)
+    count = heads * draft
+    groups = queries.shape[0] // count
+    pairs, both = groups // 2, 2 * count
+
+    def fill(pair):
+        new_keys[pair, :draft, :] = rope(blocks[pair, :, q_cols:])
+        new_values[pair, :draft, :] = blocks[groups // 2 + pair, :, q_cols:]
         for p in range(2):
             for t in range(heads // 2):
                 tile = rope(blocks[2 * pair + p, :, t * lanes : (t + 1) * lanes]) * 0.125
                 turned = pltpu.roll(tile, HEAD_DIM, 1)
                 first, second = (tile, turned) if p == 0 else (turned, tile)
                 keep = left if p == 0 else ~left
-                at = (p * heads + 2 * t) * draft
+                at = (2 * pair + p) * count + 2 * t * draft
                 queries[at : at + draft, :] = jnp.where(keep, first, 0.0)
                 queries[at + draft : at + 2 * draft, :] = jnp.where(keep, second, 0.0)
-        group = queries[...].astype(jnp.bfloat16)
-        scores = dot_nt(group, keys[:, span]) + live
-        fresh = dot_nt(group, fresh_k)
-        fresh = (fresh.reshape(2 * heads, draft, lanes) + mask[None]).reshape(fresh.shape)
-        top = jnp.maximum(
-            jnp.max(scores, axis=1, keepdims=True), jnp.max(fresh, axis=1, keepdims=True)
-        )
-        weights = jnp.exp(scores - top)
-        fresh = jnp.exp(fresh - top)
-        total = jnp.sum(weights, axis=1, keepdims=True) + jnp.sum(fresh, axis=1, keepdims=True)
-        mixed = dot_nn(weights.astype(jnp.bfloat16), values[:, span])
-        mixed = (mixed + dot_nn(fresh.astype(jnp.bfloat16), fresh_v)) / total
+
+    def columns_of(pair):
+        return slice(pair * lanes, (pair + 1) * lanes)
+
+    def asked(pair):
+        return queries[pair * both : (pair + 1) * both, :].astype(jnp.bfloat16)
+
+    def tiles(block):
+        return [block[:, i : i + lanes] for i in range(0, block.shape[1], lanes)]
+
+    def score(pair, at):
+        chunk = dot_nt(asked(pair), keys[at : at + step, columns_of(pair)])
+        chunk = chunk + live[:, at : at + step]
+        held[pair % 2, :, at : at + step] = chunk
+        return functools.reduce(jnp.maximum, tiles(chunk))
+
+    def tree_score(pair):
+        fresh = dot_nt(asked(pair), new_keys[pair].astype(jnp.bfloat16))
+        return (fresh.reshape(2 * heads, draft, lanes) + mask[None]).reshape(fresh.shape)
+
+    chunks = range(0, slots, step)
+    for pair in range(pairs):
+        fill(pair)
+    fresh = tree_score(0)
+    peak = functools.reduce(jnp.maximum, [fresh] + [score(0, at) for at in chunks])
+    for pair in range(pairs):
+        top = jnp.max(peak, axis=1, keepdims=True)
+        weights = jnp.exp(fresh - top)
+        total = weights
+        mixed = dot_nn(weights.astype(jnp.bfloat16), new_values[pair].astype(jnp.bfloat16))
+        if pair + 1 < pairs:
+            fresh = peak = tree_score(pair + 1)
+        for at in chunks:
+            if pair + 1 < pairs:
+                peak = jnp.maximum(peak, score(pair + 1, at))
+            weights = jnp.exp(held[pair % 2, :, at : at + step] - top)
+            total = total + functools.reduce(jnp.add, tiles(weights))
+            part = dot_nn(weights.astype(jnp.bfloat16), values[at : at + step, columns_of(pair)])
+            mixed = mixed + part
+        mixed = mixed / jnp.sum(total, axis=1, keepdims=True)
         for p in range(2):
             for t in range(heads // 2):
                 at = (p * heads + 2 * t) * draft
@@ -415,6 +443,12 @@
                     tile = jnp.where(left, pltpu.roll(first, HEAD_DIM, 1), second)
                 col = p * q_cols + t * lanes
                 attended[pair, :, col : col + lanes] = tile
+    picked = pick[...].astype(jnp.bfloat16)
+    for pair in range(groups // 2):
+        for half, fresh in enumerate((new_keys, new_values)):
+            at = (half * (groups // 2) + pair) * lanes
+            rows = dot_nn(picked, fresh[pair].astype(jnp.bfloat16))
+            accepted_out[:, at : at + lanes] = rows.astype(jnp.bfloat16)
     for i, out in enumerate(outs):
         out[...] = attended[(me // 2) ^ i].astype(jnp.bfloat16)
 
@@ -430,13 +464,15 @@
 
 
 def residual_kernel(*refs):
-    me, pieces, routes, out, rows = refs[0][0], refs[1:9], refs[9], refs[10], refs[11]
+    me, pieces, routes, out, rows = refs[0][0], refs[1:5], refs[5], refs[6], refs[7]
     count = pieces[0].shape[0]
-    for k, piece in enumerate(pieces):
-        rows[pl.ds(pl.multiple_of((me ^ k) * count, 8), count), :] = piece[...].astype(jnp.float32)
-    half = out.shape[0]
-    chosen = named_slots(routes, me // 2, (me % 2) * half, half).astype(jnp.bfloat16)
-    out[...] = dot_nn(chosen, rows[...].astype(jnp.bfloat16))
+    expert = me // 2
+    rows[...] = jnp.zeros_like(rows)
+    for i, piece in enumerate(pieces):
+        at = pl.multiple_of((me ^ (2 * i)) * count, 8)
+        rows[pl.ds(at, count), :] = piece[...].astype(jnp.float32)
+    chosen = named_slots(routes, expert, expert * 0, out.shape[0]).astype(jnp.bfloat16)
+    out[...] = dot_nn(chosen, rows[...].astype(jnp.bfloat16)).astype(jnp.bfloat16)
 
 
 def outproj_kernel(*refs):
@@ -475,15 +511,18 @@
     out[...] = dot_nt(first, w_own[...]) + dot_nt(second, w_other[...])
 
 
-def expert_kernel(me_ref, mine, theirs, gain, router, routes, w_gate, w_up, w_down, out, rows, active):
+def expert_kernel(me_ref, mine, theirs, kept, other, gain, *refs):
+    router, routes, w_gate, w_up, w_down, out, rows, active = refs
     me = me_ref[0]
     core, expert = me % 2, me // 2
     half = mine.shape[0]
     rows[pl.ds(pl.multiple_of(core * half, 8), half), :] = mine[...].astype(jnp.float32)
     rows[pl.ds(pl.multiple_of((1 - core) * half, 8), half), :] = theirs[...].astype(jnp.float32)
-    floats = rows[...]
+    floats = rows[...] + kept[...].astype(jnp.float32) + other[...].astype(jnp.float32)
+    floats = floats.astype(jnp.bfloat16).astype(jnp.float32)
     mean_sq = jnp.mean(floats * floats, axis=-1, keepdims=True)
-    inputs = (floats * lax.rsqrt(mean_sq + EPSILON) * gain[...]).astype(jnp.bfloat16)
+    scale = gain[...].reshape(1, gain.shape[0])
+    inputs = (floats * lax.rsqrt(mean_sq + EPSILON) * scale).astype(jnp.bfloat16)
     experts, tokens = router.shape[0], routes.shape[1]
     logits = dot_nt(inputs, router[...])
     chosen = named_slots(routes, expert, expert * 0, 2 * half).astype(jnp.bfloat16)
@@ -545,6 +584,9 @@
     me = lax.axis_index("tp").astype(jnp.int32).reshape(1)
     bf16, f32 = jnp.bfloat16, jnp.float32
 
+    def spread(blocks):
+        return [blocks[0], *(swap(blocks[i], 2 * i) for i in (2, 3, 1))]
+
     def swap(values, offset):
         return lax.ppermute(values, "tp", [(i, i ^ offset) for i in range(devices)])
 
@@ -555,26 +597,23 @@
     half = capacity // 2
     routes_t = routes.T
     router_t = w_router.T
-    gain_row = attn_gain.reshape(1, width)
-    moe_row = moe_gain.reshape(1, width)
-
-    line = {s: swap(hidden, s) for s in (6, 4, 2)}
-    other_query, other_keyval = swap(w_query, 1), swap(w_keyval, 1)
+
+    line = [hidden, *(swap(hidden, s) for s in (2, 6, 4))]
     lanes = 128
     parents = jnp.pad(parents, ((0, 0), (0, lanes - draft)))
-    early = (gain_row, moe_row, parents, load(w_query, w_keyval))
+    other_query, other_keyval = swap(w_query, 1), swap(w_keyval, 1)
+    early = (parents, load(w_query, w_keyval))
     line, early = lax.optimization_barrier((line, early))
-    gain_row, moe_row, parents, (near_query, near_keyval) = early
-    line[0] = hidden
-
+    line = [line[i] for i in (0, 1, 3, 2)]
+    parents, (near_query, near_keyval) = early
     queries, keyvals = w_query.shape[1], w_keyval.shape[1]
     columns = queries + keyvals
     projected = run(
         project_kernel,
         [((rows, 2 * columns), bf16)] * 4,
         [
-            *(line[s] for s in (0, 2, 4, 6)),
-            gain_row,
+            *line,
+            attn_gain,
             near(near_query),
             near(near_keyval),
             near(other_query),
@@ -589,7 +628,7 @@
     later = (line, w_out, cache_keys[0], cache_values[0], cache_lens)
     later, projected = lax.optimization_barrier((later, projected))
     line, w_pair, keys, values, lens = later
-    arrived = [projected[0]] + [swap(projected[i], 2 * i) for i in (1, 2, 3)]
+    arrived = spread(projected)
     tree = run(
         tree_kernel,
         [((draft, lanes), f32), ((draft, lanes), f32), ((draft, lanes), f32), ((DEPTH, lanes), f32)],
@@ -597,11 +636,10 @@
         scalars=2,
         limit=4 * MIB,
     )
+    w_other = swap(w_pair, 1)
     cached = load(keys, values)
     arrived, tree, cached = lax.optimization_barrier((arrived, tree, cached))
-    across = {s: swap(line[s], 1) for s in (0, 2, 4, 6)}
-    pieces = [piece for s in (0, 2, 4, 6) for piece in (line[s], across[s])]
-    w_other = swap(w_pair, 1)
+    arrived = [arrived[i] for i in (0, 3, 1, 2)]
     slots, kv_cols = cache_keys.shape[1:]
     attended = run(
         attend_kernel,
@@ -610,21 +648,35 @@
         scalars=2,
         scratch=[
             pltpu.VMEM((devices, rows, columns), f32),
-            pltpu.VMEM((rows * queries * 2 // HEAD_DIM, lanes), f32),
-            pltpu.VMEM((lanes, lanes), f32),
-            pltpu.VMEM((lanes, lanes), f32),
+            pltpu.VMEM((rows * HEADS, lanes), f32),
+            pltpu.VMEM((devices // 2, lanes, lanes), f32),
+            pltpu.VMEM((devices // 2, lanes, lanes), f32),
             pltpu.VMEM((devices // 2, rows, 2 * queries), f32),
+            pltpu.VMEM((2, rows * queries * 2 // HEAD_DIM, slots), f32),
         ],
-        limit=14 * MIB,
+        limit=16 * MIB,
         flops=4 * rows * HEADS * slots * HEAD_DIM,
         moved=4 * slots * kv_cols,
     )
     accepted_kv = attended[4][None]
-    (w_own, w_other), attended = lax.optimization_barrier(((w_out, w_other), attended))
-    straight = [attended[0]] + [swap(attended[i], 2 * i) for i in (1, 2, 3)]
+    later = (w_out, w_other, me)
+    (w_own, w_other, me_now), attended = lax.optimization_barrier((later, attended))
+    straight = spread(attended)
     near_out = load(w_own.T, w_other.T)
-    straight, near_out = lax.optimization_barrier((straight, near_out))
-    crossed = [swap(block, 1) for block in straight]
+    residual = run(
+        residual_kernel,
+        [((capacity, width), bf16)],
+        [me_now, *line, routes_t],
+        scratch=[pltpu.VMEM((tokens, width), f32)],
+        limit=6 * MIB,
+        flops=2 * half * tokens * width,
+        moved=tokens * width * 4,
+    )[0]
+    own_crossed = swap(straight[0], 1)
+    shadow = (near_out, residual, own_crossed)
+    straight, (near_out, residual, own_crossed) = lax.optimization_barrier((straight, shadow))
+    straight = [straight[i] for i in (0, 3, 1, 2)]
+    crossed = [own_crossed, *(swap(block, 1) for block in straight[1:])]
     blocks = [block for pair in zip(straight, crossed) for block in pair]
     out_flops = 2 * 4 * half * 2 * queries * width
     dispatched = run(
@@ -636,10 +688,11 @@
         flops=out_flops,
         moved=4 * queries * width,
     )
-    arrived = [swap(dispatched[i], 2 * i) for i in (1, 2, 3)]
-    (me_then, experts), _ = lax.optimization_barrier(
-        ((me, (w_gate, w_up, w_down)), dispatched[1])
-    )
+    arrived = spread(dispatched)[1:]
+    (me_then, residual, experts), _ = lax.optimization_barrier(
+        ((me, residual, (w_gate, w_up, w_down)), dispatched[1])
+    )
+    residuals = (residual, swap(residual, 1))
     sums = run(
         token_kernel,
         [((4 * rows, width), f32)],
@@ -649,20 +702,10 @@
         flops=out_flops,
         moved=4 * queries * width,
     )[0]
-    residual = run(
-        residual_kernel,
-        [((half, width), f32)],
-        [me_then, *pieces, routes_t],
-        scratch=[pltpu.VMEM((tokens, width), f32)],
-        limit=6 * MIB,
-        flops=2 * half * tokens * width,
-        moved=tokens * width * 4,
-    )[0]
     near_weights = load(*experts)
-    middle, arrived, sums, residual, near_weights = lax.optimization_barrier(
-        (dispatched[0], arrived, sums, residual, near_weights)
-    )
-    middle = middle + residual
+    middle, arrived, sums, residuals, near_weights = lax.optimization_barrier(
+        (dispatched[0], arrived, sums, residuals, near_weights)
+    )
     for block in arrived:
         middle = middle + block.astype(f32)
     middle = middle.astype(bf16)
@@ -673,7 +716,8 @@
             me,
             middle,
             swap(middle, 1),
-            moe_row,
+            *residuals,
+            moe_gain,
             router_t,
             routes_t,
             *map(near, near_weights),
@@ -691,9 +735,9 @@
         flops=2 * capacity * tokens * width,
         moved=tokens * width * 4,
     )
-    layer_out = combined[0]
-    for i in (1, 2, 3):
-        layer_out = layer_out + swap(combined[i], 2 * i).astype(f32)
+    layer_out, *arrived = spread(combined)
+    for block in arrived:
+        layer_out = layer_out + block.astype(f32)
     return (layer_out.astype(bf16), accepted_kv)
 
 

time: 89.9 us -> 87.9 us (0.978)
  starting transfers between devices: 25.2 us -> 24.1 us
    ppermute x28 -> x25, starting transfers between devices: 25.2 us -> 24.1 us  [swap(): return lax.ppermute(values, 'tp', [(i, i ^ offset) for i in range(devices)])]
    ppermute x28 -> x25, waiting for transfers between devices: 25.3 us -> 25 us  [swap(): return lax.ppermute(values, 'tp', [(i, i ^ offset) for i in range(devices)])]
  transfers between devices with their start and end apart: 28 -> 25, of which waited for: 10 -> 12; matrix products, arithmetic and copies ran while one was open for 0% -> 0% of each run, Pallas kernels for 31% -> 28%
where the time goes in v4:
time: 87.9 us; the launch traced here: 87.7 us
  Pallas kernels  35.6 us (41%)
  waiting for transfers between devices  25 us (28%)
  starting transfers between devices  24.1 us (27%)
  between operations  2.15 us (2%)
    ppermute x25, waiting for transfers between devices, swap(): return lax.ppermute(values, 'tp', [(i, i ^ offset) for i in range(devices)])  25 us
    ppermute x25, starting transfers between devices, swap(): return lax.ppermute(values, 'tp', [(i, i ^ offset) for i in range(devices)])  24.1 us
    pallas_call x8, Pallas kernels, run(): pl.pallas_call(kernel, out_shape=tuple((jax.ShapeDtypeStruct(s, t) for s,...  20.4 us
    pallas_call x4, Pallas kernels, load(): pl.pallas_call(kernel, out_shape=tuple((pltpu.VMEM(a.shape, a.dtype) for...  15.3 us
  transfers between devices with their start and end apart: 25, of which 12 were waited for; matrix products, arithmetic and copies ran while one was open for 0% of the time, Pallas kernels for 28%

profile of v4, /device:TPU:0, one launch (start us, length us, event | category | flops | bytes accessed | tf_op | source)
XLA Modules:
  0.0 87.7 jit_solution(12136804532243428172)
XLA Ops:
  1.3 4.0 %collective-permute-start.2 = (bf16[24,2880]{1,0:T(8,128)(2,1)}, bf16[24,2880]{1,0:T(8,128)(2,1)S(1)}, u32[]{:S(2)}, u32[]{:S(2)}) collective-permute-start(bf16[24,2880]{1,0:T(8,128)(2,1)} %refs_5_.1), channel_id=1, source_target_pairs={{0,4},{1,5},{2,6},{3,7},{4,0},{5,1},{6,2},{7,3},{8,12},{9,13},{10,... | collective-permute-start | bytes 414728 | tf_op jit(solution)/shard_map/ppermute | solution.py:591
  5.3 1.3 %collective-permute-start.1 = (bf16[24,2880]{1,0:T(8,128)(2,1)}, bf16[24,2880]{1,0:T(8,128)(2,1)S(1)}, u32[]{:S(2)}, u32[]{:S(2)}) collective-permute-start(bf16[24,2880]{1,0:T(8,128)(2,1)} %refs_5_.1), channel_id=1, source_target_pairs={{0,6},{1,7},{2,4},{3,5},{4,2},{5,3},{6,0},{7,1},{8,14},{9,15},{10,... | collective-permute-start | bytes 414728 | tf_op jit(solution)/shard_map/ppermute | solution.py:591
  6.9 2.0 %shard_map.167 = (bf16[2880,512]{1,0:T(8,128)(2,1)S(1)}, bf16[2880,128]{1,0:T(8,128)(2,1)S(1)}) custom-call(bf16[2880,512]{1,0:T(8,128)(2,1)} %refs_0_.1, bf16[2880,128]{1,0:T(8,128)(2,1)} %refs_1_.2), custom_call_target="tpu_custom_call" | custom-call | bytes 7372800 | tf_op jit(solution)/shard_map/pallas_call | solution.py:273
  8.9 7.2 %collective-permute-done.2.refs_2_.refs_3_ = bf16[24,2880]{1,0:T(8,128)(2,1)S(1)} collective-permute-done((bf16[24,2880]{1,0:T(8,128)(2,1)}, bf16[24,2880]{1,0:T(8,128)(2,1)S(1)}, u32[]{:S(2)}, u32[]{:S(2)}) %collective-permute-start.2) | collective-permute-done | bytes 138272 | tf_op jit(solution)/shard_map/ppermute | solution.py:591
  16.1 0.8 collective-permute-done.refs_1_.refs_2_
  16.9 1.6 %shard_map.168 = (bf16[24,1280]{1,0:T(8,128)(2,1)S(1)}, bf16[24,1280]{1,0:T(8,128)(2,1)S(1)}, bf16[24,1280]{1,0:T(8,128)(2,1)S(1)}, bf16[24,1280]{1,0:T(8,128)(2,1)S(1)}) custom-call(bf16[24,2880]{1,0:T(8,128)(2,1)S(1)} %copy-done, bf16[24,2880]{1,0:T(8,128)(2,1)S(1)} %collective-permute-done.refs_1_.refs_2_, ...), custom_call_target="tpu_custom_call" | custom-call | flops 707788800 | bytes 3686400 | tf_op jit(solution)/shard_map/pallas_call | solution.py:240
  18.6 4.4 %collective-permute-start.6 = (bf16[24,1280]{1,0:T(8,128)(2,1)S(1)}, bf16[24,1280]{1,0:T(8,128)(2,1)S(1)}, u32[]{:S(2)}, u32[]{:S(2)}) collective-permute-start(bf16[24,1280]{1,0:T(8,128)(2,1)S(1)} %get-tuple-element.105), channel_id=1, source_target_pairs={{0,4},{1,5},{2,6},{3,7},{4,0},{5,1},{6,2},{7,3},{8,12},{9,13},{10,... | collective-permute-start | bytes 184328 | tf_op jit(solution)/shard_map/ppermute | solution.py:591
  24.9 0.7 shard_map.169
  25.7 2.2 %shard_map.170 = (bf16[2048,512]{1,0:T(8,128)(2,1)S(1)}, bf16[2048,512]{1,0:T(8,128)(2,1)S(1)}) custom-call(bf16[2048,512]{1,0:T(8,128)(2,1)} %bitcast.13, bf16[2048,512]{1,0:T(8,128)(2,1)} %bitcast.14), custom_call_target="tpu_custom_call" | custom-call | bytes 8388608 | tf_op jit(solution)/shard_map/pallas_call | solution.py:273
  27.9 1.6 %collective-permute-done.7.refs_5_ = bf16[24,1280]{1,0:T(8,128)(2,1)S(1)} collective-permute-done((bf16[24,1280]{1,0:T(8,128)(2,1)S(1)}, bf16[24,1280]{1,0:T(8,128)(2,1)S(1)}, u32[]{:S(2)}, u32[]{:S(2)}) %collective-permute-start.7) | collective-permute-done | bytes 61472 | tf_op jit(solution)/shard_map/ppermute | solution.py:591
  29.6 6.0 %shard_map.171 = (bf16[24,1024]{1,0:T(8,128)(2,1)S(1)}, bf16[24,1024]{1,0:T(8,128)(2,1)S(1)}, bf16[24,1024]{1,0:T(8,128)(2,1)S(1)}, bf16[24,1024]{1,0:T(8,128)(2,1)S(1)}, bf16[8,1024]{1,0:T(8,128)(2,1)}) custom-call(s32[1]{0:T(128)} %bitcast.refs_0_.me_ref, s32[1]{0:T(128)S(6)} %copy.18.lens.refs_1_, bf16[24,1280]{1,0:T(8,128)(2,1)S(1)} %get-tuple-element.118.refs_2_, ...), custom_call_target="tpu_custom_call" | custom-call | flops 805306368 | bytes 4194304 | tf_op jit(solution)/shard_map/pallas_call | solution.py:240
  35.6 2.1 %collective-permute-start.9 = (bf16[24,1024]{1,0:T(8,128)(2,1)S(1)}, bf16[24,1024]{1,0:T(8,128)(2,1)S(1)}, u32[]{:S(2)}, u32[]{:S(2)}) collective-permute-start(bf16[24,1024]{1,0:T(8,128)(2,1)S(1)} %get-tuple-element.134), channel_id=1, source_target_pairs={{0,4},{1,5},{2,6},{3,7},{4,0},{5,1},{6,2},{7,3},{8,12},{9,13},{10,... | collective-permute-start | bytes 147464 | tf_op jit(solution)/shard_map/ppermute | solution.py:591
  37.7 0.8 collective-permute-start.10
  38.5 0.6 collective-permute-start.11
  39.1 2.8 %shard_map.172 = (bf16[2880,512]{1,0:T(8,128)(2,1)S(1)}, bf16[2880,512]{1,0:T(8,128)(2,1)S(1)}) custom-call(bf16[2880,512]{1,0:T(8,128)(2,1)} %bitcast.3.refs_0_, bf16[2880,512]{1,0:T(8,128)(2,1)} %bitcast.4.refs_1_), custom_call_target="tpu_custom_call" | custom-call | bytes 11796480 | tf_op jit(solution)/shard_map/pallas_call | solution.py:273
  41.8 0.6 shard_map.173.kept
  42.4 1.1 %collective-permute-done.10.refs_7_.refs_4_ = bf16[24,1024]{1,0:T(8,128)(2,1)S(1)} collective-permute-done((bf16[24,1024]{1,0:T(8,128)(2,1)S(1)}, bf16[24,1024]{1,0:T(8,128)(2,1)S(1)}, u32[]{:S(2)}, u32[]{:S(2)}) %collective-permute-start.10) | collective-permute-done | bytes 49184 | tf_op jit(solution)/shard_map/ppermute | solution.py:591
  44.2 0.6 collective-permute-done.13.refs_4_
  45.3 2.2 %shard_map.174 = (f32[24,2880]{1,0:T(8,128)S(1)}, bf16[24,2880]{1,0:T(8,128)(2,1)S(1)}, bf16[24,2880]{1,0:T(8,128)(2,1)S(1)}, bf16[24,2880]{1,0:T(8,128)(2,1)S(1)}) custom-call(s32[1]{0:T(128)} %bitcast.refs_0_.me_ref, bf16[24,1024]{1,0:T(8,128)(2,1)S(1)} %get-tuple-element.146.refs_1_, bf16[24,1024]{1,0:T(8,128)(2,1)S(1)} %collective-permute-done.12.refs_2_, ...), custom_call_target="tpu_custom_call" | custom-call | flops 566231040 | bytes 5898240 | tf_op jit(solution)/shard_map/pallas_call | solution.py:240
  47.7 2.3 %collective-permute-start.16 = (bf16[24,2880]{1,0:T(8,128)(2,1)S(1)}, bf16[24,2880]{1,0:T(8,128)(2,1)S(1)}, u32[]{:S(2)}, u32[]{:S(2)}) collective-permute-start(bf16[24,2880]{1,0:T(8,128)(2,1)S(1)} %get-tuple-element.154), channel_id=1, source_target_pairs={{0,4},{1,5},{2,6},{3,7},{4,0},{5,1},{6,2},{7,3},{8,12},{9,13},{10,... | collective-permute-start | bytes 414728 | tf_op jit(solution)/shard_map/ppermute | solution.py:591
  50.1 0.7 collective-permute-start.17
  51.2 8.3 %shard_map.176 = (bf16[1440,2880]{1,0:T(8,128)(2,1)S(1)}, bf16[1440,2880]{1,0:T(8,128)(2,1)S(1)}, bf16[1440,2880]{1,0:T(8,128)(2,1)S(1)}) custom-call(bf16[1440,2880]{1,0:T(8,128)(2,1)} %refs_0_.3, bf16[1440,2880]{1,0:T(8,128)(2,1)} %refs_1_.4, bf16[1440,2880]{1,0:T(8,128)(2,1)} %refs_2_), custom_call_target="tpu_custom_call" | custom-call | bytes 49766400 | tf_op jit(solution)/shard_map/pallas_call | solution.py:273
  59.5 1.9 %shard_map.175.refs_4_ = f32[96,2880]{1,0:T(8,128)S(1)} custom-call(s32[1]{0:T(128)} %bitcast.refs_0_.me_ref, bf16[24,1024]{1,0:T(8,128)(2,1)S(1)} %get-tuple-element.146.refs_1_, bf16[24,1024]{1,0:T(8,128)(2,1)S(1)} %collective-permute-done.11.refs_3_.refs_2_, bf16[24,1024]{1,0:T(8,128)(2,1)S(1)} %collective-permute-done.9.refs_5_.refs_3_, ...), custom_call_target="tpu_custom_call" | custom-call | flops 566231040 | bytes 5898240 | tf_op jit(solution)/shard_map/pallas_call | solution.py:240
  62.2 1.3 %collective-permute-done.20.theirs = bf16[24,2880]{1,0:T(8,128)(2,1)S(1)} collective-permute-done((bf16[24,2880]{1,0:T(8,128)(2,1)S(1)}, bf16[24,2880]{1,0:T(8,128)(2,1)S(1)}, u32[]{:S(2)}, u32[]{:S(2)}) %collective-permute-start.20) | collective-permute-done | bytes 138272 | tf_op jit(solution)/shard_map/ppermute | solution.py:591
  63.5 6.6 %shard_map.177.refs_1_ = bf16[48,2880]{1,0:T(8,128)(2,1)S(1)} custom-call(s32[1]{0:T(128)} %bitcast.refs_0_.me_ref, bf16[24,2880]{1,0:T(8,128)(2,1)S(1)} %add_convert_fusion.1.mine, bf16[24,2880]{1,0:T(8,128)(2,1)S(1)} %collective-permute-done.20.theirs, bf16[48,2880]{1,0:T(8,128)(2,1)S(1)} %shard_map.173.kept, ...), custom_call_target="tpu_custom_call" | custom-call | flops 1194393600 | bytes 24883200 | tf_op jit(solution)/shard_map/pallas_call | solution.py:240
  70.4 1.4 %collective-permute-done.21.refs_2_ = bf16[48,2880]{1,0:T(8,128)(2,1)S(1)} collective-permute-done((bf16[48,2880]{1,0:T(8,128)(2,1)S(1)}, bf16[48,2880]{1,0:T(8,128)(2,1)S(1)}, u32[]{:S(2)}, u32[]{:S(2)}) %collective-permute-start.21) | collective-permute-done | bytes 276512 | tf_op jit(solution)/shard_map/ppermute | solution.py:591
  71.8 0.8 shard_map.178
  72.6 2.9 %collective-permute-start.22 = (bf16[24,2880]{1,0:T(8,128)(2,1)S(1)}, bf16[24,2880]{1,0:T(8,128)(2,1)S(1)}, u32[]{:S(2)}, u32[]{:S(2)}) collective-permute-start(bf16[24,2880]{1,0:T(8,128)(2,1)S(1)} %get-tuple-element.177), channel_id=1, source_target_pairs={{0,4},{1,5},{2,6},{3,7},{4,0},{5,1},{6,2},{7,3},{8,12},{9,13},{10,... | collective-permute-start | bytes 414728 | tf_op jit(solution)/shard_map/ppermute | solution.py:591
  75.5 1.8 %collective-permute-start.23 = (bf16[24,2880]{1,0:T(8,128)(2,1)S(1)}, bf16[24,2880]{1,0:T(8,128)(2,1)S(1)}, u32[]{:S(2)}, u32[]{:S(2)}) collective-permute-start(bf16[24,2880]{1,0:T(8,128)(2,1)S(1)} %get-tuple-element.178), channel_id=1, source_target_pairs={{0,6},{1,7},{2,4},{3,5},{4,2},{5,3},{6,0},{7,1},{8,14},{9,15},{10,... | collective-permute-start | bytes 414728 | tf_op jit(solution)/shard_map/ppermute | solution.py:591
  77.3 8.9 %collective-permute-done.22 = bf16[24,2880]{1,0:T(8,128)(2,1)S(1)} collective-permute-done((bf16[24,2880]{1,0:T(8,128)(2,1)S(1)}, bf16[24,2880]{1,0:T(8,128)(2,1)S(1)}, u32[]{:S(2)}, u32[]{:S(2)}) %collective-permute-start.22) | collective-permute-done | bytes 138272 | tf_op jit(solution)/shard_map/ppermute | solution.py:591
  86.2 0.8 collective-permute-done.24
  87.0 0.7 add_convert_fusion
  (45 shorter events, 4.3 us)
Async XLA Ops:
  0.6 16.2 %copy-start = (bf16[24,2880]{1,0:T(8,128)(2,1)S(1)}, bf16[24,2880]{1,0:T(8,128)(2,1)}, u32[]{:S(2)}) copy-start(bf16[24,2880]{1,0:T(8,128)(2,1)} %refs_5_.1) | copy-start | bytes 414724
  0.6 8.2 %copy-start.5 = (s32[1,24]{1,0:T(1,128)S(1)}, s32[1,24]{1,0:T(1,128)}, u32[]{:S(2)}) copy-start(s32[1,24]{1,0:T(1,128)} %param.24) | copy-start | bytes 292
  0.7 16.2 %copy-start.3 = (f32[2880]{0:T(1024)S(1)}, f32[2880]{0:T(1024)}, u32[]{:S(2)}) copy-start(f32[2880]{0:T(1024)} %refs_4_.1) | copy-start | bytes 34564
  0.7 16.2 %collective-permute-start.3 = (bf16[2880,512]{1,0:T(8,128)(2,1)}, bf16[2880,512]{1,0:T(8,128)(2,1)S(1)}, u32[]{:S(2)}, u32[]{:S(2)}) collective-permute-start(bf16[2880,512]{1,0:T(8,128)(2,1)} %refs_0_.1), channel_id=1, source_target_pairs={{0,1},{1,0},{2,3},{3,2},{4,5},{5,4},{6,7},{7,6},{8,9},{9,8},{10,11... | collective-permute-start | bytes 8847368 | tf_op jit(solution)/shard_map/ppermute | solution.py:591
  1.2 15.7 %collective-permute-start.4 = (bf16[2880,128]{1,0:T(8,128)(2,1)}, bf16[2880,128]{1,0:T(8,128)(2,1)S(1)}, u32[]{:S(2)}, u32[]{:S(2)}) collective-permute-start(bf16[2880,128]{1,0:T(8,128)(2,1)} %refs_1_.2), channel_id=1, source_target_pairs={{0,1},{1,0},{2,3},{3,2},{4,5},{5,4},{6,7},{7,6},{8,9},{9,8},{10,11... | collective-permute-start | bytes 2211848 | tf_op jit(solution)/shard_map/ppermute | solution.py:591
  1.3 14.8 %collective-permute-start.2 = (bf16[24,2880]{1,0:T(8,128)(2,1)}, bf16[24,2880]{1,0:T(8,128)(2,1)S(1)}, u32[]{:S(2)}, u32[]{:S(2)}) collective-permute-start(bf16[24,2880]{1,0:T(8,128)(2,1)} %refs_5_.1), channel_id=1, source_target_pairs={{0,4},{1,5},{2,6},{3,7},{4,0},{5,1},{6,2},{7,3},{8,12},{9,13},{10,... | collective-permute-start | bytes 414728 | tf_op jit(solution)/shard_map/ppermute | solution.py:591
  5.3 10.8 %collective-permute-start.1 = (bf16[24,2880]{1,0:T(8,128)(2,1)}, bf16[24,2880]{1,0:T(8,128)(2,1)S(1)}, u32[]{:S(2)}, u32[]{:S(2)}) collective-permute-start(bf16[24,2880]{1,0:T(8,128)(2,1)} %refs_5_.1), channel_id=1, source_target_pairs={{0,6},{1,7},{2,4},{3,5},{4,2},{5,3},{6,0},{7,1},{8,14},{9,15},{10,... | collective-permute-start | bytes 414728 | tf_op jit(solution)/shard_map/ppermute | solution.py:591
  6.6 10.2 %collective-permute-start = (bf16[24,2880]{1,0:T(8,128)(2,1)}, bf16[24,2880]{1,0:T(8,128)(2,1)S(1)}, u32[]{:S(2)}, u32[]{:S(2)}) collective-permute-start(bf16[24,2880]{1,0:T(8,128)(2,1)} %refs_5_.1), channel_id=1, source_target_pairs={{0,2},{1,3},{2,0},{3,1},{4,6},{5,7},{6,4},{7,5},{8,10},{9,11},{10,... | collective-permute-start | bytes 414728 | tf_op jit(solution)/shard_map/ppermute | solution.py:591
  18.5 17.1 %collective-permute-start.5 = (bf16[512,2880]{0,1:T(8,128)(2,1)}, bf16[512,2880]{0,1:T(8,128)(2,1)}, u32[]{:S(2)}, u32[]{:S(2)}) collective-permute-start(bf16[512,2880]{0,1:T(8,128)(2,1)} %param.20), channel_id=1, source_target_pairs={{0,1},{1,0},{2,3},{3,2},{4,5},{5,4},{6,7},{7,6},{8,9},{9,8},{10,11... | collective-permute-start | bytes 8847368 | tf_op jit(solution)/shard_map/ppermute | solution.py:591
  18.6 9.3 %collective-permute-start.6 = (bf16[24,1280]{1,0:T(8,128)(2,1)S(1)}, bf16[24,1280]{1,0:T(8,128)(2,1)S(1)}, u32[]{:S(2)}, u32[]{:S(2)}) collective-permute-start(bf16[24,1280]{1,0:T(8,128)(2,1)S(1)} %get-tuple-element.105), channel_id=1, source_target_pairs={{0,4},{1,5},{2,6},{3,7},{4,0},{5,1},{6,2},{7,3},{8,12},{9,13},{10,... | collective-permute-start | bytes 184328 | tf_op jit(solution)/shard_map/ppermute | solution.py:591
  23.0 6.5 %collective-permute-start.7 = (bf16[24,1280]{1,0:T(8,128)(2,1)S(1)}, bf16[24,1280]{1,0:T(8,128)(2,1)S(1)}, u32[]{:S(2)}, u32[]{:S(2)}) collective-permute-start(bf16[24,1280]{1,0:T(8,128)(2,1)S(1)} %get-tuple-element.106), channel_id=1, source_target_pairs={{0,6},{1,7},{2,4},{3,5},{4,2},{5,3},{6,0},{7,1},{8,14},{9,15},{10,... | collective-permute-start | bytes 184328 | tf_op jit(solution)/shard_map/ppermute | solution.py:591
  23.6 6.0 %collective-permute-start.8 = (bf16[24,1280]{1,0:T(8,128)(2,1)S(1)}, bf16[24,1280]{1,0:T(8,128)(2,1)S(1)}, u32[]{:S(2)}, u32[]{:S(2)}) collective-permute-start(bf16[24,1280]{1,0:T(8,128)(2,1)S(1)} %get-tuple-element.107), channel_id=1, source_target_pairs={{0,2},{1,3},{2,0},{3,1},{4,6},{5,7},{6,4},{7,5},{8,10},{9,11},{10,... | collective-permute-start | bytes 184328 | tf_op jit(solution)/shard_map/ppermute | solution.py:591
  35.6 6.9 %collective-permute-start.9 = (bf16[24,1024]{1,0:T(8,128)(2,1)S(1)}, bf16[24,1024]{1,0:T(8,128)(2,1)S(1)}, u32[]{:S(2)}, u32[]{:S(2)}) collective-permute-start(bf16[24,1024]{1,0:T(8,128)(2,1)S(1)} %get-tuple-element.134), channel_id=1, source_target_pairs={{0,4},{1,5},{2,6},{3,7},{4,0},{5,1},{6,2},{7,3},{8,12},{9,13},{10,... | collective-permute-start | bytes 147464 | tf_op jit(solution)/shard_map/ppermute | solution.py:591
  37.7 5.9 %collective-permute-start.10 = (bf16[24,1024]{1,0:T(8,128)(2,1)S(1)}, bf16[24,1024]{1,0:T(8,128)(2,1)S(1)}, u32[]{:S(2)}, u32[]{:S(2)}) collective-permute-start(bf16[24,1024]{1,0:T(8,128)(2,1)S(1)} %get-tuple-element.135), channel_id=1, source_target_pairs={{0,6},{1,7},{2,4},{3,5},{4,2},{5,3},{6,0},{7,1},{8,14},{9,15},{10,... | collective-permute-start | bytes 147464 | tf_op jit(solution)/shard_map/ppermute | solution.py:591
  38.5 5.1 %collective-permute-start.11 = (bf16[24,1024]{1,0:T(8,128)(2,1)S(1)}, bf16[24,1024]{1,0:T(8,128)(2,1)S(1)}, u32[]{:S(2)}, u32[]{:S(2)}) collective-permute-start(bf16[24,1024]{1,0:T(8,128)(2,1)S(1)} %get-tuple-element.136), channel_id=1, source_target_pairs={{0,2},{1,3},{2,0},{3,1},{4,6},{5,7},{6,4},{7,5},{8,10},{9,11},{10,... | collective-permute-start | bytes 147464 | tf_op jit(solution)/shard_map/ppermute | solution.py:591
  39.0 4.5 %collective-permute-start.12 = (bf16[24,1024]{1,0:T(8,128)(2,1)S(1)}, bf16[24,1024]{1,0:T(8,128)(2,1)S(1)}, u32[]{:S(2)}, u32[]{:S(2)}) collective-permute-start(bf16[24,1024]{1,0:T(8,128)(2,1)S(1)} %get-tuple-element.146.refs_1_), channel_id=1, source_target_pairs={{0,1},{1,0},{2,3},{3,2},{4,5},{5,4},{6,7},{7,6},{8,9},{9,8},{10,11... | collective-permute-start | bytes 147464 | tf_op jit(solution)/shard_map/ppermute | solution.py:591
  39.0 2.8 %copy-start.2 = (s32[192,4]{0,1:T(4,128)S(1)}, s32[192,4]{0,1:T(4,128)}, u32[]{:S(2)}) copy-start(s32[192,4]{0,1:T(4,128)} %param.28) | copy-start | bytes 9220
  43.6 1.2 %collective-permute-start.13 = (bf16[24,1024]{1,0:T(8,128)(2,1)S(1)}, bf16[24,1024]{1,0:T(8,128)(2,1)S(1)}, u32[]{:S(2)}, u32[]{:S(2)}) collective-permute-start(bf16[24,1024]{1,0:T(8,128)(2,1)S(1)} %collective-permute-done.11.refs_3_.refs_2_), channel_id=1, source_target_pairs={{0,1},{1,0},{2,3},{3,2},{4,5},{5,4},{6,7},{7,6},{8,9},{9,8},{10,11... | collective-permute-start | bytes 147464 | tf_op jit(solution)/shard_map/ppermute | solution.py:591
  43.6 1.4 %collective-permute-start.14 = (bf16[24,1024]{1,0:T(8,128)(2,1)S(1)}, bf16[24,1024]{1,0:T(8,128)(2,1)S(1)}, u32[]{:S(2)}, u32[]{:S(2)}) collective-permute-start(bf16[24,1024]{1,0:T(8,128)(2,1)S(1)} %collective-permute-done.9.refs_5_.refs_3_), channel_id=1, source_target_pairs={{0,1},{1,0},{2,3},{3,2},{4,5},{5,4},{6,7},{7,6},{8,9},{9,8},{10,11... | collective-permute-start | bytes 147464 | tf_op jit(solution)/shard_map/ppermute | solution.py:591
  44.1 1.2 %collective-permute-start.15 = (bf16[24,1024]{1,0:T(8,128)(2,1)S(1)}, bf16[24,1024]{1,0:T(8,128)(2,1)S(1)}, u32[]{:S(2)}, u32[]{:S(2)}) collective-permute-start(bf16[24,1024]{1,0:T(8,128)(2,1)S(1)} %collective-permute-done.10.refs_7_.refs_4_), channel_id=1, source_target_pairs={{0,1},{1,0},{2,3},{3,2},{4,5},{5,4},{6,7},{7,6},{8,9},{9,8},{10,11... | collective-permute-start | bytes 147464 | tf_op jit(solution)/shard_map/ppermute | solution.py:591
  47.5 14.5 %collective-permute-start.19 = (bf16[48,2880]{1,0:T(8,128)(2,1)S(1)}, bf16[48,2880]{1,0:T(8,128)(2,1)S(1)}, u32[]{:S(2)}, u32[]{:S(2)}) collective-permute-start(bf16[48,2880]{1,0:T(8,128)(2,1)S(1)} %shard_map.173.kept), channel_id=1, source_target_pairs={{0,1},{1,0},{2,3},{3,2},{4,5},{5,4},{6,7},{7,6},{8,9},{9,8},{10,11... | collective-permute-start | bytes 829448 | tf_op jit(solution)/shard_map/ppermute | solution.py:591
  47.7 13.7 %collective-permute-start.16 = (bf16[24,2880]{1,0:T(8,128)(2,1)S(1)}, bf16[24,2880]{1,0:T(8,128)(2,1)S(1)}, u32[]{:S(2)}, u32[]{:S(2)}) collective-permute-start(bf16[24,2880]{1,0:T(8,128)(2,1)S(1)} %get-tuple-element.154), channel_id=1, source_target_pairs={{0,4},{1,5},{2,6},{3,7},{4,0},{5,1},{6,2},{7,3},{8,12},{9,13},{10,... | collective-permute-start | bytes 414728 | tf_op jit(solution)/shard_map/ppermute | solution.py:591
  50.1 11.3 %collective-permute-start.17 = (bf16[24,2880]{1,0:T(8,128)(2,1)S(1)}, bf16[24,2880]{1,0:T(8,128)(2,1)S(1)}, u32[]{:S(2)}, u32[]{:S(2)}) collective-permute-start(bf16[24,2880]{1,0:T(8,128)(2,1)S(1)} %get-tuple-element.155), channel_id=1, source_target_pairs={{0,6},{1,7},{2,4},{3,5},{4,2},{5,3},{6,0},{7,1},{8,14},{9,15},{10,... | collective-permute-start | bytes 414728 | tf_op jit(solution)/shard_map/ppermute | solution.py:591
  50.8 11.2 %collective-permute-start.18 = (bf16[24,2880]{1,0:T(8,128)(2,1)S(1)}, bf16[24,2880]{1,0:T(8,128)(2,1)S(1)}, u32[]{:S(2)}, u32[]{:S(2)}) collective-permute-start(bf16[24,2880]{1,0:T(8,128)(2,1)S(1)} %get-tuple-element.156), channel_id=1, source_target_pairs={{0,2},{1,3},{2,0},{3,1},{4,6},{5,7},{6,4},{7,5},{8,10},{9,11},{10,... | collective-permute-start | bytes 414728 | tf_op jit(solution)/shard_map/ppermute | solution.py:591
  59.5 4.0 %copy-start.1 = (bf16[2880,32]{0,1:T(8,128)(2,1)S(1)}, bf16[2880,32]{0,1:T(8,128)(2,1)}, u32[]{:S(2)}) copy-start(bf16[2880,32]{0,1:T(8,128)(2,1)} %param.27) | copy-start | bytes 552964
  59.5 4.0 %copy-start.4 = (f32[2880]{0:T(1024)S(1)}, f32[2880]{0:T(1024)}, u32[]{:S(2)}) copy-start(f32[2880]{0:T(1024)} %gain.1) | copy-start | bytes 34564
  62.1 1.4 %collective-permute-start.20 = (bf16[24,2880]{1,0:T(8,128)(2,1)S(1)}, bf16[24,2880]{1,0:T(8,128)(2,1)S(1)}, u32[]{:S(2)}, u32[]{:S(2)}) collective-permute-start(bf16[24,2880]{1,0:T(8,128)(2,1)S(1)} %add_convert_fusion.1.mine), channel_id=1, source_target_pairs={{0,1},{1,0},{2,3},{3,2},{4,5},{5,4},{6,7},{7,6},{8,9},{9,8},{10,11... | collective-permute-start | bytes 414728 | tf_op jit(solution)/shard_map/ppermute | solution.py:591
  70.2 1.6 %collective-permute-start.21 = (bf16[48,2880]{1,0:T(8,128)(2,1)S(1)}, bf16[48,2880]{1,0:T(8,128)(2,1)S(1)}, u32[]{:S(2)}, u32[]{:S(2)}) collective-permute-start(bf16[48,2880]{1,0:T(8,128)(2,1)S(1)} %shard_map.177.refs_1_), channel_id=1, source_target_pairs={{0,1},{1,0},{2,3},{3,2},{4,5},{5,4},{6,7},{7,6},{8,9},{9,8},{10,11... | collective-permute-start | bytes 829448 | tf_op jit(solution)/shard_map/ppermute | solution.py:591
  72.6 13.6 %collective-permute-start.22 = (bf16[24,2880]{1,0:T(8,128)(2,1)S(1)}, bf16[24,2880]{1,0:T(8,128)(2,1)S(1)}, u32[]{:S(2)}, u32[]{:S(2)}) collective-permute-start(bf16[24,2880]{1,0:T(8,128)(2,1)S(1)} %get-tuple-element.177), channel_id=1, source_target_pairs={{0,4},{1,5},{2,6},{3,7},{4,0},{5,1},{6,2},{7,3},{8,12},{9,13},{10,... | collective-permute-start | bytes 414728 | tf_op jit(solution)/shard_map/ppermute | solution.py:591
  75.5 10.7 %collective-permute-start.23 = (bf16[24,2880]{1,0:T(8,128)(2,1)S(1)}, bf16[24,2880]{1,0:T(8,128)(2,1)S(1)}, u32[]{:S(2)}, u32[]{:S(2)}) collective-permute-start(bf16[24,2880]{1,0:T(8,128)(2,1)S(1)} %get-tuple-element.178), channel_id=1, source_target_pairs={{0,6},{1,7},{2,4},{3,5},{4,2},{5,3},{6,0},{7,1},{8,14},{9,15},{10,... | collective-permute-start | bytes 414728 | tf_op jit(solution)/shard_map/ppermute | solution.py:591
  77.3 9.7 %collective-permute-start.24 = (bf16[24,2880]{1,0:T(8,128)(2,1)S(1)}, bf16[24,2880]{1,0:T(8,128)(2,1)S(1)}, u32[]{:S(2)}, u32[]{:S(2)}) collective-permute-start(bf16[24,2880]{1,0:T(8,128)(2,1)S(1)} %get-tuple-element.179), channel_id=1, source_target_pairs={{0,2},{1,3},{2,0},{3,1},{4,6},{5,7},{6,4},{7,5},{8,10},{9,11},{10,... | collective-permute-start | bytes 414728 | tf_op jit(solution)/shard_map/ppermute | solution.py:591

commit v5 on v4

--- a/solution.py
+++ b/solution.py
@@ -348,16 +348,17 @@
         at += width
 
 
-def attend_kernel(*refs):
+def attend_kernel(ways, accept, *refs):
     me, lens = refs[0][0], refs[1][0]
     arrived = refs[2:6]
     cos, sin, bias, pick, keys, values = refs[6:12]
-    outs, accepted_out = refs[12:16], refs[16]
-    blocks, queries, new_keys, new_values, attended, held = refs[17:]
+    outs, rest = refs[12 : 12 + len(ways)], list(refs[12 + len(ways) :])
+    accepted_out = rest.pop(0) if accept else None
+    blocks, queries, new_keys, new_values, held = rest
     draft = cos.shape[0]
     lanes = 2 * HEAD_DIM
+    columns = blocks.shape[2]
     for i in range(4):
-        columns = blocks.shape[2]
         blocks[me ^ (2 * i)] = arrived[i][:, :columns].astype(jnp.float32)
         blocks[me ^ (2 * i + 1)] = arrived[i][:, columns:].astype(jnp.float32)
     lane = iota((draft, lanes), 1)
@@ -375,62 +376,63 @@
 
     new_keys[...] = jnp.zeros_like(new_keys)
     new_values[...] = jnp.zeros_like(new_values)
-    q_cols = blocks.shape[2] - lanes
+    q_cols = columns - lanes
     heads = q_cols // HEAD_DIM
     count = heads * draft
-    groups = queries.shape[0] // count
-    pairs, both = groups // 2, 2 * count
-
-    def fill(pair):
-        new_keys[pair, :draft, :] = rope(blocks[pair, :, q_cols:])
-        new_values[pair, :draft, :] = blocks[groups // 2 + pair, :, q_cols:]
+    both = 2 * count
+    pairs = [(me // 2) ^ way for way in ways]
+
+    def columns_of(n):
+        return pl.ds(pl.multiple_of(pairs[n] * lanes, lanes), lanes)
+
+    def fill(n):
+        new_keys[n, :draft, :] = rope(blocks[pairs[n], :, q_cols:])
+        new_values[n, :draft, :] = blocks[4 + pairs[n], :, q_cols:]
         for p in range(2):
             for t in range(heads // 2):
-                tile = rope(blocks[2 * pair + p, :, t * lanes : (t + 1) * lanes]) * 0.125
+                tile = rope(blocks[2 * pairs[n] + p, :, t * lanes : (t + 1) * lanes]) * 0.125
                 turned = pltpu.roll(tile, HEAD_DIM, 1)
                 first, second = (tile, turned) if p == 0 else (turned, tile)
                 keep = left if p == 0 else ~left
-                at = (2 * pair + p) * count + 2 * t * draft
+                at = n * both + p * count + 2 * t * draft
                 queries[at : at + draft, :] = jnp.where(keep, first, 0.0)
                 queries[at + draft : at + 2 * draft, :] = jnp.where(keep, second, 0.0)
 
-    def columns_of(pair):
-        return slice(pair * lanes, (pair + 1) * lanes)
-
-    def asked(pair):
-        return queries[pair * both : (pair + 1) * both, :].astype(jnp.bfloat16)
+    def asked(n):
+        return queries[n * both : (n + 1) * both, :].astype(jnp.bfloat16)
 
     def tiles(block):
         return [block[:, i : i + lanes] for i in range(0, block.shape[1], lanes)]
 
-    def score(pair, at):
-        chunk = dot_nt(asked(pair), keys[at : at + step, columns_of(pair)])
+    def score(n, at):
+        chunk = dot_nt(asked(n), keys[at : at + step, columns_of(n)])
         chunk = chunk + live[:, at : at + step]
-        held[pair % 2, :, at : at + step] = chunk
+        held[n % 2, :, at : at + step] = chunk
         return functools.reduce(jnp.maximum, tiles(chunk))
 
-    def tree_score(pair):
-        fresh = dot_nt(asked(pair), new_keys[pair].astype(jnp.bfloat16))
+    def tree_score(n):
+        fresh = dot_nt(asked(n), new_keys[n].astype(jnp.bfloat16))
         return (fresh.reshape(2 * heads, draft, lanes) + mask[None]).reshape(fresh.shape)
 
     chunks = range(0, slots, step)
-    for pair in range(pairs):
-        fill(pair)
+    for n in range(len(ways)):
+        fill(n)
     fresh = tree_score(0)
     peak = functools.reduce(jnp.maximum, [fresh] + [score(0, at) for at in chunks])
-    for pair in range(pairs):
+    for n, out in enumerate(outs):
         top = jnp.max(peak, axis=1, keepdims=True)
         weights = jnp.exp(fresh - top)
         total = weights
-        mixed = dot_nn(weights.astype(jnp.bfloat16), new_values[pair].astype(jnp.bfloat16))
-        if pair + 1 < pairs:
-            fresh = peak = tree_score(pair + 1)
+        mixed = dot_nn(weights.astype(jnp.bfloat16), new_values[n].astype(jnp.bfloat16))
+        more = n + 1 < len(ways)
+        if more:
+            fresh = peak = tree_score(n + 1)
         for at in chunks:
-            if pair + 1 < pairs:
-                peak = jnp.maximum(peak, score(pair + 1, at))
-            weights = jnp.exp(held[pair % 2, :, at : at + step] - top)
+            if more:
+                peak = jnp.maximum(peak, score(n + 1, at))
+            weights = jnp.exp(held[n % 2, :, at : at + step] - top)
             total = total + functools.reduce(jnp.add, tiles(weights))
-            part = dot_nn(weights.astype(jnp.bfloat16), values[at : at + step, columns_of(pair)])
+            part = dot_nn(weights.astype(jnp.bfloat16), values[at : at + step, columns_of(n)])
             mixed = mixed + part
         mixed = mixed / jnp.sum(total, axis=1, keepdims=True)
         for p in range(2):
@@ -442,53 +444,77 @@
                 else:
                     tile = jnp.where(left, pltpu.roll(first, HEAD_DIM, 1), second)
                 col = p * q_cols + t * lanes
-                attended[pair, :, col : col + lanes] = tile
-    picked = pick[...].astype(jnp.bfloat16)
-    for pair in range(groups // 2):
-        for half, fresh in enumerate((new_keys, new_values)):
-            at = (half * (groups // 2) + pair) * lanes
-            rows = dot_nn(picked, fresh[pair].astype(jnp.bfloat16))
-            accepted_out[:, at : at + lanes] = rows.astype(jnp.bfloat16)
-    for i, out in enumerate(outs):
-        out[...] = attended[(me // 2) ^ i].astype(jnp.bfloat16)
-
-
-def named_slots(routes, expert, first, count):
+                out[:, col : col + lanes] = tile.astype(jnp.bfloat16)
+    if accept:
+        picked = pick[...].astype(jnp.bfloat16)
+        for pair in range(4):
+            new_keys[0, :draft, :] = rope(blocks[pair, :, q_cols:])
+            new_values[0, :draft, :] = blocks[4 + pair, :, q_cols:]
+            for half, fresh in enumerate((new_keys, new_values)):
+                at = (4 * half + pair) * lanes
+                rows = dot_nn(picked, fresh[0].astype(jnp.bfloat16))
+                accepted_out[:, at : at + lanes] = rows.astype(jnp.bfloat16)
+
+
+def slot_order(routes, expert):
     tokens = routes.shape[1]
     hits = jnp.max((routes[...] == expert).astype(jnp.float32), axis=0, keepdims=True)
     upper = (iota((tokens, tokens), 0) <= iota((tokens, tokens), 1)).astype(jnp.bfloat16)
     wide = jnp.broadcast_to(hits, (16, tokens)).astype(jnp.bfloat16)
-    order = dot_nn(wide, upper)[:1]
-    place = iota((count, tokens), 0).astype(jnp.float32) + (first + 1).astype(jnp.float32)
-    return jnp.where((order == place) & (hits > 0.5), 1.0, 0.0)
-
-
-def residual_kernel(*refs):
-    me, pieces, routes, out, rows = refs[0][0], refs[1:5], refs[5], refs[6], refs[7]
-    count = pieces[0].shape[0]
-    expert = me // 2
+    return dot_nn(wide, upper)[:1] * hits
+
+
+def slot_rows(order, first, count):
+    place = iota((count, order.shape[1]), 0).astype(jnp.float32) + (first + 1).astype(jnp.float32)
+    return jnp.where(order == place, 1.0, 0.0)
+
+
+def slots_kernel(*refs):
+    me, pieces, routes, rest = refs[0][0], refs[1:5], refs[5], refs[6:]
+    kept, given, table, home, named_out, rows = rest
+    core, expert = me % 2, me // 2
+    count, half = pieces[0].shape[0], kept.shape[0]
+    for i in range(4):
+        order = slot_order(routes, expert ^ i)
+        for side, first in enumerate((core * half, (1 - core) * half)):
+            at = (4 * side + i) * half
+            table[at : at + half, :] = slot_rows(order, first, half)
+        if i == 0:
+            chosen = slot_rows(order, expert * 0, 2 * half).astype(jnp.bfloat16)
+    home[...] = chosen
     rows[...] = jnp.zeros_like(rows)
     for i, piece in enumerate(pieces):
         at = pl.multiple_of((me ^ (2 * i)) * count, 8)
         rows[pl.ds(at, count), :] = piece[...].astype(jnp.float32)
-    chosen = named_slots(routes, expert, expert * 0, out.shape[0]).astype(jnp.bfloat16)
-    out[...] = dot_nn(chosen, rows[...].astype(jnp.bfloat16)).astype(jnp.bfloat16)
-
-
-def outproj_kernel(*refs):
-    me, pieces = refs[0][0], refs[1:9]
-    w_own, w_other, routes = refs[9:12]
-    own, sends = refs[12], refs[13:16]
-    rows, chosen = refs[16:]
+    found = rows[...].astype(jnp.bfloat16)
+    kept[...] = dot_nn(table[:half, :].astype(jnp.bfloat16), found).astype(jnp.bfloat16)
+    given[...] = dot_nn(table[4 * half : 5 * half, :].astype(jnp.bfloat16), found).astype(jnp.bfloat16)
+    experts, tokens = named_out.shape[1], routes.shape[1]
+    named = jnp.zeros((experts, tokens), jnp.float32)
+    for i in range(routes.shape[0]):
+        named = jnp.maximum(
+            named, (iota((experts, tokens), 0) == routes[i : i + 1, :]).astype(jnp.float32)
+        )
+    named_out[...] = dot_nt(chosen, named.astype(jnp.bfloat16))
+
+
+def pick_kernel(*refs):
+    me, pieces, (table, kept, given, rows) = refs[0][0], refs[1:5], refs[5:]
     count = pieces[0].shape[0]
-    half = own.shape[0]
-    core = me % 2
-    for k, piece in enumerate(pieces):
-        rows[pl.ds(pl.multiple_of((me ^ k) * count, 8), count), :] = piece[...].astype(jnp.float32)
-    for i in range(4):
-        chosen[i * half : (i + 1) * half, :] = named_slots(routes, (me // 2) ^ i, core * half, half)
-    picked = dot_nn(chosen[...].astype(jnp.bfloat16), rows[...].astype(jnp.bfloat16))
-    width = w_own.shape[1]
+    rows[...] = jnp.zeros_like(rows)
+    for i, piece in enumerate(pieces):
+        at = pl.multiple_of((me ^ (2 * i)) * count, 8)
+        rows[pl.ds(at, count), :] = piece[...].astype(jnp.float32)
+    picked = dot_nn(table[...].astype(jnp.bfloat16), rows[...].astype(jnp.bfloat16))
+    half = kept.shape[0]
+    kept[...] = picked[:half].astype(jnp.bfloat16)
+    given[...] = picked[half:].astype(jnp.bfloat16)
+
+
+def outproj_kernel(me_ref, kept, taken, w_own, w_other, own, *sends):
+    core = me_ref[0] % 2
+    half, width = own.shape[0], w_own.shape[1]
+    picked = kept[...].astype(jnp.float32) + taken[...].astype(jnp.float32)
     low, high = picked[:, :width], picked[:, width:]
     first = jnp.where(core == 0, low, high).astype(jnp.bfloat16)
     second = jnp.where(core == 0, high, low).astype(jnp.bfloat16)
@@ -511,28 +537,19 @@
     out[...] = dot_nt(first, w_own[...]) + dot_nt(second, w_other[...])
 
 
-def expert_kernel(me_ref, mine, theirs, kept, other, gain, *refs):
-    router, routes, w_gate, w_up, w_down, out, rows, active = refs
+def expert_kernel(me_ref, mine, theirs, gain, *refs):
+    router, named_ref, w_gate, w_up, w_down, out, rows, active = refs
     me = me_ref[0]
     core, expert = me % 2, me // 2
     half = mine.shape[0]
     rows[pl.ds(pl.multiple_of(core * half, 8), half), :] = mine[...].astype(jnp.float32)
     rows[pl.ds(pl.multiple_of((1 - core) * half, 8), half), :] = theirs[...].astype(jnp.float32)
-    floats = rows[...] + kept[...].astype(jnp.float32) + other[...].astype(jnp.float32)
-    floats = floats.astype(jnp.bfloat16).astype(jnp.float32)
+    floats = rows[...]
     mean_sq = jnp.mean(floats * floats, axis=-1, keepdims=True)
     scale = gain[...].reshape(1, gain.shape[0])
     inputs = (floats * lax.rsqrt(mean_sq + EPSILON) * scale).astype(jnp.bfloat16)
-    experts, tokens = router.shape[0], routes.shape[1]
-    logits = dot_nt(inputs, router[...])
-    chosen = named_slots(routes, expert, expert * 0, 2 * half).astype(jnp.bfloat16)
-    named = jnp.zeros((experts, tokens), jnp.float32)
-    for i in range(routes.shape[0]):
-        named = jnp.maximum(
-            named, (iota((experts, tokens), 0) == routes[i : i + 1, :]).astype(jnp.float32)
-        )
-    named = dot_nt(chosen, named.astype(jnp.bfloat16)) > 0.5
-    logits = jnp.where(named, logits, NEGATIVE)
+    named = named_ref[...] > 0.5
+    logits = jnp.where(named, dot_nt(inputs, router[...]), NEGATIVE)
     odds = jnp.exp(logits - jnp.max(logits, axis=1, keepdims=True))
     here = named & (iota(logits.shape, 1) == expert)
     share = jnp.sum(jnp.where(here, odds, 0.0), axis=1, keepdims=True)
@@ -544,14 +561,12 @@
     out[...] = (dot_nn(active[...], w_down[...]) * share).astype(jnp.bfloat16)
 
 
-def combine_kernel(*refs):
-    me, mine, theirs, routes, sums, hidden = refs[0][0], *refs[1:6]
-    own, sends, rows = refs[6], refs[7:10], refs[10]
+def combine_kernel(me_ref, mine, theirs, home, sums, hidden, own, *refs):
+    sends, rows = refs[:3], refs[3]
+    me = me_ref[0]
     count = hidden.shape[0]
     total = (mine[...].astype(jnp.float32) + theirs[...].astype(jnp.float32)).astype(jnp.bfloat16)
-    expert = me // 2
-    chosen = named_slots(routes, expert, expert * 0, total.shape[0]).astype(jnp.bfloat16)
-    rows[...] = dot_tn(chosen, total)
+    rows[...] = dot_tn(home[...], total)
 
     def of(i):
         start = pl.multiple_of((me ^ (2 * i)) * count, 8)
@@ -584,8 +599,8 @@
     me = lax.axis_index("tp").astype(jnp.int32).reshape(1)
     bf16, f32 = jnp.bfloat16, jnp.float32
 
-    def spread(blocks):
-        return [blocks[0], *(swap(blocks[i], 2 * i) for i in (2, 3, 1))]
+    def spread(blocks, order):
+        return [blocks[0], *(swap(blocks[i], 2 * i) for i in order)]
 
     def swap(values, offset):
         return lax.ppermute(values, "tp", [(i, i ^ offset) for i in range(devices)])
@@ -628,7 +643,7 @@
     later = (line, w_out, cache_keys[0], cache_values[0], cache_lens)
     later, projected = lax.optimization_barrier((later, projected))
     line, w_pair, keys, values, lens = later
-    arrived = spread(projected)
+    arrived = spread(projected, (2, 1, 3))
     tree = run(
         tree_kernel,
         [((draft, lanes), f32), ((draft, lanes), f32), ((draft, lanes), f32), ((DEPTH, lanes), f32)],
@@ -638,61 +653,82 @@
     )
     w_other = swap(w_pair, 1)
     cached = load(keys, values)
-    arrived, tree, cached = lax.optimization_barrier((arrived, tree, cached))
-    arrived = [arrived[i] for i in (0, 3, 1, 2)]
-    slots, kv_cols = cache_keys.shape[1:]
-    attended = run(
-        attend_kernel,
-        [((rows, 2 * queries), bf16)] * 4 + [((DEPTH, 2 * kv_cols), bf16)],
-        [me, cache_lens, *arrived, *tree, near(cached[0]), near(cached[1])],
-        scalars=2,
-        scratch=[
-            pltpu.VMEM((devices, rows, columns), f32),
-            pltpu.VMEM((rows * HEADS, lanes), f32),
-            pltpu.VMEM((devices // 2, lanes, lanes), f32),
-            pltpu.VMEM((devices // 2, lanes, lanes), f32),
-            pltpu.VMEM((devices // 2, rows, 2 * queries), f32),
-            pltpu.VMEM((2, rows * queries * 2 // HEAD_DIM, slots), f32),
+    slotted = run(
+        slots_kernel,
+        [
+            ((half, width), bf16),
+            ((half, width), bf16),
+            ((8 * half, tokens), f32),
+            ((capacity, tokens), bf16),
+            ((capacity, w_router.shape[1]), f32),
         ],
-        limit=16 * MIB,
-        flops=4 * rows * HEADS * slots * HEAD_DIM,
-        moved=4 * slots * kv_cols,
-    )
-    accepted_kv = attended[4][None]
-    later = (w_out, w_other, me)
-    (w_own, w_other, me_now), attended = lax.optimization_barrier((later, attended))
-    straight = spread(attended)
-    near_out = load(w_own.T, w_other.T)
-    residual = run(
-        residual_kernel,
-        [((capacity, width), bf16)],
-        [me_now, *line, routes_t],
+        [me, *line, routes_t],
         scratch=[pltpu.VMEM((tokens, width), f32)],
         limit=6 * MIB,
-        flops=2 * half * tokens * width,
+        flops=4 * half * tokens * width,
         moved=tokens * width * 4,
-    )[0]
-    own_crossed = swap(straight[0], 1)
-    shadow = (near_out, residual, own_crossed)
-    straight, (near_out, residual, own_crossed) = lax.optimization_barrier((straight, shadow))
+    )
+    shadow = (tree, cached, slotted)
+    arrived, shadow = lax.optimization_barrier((arrived, shadow))
+    tree, cached, (kept, given, table, home, named) = shadow
+    taken = swap(given, 1)
+    arrived = [arrived[i] for i in (0, 2, 1, 3)]
+    slots, kv_cols = cache_keys.shape[1:]
+    def attend(inputs, ways, accept):
+        outs = [((rows, 2 * queries), bf16)] * len(ways)
+        per_way = rows * queries * 2 // HEAD_DIM
+        return run(
+            functools.partial(attend_kernel, ways, accept),
+            outs + [((DEPTH, 2 * kv_cols), bf16)] * accept,
+            inputs,
+            scalars=2,
+            scratch=[
+                pltpu.VMEM((devices, rows, columns), f32),
+                pltpu.VMEM((len(ways) * per_way, lanes), f32),
+                pltpu.VMEM((len(ways), lanes, lanes), f32),
+                pltpu.VMEM((len(ways), lanes, lanes), f32),
+                pltpu.VMEM((min(len(ways), 2), per_way, slots), f32),
+            ],
+            limit=16 * MIB,
+            flops=len(ways) * rows * HEADS * slots * HEAD_DIM,
+            moved=len(ways) * slots * kv_cols,
+        )
+
+    lengths = cache_lens
+    inputs = [me, lengths, *arrived, *tree, near(cached[0]), near(cached[1])]
+    attended = attend(inputs, (1, 2, 3), False)
+    later = (w_out, w_other, me, lengths)
+    later, attended, taken = lax.optimization_barrier((later, attended, taken))
+    w_own, w_other, me_now, lengths = later
+    inputs[:2] = [me_now, lengths]
+    own, accepted_kv = attend(inputs, (0,), True)
+    straight = spread([own, *attended], (2, 3, 1))
+    accepted_kv = accepted_kv[None]
+    near_out = load(w_own.T, w_other.T)
+    straight, near_out = lax.optimization_barrier((straight, near_out))
     straight = [straight[i] for i in (0, 3, 1, 2)]
-    crossed = [own_crossed, *(swap(block, 1) for block in straight[1:])]
-    blocks = [block for pair in zip(straight, crossed) for block in pair]
+    picked = run(
+        pick_kernel,
+        [((4 * half, 2 * queries), bf16)] * 2,
+        [me, *straight, table],
+        scratch=[pltpu.VMEM((tokens, 2 * queries), f32)],
+        limit=6 * MIB,
+        flops=16 * half * tokens * 2 * queries,
+        moved=8 * half * 2 * queries * 2,
+    )
     out_flops = 2 * 4 * half * 2 * queries * width
     dispatched = run(
         outproj_kernel,
         [((half, width), f32)] + [((half, width), bf16)] * 3,
-        [me, *blocks, *map(near, near_out), routes_t],
-        scratch=[pltpu.VMEM((tokens, 2 * queries), f32), pltpu.VMEM((4 * half, tokens), f32)],
+        [me, picked[0], swap(picked[1], 1), *map(near, near_out)],
         limit=10 * MIB,
         flops=out_flops,
         moved=4 * queries * width,
     )
-    arrived = spread(dispatched)[1:]
-    (me_then, residual, experts), _ = lax.optimization_barrier(
-        ((me, residual, (w_gate, w_up, w_down)), dispatched[1])
-    )
-    residuals = (residual, swap(residual, 1))
+    arrived = spread(dispatched, (2, 3, 1))[1:]
+    (me_then, experts), _ = lax.optimization_barrier(
+        ((me, (w_gate, w_up, w_down)), dispatched[1])
+    )
     sums = run(
         token_kernel,
         [((4 * rows, width), f32)],
@@ -703,9 +739,10 @@
         moved=4 * queries * width,
     )[0]
     near_weights = load(*experts)
-    middle, arrived, sums, residuals, near_weights = lax.optimization_barrier(
-        (dispatched[0], arrived, sums, residuals, near_weights)
-    )
+    middle, arrived, sums, taken, near_weights = lax.optimization_barrier(
+        (dispatched[0], arrived, sums, taken, near_weights)
+    )
+    arrived = [kept, taken, *arrived]
     for block in arrived:
         middle = middle + block.astype(f32)
     middle = middle.astype(bf16)
@@ -716,10 +753,9 @@
             me,
             middle,
             swap(middle, 1),
-            *residuals,
             moe_gain,
             router_t,
-            routes_t,
+            named,
             *map(near, near_weights),
         ],
         scratch=[pltpu.VMEM((capacity, width), f32), pltpu.VMEM((capacity, w_down.shape[0]), bf16)],
@@ -730,12 +766,12 @@
     combined = run(
         combine_kernel,
         [((rows, width), f32)] + [((rows, width), bf16)] * 3,
-        [me, expert_rows, swap(expert_rows, 1), routes_t, sums, hidden],
+        [me, expert_rows, swap(expert_rows, 1), home, sums, hidden],
         scratch=[pltpu.VMEM((tokens, width), f32)],
         flops=2 * capacity * tokens * width,
         moved=tokens * width * 4,
     )
-    layer_out, *arrived = spread(combined)
+    layer_out, *arrived = spread(combined, (2, 3, 1))
     for block in arrived:
         layer_out = layer_out + block.astype(f32)
     return (layer_out.astype(bf16), accepted_kv)

time: 87.9 us -> 87.1 us (level)
  waiting for transfers between devices: 25 us -> 22.6 us
  Pallas kernels: 35.6 us -> 36.5 us
    ppermute x25 -> x22, waiting for transfers between devices: 25 us -> 22.6 us  [swap(): return lax.ppermute(values, 'tp', [(i, i ^ offset) for i in range(devices)])]
    pallas_call x8 -> x10, Pallas kernels: 20.4 us -> 21.3 us  [run(): pl.pallas_call(kernel, out_shape=tuple((jax.ShapeDtypeStruct(s, t) for s,...]
    ppermute x25 -> x22, starting transfers between devices: 24.1 us -> 24.7 us  [swap(): return lax.ppermute(values, 'tp', [(i, i ^ offset) for i in range(devices)])]
  transfers between devices with their start and end apart: 25 -> 22, of which waited for: 12 -> 8; matrix products, arithmetic and copies ran while one was open for 0% -> 0% of each run, Pallas kernels for 28% -> 29%
where the time goes in v5:
time: 87.1 us; the launch traced here: 86.9 us
  Pallas kernels  36.5 us (42%)
  starting transfers between devices  24.7 us (28%)
  waiting for transfers between devices  22.6 us (26%)
  between operations  2.19 us (3%)
    ppermute x22, starting transfers between devices, swap(): return lax.ppermute(values, 'tp', [(i, i ^ offset) for i in range(devices)])  24.7 us
    ppermute x22, waiting for transfers between devices, swap(): return lax.ppermute(values, 'tp', [(i, i ^ offset) for i in range(devices)])  22.6 us
    pallas_call x10, Pallas kernels, run(): pl.pallas_call(kernel, out_shape=tuple((jax.ShapeDtypeStruct(s, t) for s,...  21.3 us
    pallas_call x4, Pallas kernels, load(): pl.pallas_call(kernel, out_shape=tuple((pltpu.VMEM(a.shape, a.dtype) for...  15.3 us
  transfers between devices with their start and end apart: 22, of which 8 were waited for; matrix products, arithmetic and copies ran while one was open for 0% of the time, Pallas kernels for 29%

profile of v5, /device:TPU:0, one launch (start us, length us, event | category | flops | bytes accessed | tf_op | source)
XLA Modules:
  0.0 86.9 jit_solution(14503391294138894092)
XLA Ops:
  1.3 4.0 %collective-permute-start.2 = (bf16[24,2880]{1,0:T(8,128)(2,1)}, bf16[24,2880]{1,0:T(8,128)(2,1)S(1)}, u32[]{:S(2)}, u32[]{:S(2)}) collective-permute-start(bf16[24,2880]{1,0:T(8,128)(2,1)} %hidden.1), channel_id=1, source_target_pairs={{0,4},{1,5},{2,6},{3,7},{4,0},{5,1},{6,2},{7,3},{8,12},{9,13},{10,... | collective-permute-start | bytes 414728 | tf_op jit(solution)/shard_map/ppermute | solution.py:606
  5.3 1.3 %collective-permute-start.1 = (bf16[24,2880]{1,0:T(8,128)(2,1)}, bf16[24,2880]{1,0:T(8,128)(2,1)S(1)}, u32[]{:S(2)}, u32[]{:S(2)}) collective-permute-start(bf16[24,2880]{1,0:T(8,128)(2,1)} %hidden.1), channel_id=1, source_target_pairs={{0,6},{1,7},{2,4},{3,5},{4,2},{5,3},{6,0},{7,1},{8,14},{9,15},{10,... | collective-permute-start | bytes 414728 | tf_op jit(solution)/shard_map/ppermute | solution.py:606
  6.9 2.0 %shard_map.167 = (bf16[2880,512]{1,0:T(8,128)(2,1)S(1)}, bf16[2880,128]{1,0:T(8,128)(2,1)S(1)}) custom-call(bf16[2880,512]{1,0:T(8,128)(2,1)} %refs_0_.1, bf16[2880,128]{1,0:T(8,128)(2,1)} %refs_1_.2), custom_call_target="tpu_custom_call" | custom-call | bytes 7372800 | tf_op jit(solution)/shard_map/pallas_call | solution.py:273
  8.9 7.2 %collective-permute-done.2.refs_2_.refs_3_ = bf16[24,2880]{1,0:T(8,128)(2,1)S(1)} collective-permute-done((bf16[24,2880]{1,0:T(8,128)(2,1)}, bf16[24,2880]{1,0:T(8,128)(2,1)S(1)}, u32[]{:S(2)}, u32[]{:S(2)}) %collective-permute-start.2) | collective-permute-done | bytes 138272 | tf_op jit(solution)/shard_map/ppermute | solution.py:606
  16.1 0.8 collective-permute-done.refs_1_.refs_2_
  16.9 1.6 %shard_map.168 = (bf16[24,1280]{1,0:T(8,128)(2,1)S(1)}, bf16[24,1280]{1,0:T(8,128)(2,1)S(1)}, bf16[24,1280]{1,0:T(8,128)(2,1)S(1)}, bf16[24,1280]{1,0:T(8,128)(2,1)S(1)}) custom-call(bf16[24,2880]{1,0:T(8,128)(2,1)S(1)} %copy-done, bf16[24,2880]{1,0:T(8,128)(2,1)S(1)} %collective-permute-done.refs_1_.refs_2_, ...), custom_call_target="tpu_custom_call" | custom-call | flops 707788800 | bytes 3686400 | tf_op jit(solution)/shard_map/pallas_call | solution.py:240
  18.6 4.4 %collective-permute-start.6 = (bf16[24,1280]{1,0:T(8,128)(2,1)S(1)}, bf16[24,1280]{1,0:T(8,128)(2,1)S(1)}, u32[]{:S(2)}, u32[]{:S(2)}) collective-permute-start(bf16[24,1280]{1,0:T(8,128)(2,1)S(1)} %get-tuple-element.114), channel_id=1, source_target_pairs={{0,4},{1,5},{2,6},{3,7},{4,0},{5,1},{6,2},{7,3},{8,12},{9,13},{10,... | collective-permute-start | bytes 184328 | tf_op jit(solution)/shard_map/ppermute | solution.py:606
  23.0 1.5 %collective-permute-start.8 = (bf16[24,1280]{1,0:T(8,128)(2,1)S(1)}, bf16[24,1280]{1,0:T(8,128)(2,1)S(1)}, u32[]{:S(2)}, u32[]{:S(2)}) collective-permute-start(bf16[24,1280]{1,0:T(8,128)(2,1)S(1)} %get-tuple-element.116), channel_id=1, source_target_pairs={{0,6},{1,7},{2,4},{3,5},{4,2},{5,3},{6,0},{7,1},{8,14},{9,15},{10,... | collective-permute-start | bytes 184328 | tf_op jit(solution)/shard_map/ppermute | solution.py:606
  25.9 0.7 shard_map.169
  26.6 2.2 %shard_map.170 = (bf16[2048,512]{1,0:T(8,128)(2,1)S(1)}, bf16[2048,512]{1,0:T(8,128)(2,1)S(1)}) custom-call(bf16[2048,512]{1,0:T(8,128)(2,1)} %bitcast.10, bf16[2048,512]{1,0:T(8,128)(2,1)} %bitcast.11), custom_call_target="tpu_custom_call" | custom-call | bytes 8388608 | tf_op jit(solution)/shard_map/pallas_call | solution.py:273
  28.8 0.9 shard_map.171
  29.8 4.1 %shard_map.172 = (bf16[24,1024]{1,0:T(8,128)(2,1)S(1)}, bf16[24,1024]{1,0:T(8,128)(2,1)S(1)}, bf16[24,1024]{1,0:T(8,128)(2,1)S(1)}) custom-call(s32[1]{0:T(128)} %bitcast.refs_0_.me_ref, s32[1]{0:T(128)S(6)} %copy.18.lens.refs_1_, bf16[24,1280]{1,0:T(8,128)(2,1)S(1)} %get-tuple-element.136.refs_2_, bf16[24,1280]{1,0:T(8,128)(2,1)S(1)} %collective-permute-done.7.refs_3_, ...), custom_call_target="tpu_custom_call" | custom-call | flops 603979776 | bytes 3145728 | tf_op jit(solution)/shard_map/pallas_call | solution.py:240
  33.9 2.2 %collective-permute-start.10 = (bf16[24,1024]{1,0:T(8,128)(2,1)S(1)}, bf16[24,1024]{1,0:T(8,128)(2,1)S(1)}, u32[]{:S(2)}, u32[]{:S(2)}) collective-permute-start(bf16[24,1024]{1,0:T(8,128)(2,1)S(1)} %get-tuple-element.153), channel_id=1, source_target_pairs={{0,4},{1,5},{2,6},{3,7},{4,0},{5,1},{6,2},{7,3},{8,12},{9,13},{10,... | collective-permute-start | bytes 147464 | tf_op jit(solution)/shard_map/ppermute | solution.py:606
  36.1 0.8 collective-permute-start.11
  36.8 0.6 collective-permute-start.12
  37.5 2.7 %shard_map.174 = (bf16[2880,512]{1,0:T(8,128)(2,1)S(1)}, bf16[2880,512]{1,0:T(8,128)(2,1)S(1)}) custom-call(bf16[2880,512]{1,0:T(8,128)(2,1)} %bitcast.4.refs_0_, bf16[2880,512]{1,0:T(8,128)(2,1)} %bitcast.5.refs_1_), custom_call_target="tpu_custom_call" | custom-call | bytes 11796480 | tf_op jit(solution)/shard_map/pallas_call | solution.py:273
  40.2 2.5 %shard_map.173 = (bf16[24,1024]{1,0:T(8,128)(2,1)S(1)}, bf16[8,1024]{1,0:T(8,128)(2,1)}) custom-call(s32[1]{0:T(128)} %bitcast.refs_0_.me_ref, s32[1]{0:T(128)S(6)} %copy.18.lens.refs_1_, bf16[24,1280]{1,0:T(8,128)(2,1)S(1)} %get-tuple-element.136.refs_2_, bf16[24,1280]{1,0:T(8,128)(2,1)S(1)} %collective-permute-done.7.refs_3_, ...), custom_call_target="tpu_custom_call" | custom-call | flops 201326592 | bytes 1048576 | tf_op jit(solution)/shard_map/pallas_call | solution.py:240
  43.2 1.4 %collective-permute-done.13.taken = bf16[96,1024]{1,0:T(8,128)(2,1)S(1)} collective-permute-done((bf16[96,1024]{1,0:T(8,128)(2,1)S(1)}, bf16[96,1024]{1,0:T(8,128)(2,1)S(1)}, u32[]{:S(2)}, u32[]{:S(2)}) %collective-permute-start.13) | collective-permute-done | bytes 196640 | tf_op jit(solution)/shard_map/ppermute | solution.py:606
  44.6 1.9 %shard_map.176 = (f32[24,2880]{1,0:T(8,128)S(1)}, bf16[24,2880]{1,0:T(8,128)(2,1)S(1)}, bf16[24,2880]{1,0:T(8,128)(2,1)S(1)}, bf16[24,2880]{1,0:T(8,128)(2,1)S(1)}) custom-call(s32[1]{0:T(128)} %bitcast.refs_0_.me_ref, bf16[96,1024]{1,0:T(8,128)(2,1)S(1)} %get-tuple-element.165.kept, bf16[96,1024]{1,0:T(8,128)(2,1)S(1)} %collective-permute-done.13.taken, ...), custom_call_target="tpu_custom_call" | custom-call | flops 566231040 | bytes 5898240 | tf_op jit(solution)/shard_map/pallas_call | solution.py:240
  46.5 3.0 %collective-permute-start.14 = (bf16[24,2880]{1,0:T(8,128)(2,1)S(1)}, bf16[24,2880]{1,0:T(8,128)(2,1)S(1)}, u32[]{:S(2)}, u32[]{:S(2)}) collective-permute-start(bf16[24,2880]{1,0:T(8,128)(2,1)S(1)} %get-tuple-element.170), channel_id=1, source_target_pairs={{0,4},{1,5},{2,6},{3,7},{4,0},{5,1},{6,2},{7,3},{8,12},{9,13},{10,... | collective-permute-start | bytes 414728 | tf_op jit(solution)/shard_map/ppermute | solution.py:606
  49.5 0.8 collective-permute-start.15
  50.3 8.3 %shard_map.178 = (bf16[1440,2880]{1,0:T(8,128)(2,1)S(1)}, bf16[1440,2880]{1,0:T(8,128)(2,1)S(1)}, bf16[1440,2880]{1,0:T(8,128)(2,1)S(1)}) custom-call(bf16[1440,2880]{1,0:T(8,128)(2,1)} %refs_0_.3, bf16[1440,2880]{1,0:T(8,128)(2,1)} %refs_1_.4, bf16[1440,2880]{1,0:T(8,128)(2,1)} %refs_2_), custom_call_target="tpu_custom_call" | custom-call | bytes 49766400 | tf_op jit(solution)/shard_map/pallas_call | solution.py:273
  58.6 1.9 %shard_map.177.sums = f32[96,2880]{1,0:T(8,128)S(1)} custom-call(s32[1]{0:T(128)} %bitcast.refs_0_.me_ref, bf16[24,1024]{1,0:T(8,128)(2,1)S(1)} %get-tuple-element.160.refs_1_, bf16[24,1024]{1,0:T(8,128)(2,1)S(1)} %collective-permute-done.12.refs_2_, bf16[24,1024]{1,0:T(8,128)(2,1)S(1)} %collective-permute-done.10.refs_3_, ...), custom_call_target="tpu_custom_call" | custom-call | flops 566231040 | bytes 5898240 | tf_op jit(solution)/shard_map/pallas_call | solution.py:240
  61.2 1.3 %collective-permute-done.17.theirs = bf16[24,2880]{1,0:T(8,128)(2,1)S(1)} collective-permute-done((bf16[24,2880]{1,0:T(8,128)(2,1)S(1)}, bf16[24,2880]{1,0:T(8,128)(2,1)S(1)}, u32[]{:S(2)}, u32[]{:S(2)}) %collective-permute-start.17) | collective-permute-done | bytes 138272 | tf_op jit(solution)/shard_map/ppermute | solution.py:606
  62.5 6.7 %shard_map.179.mine = bf16[48,2880]{1,0:T(8,128)(2,1)S(1)} custom-call(s32[1]{0:T(128)} %bitcast.refs_0_.me_ref, bf16[24,2880]{1,0:T(8,128)(2,1)S(1)} %add_convert_fusion.1.mine, bf16[24,2880]{1,0:T(8,128)(2,1)S(1)} %collective-permute-done.17.theirs, f32[2880]{0:T(1024)S(1)} %copy-done.3, bf16[32,2880]{1,0:T(8,128)(2,1)S(1)} %bitcast.8, ...), custom_call_target="tpu_custom_call" | custom-call | flops 1194393600 | bytes 24883200 | tf_op jit(solution)/shard_map/pallas_call | solution.py:240
  69.4 1.4 %collective-permute-done.18.theirs = bf16[48,2880]{1,0:T(8,128)(2,1)S(1)} collective-permute-done((bf16[48,2880]{1,0:T(8,128)(2,1)S(1)}, bf16[48,2880]{1,0:T(8,128)(2,1)S(1)}, u32[]{:S(2)}, u32[]{:S(2)}) %collective-permute-start.18) | collective-permute-done | bytes 276512 | tf_op jit(solution)/shard_map/ppermute | solution.py:606
  70.9 0.6 shard_map.180
  71.5 3.2 %collective-permute-start.19 = (bf16[24,2880]{1,0:T(8,128)(2,1)S(1)}, bf16[24,2880]{1,0:T(8,128)(2,1)S(1)}, u32[]{:S(2)}, u32[]{:S(2)}) collective-permute-start(bf16[24,2880]{1,0:T(8,128)(2,1)S(1)} %get-tuple-element.194), channel_id=1, source_target_pairs={{0,4},{1,5},{2,6},{3,7},{4,0},{5,1},{6,2},{7,3},{8,12},{9,13},{10,... | collective-permute-start | bytes 414728 | tf_op jit(solution)/shard_map/ppermute | solution.py:606
  74.7 1.5 %collective-permute-start.20 = (bf16[24,2880]{1,0:T(8,128)(2,1)S(1)}, bf16[24,2880]{1,0:T(8,128)(2,1)S(1)}, u32[]{:S(2)}, u32[]{:S(2)}) collective-permute-start(bf16[24,2880]{1,0:T(8,128)(2,1)S(1)} %get-tuple-element.195), channel_id=1, source_target_pairs={{0,6},{1,7},{2,4},{3,5},{4,2},{5,3},{6,0},{7,1},{8,14},{9,15},{10,... | collective-permute-start | bytes 414728 | tf_op jit(solution)/shard_map/ppermute | solution.py:606
  76.2 9.1 %collective-permute-done.19 = bf16[24,2880]{1,0:T(8,128)(2,1)S(1)} collective-permute-done((bf16[24,2880]{1,0:T(8,128)(2,1)S(1)}, bf16[24,2880]{1,0:T(8,128)(2,1)S(1)}, u32[]{:S(2)}, u32[]{:S(2)}) %collective-permute-start.19) | collective-permute-done | bytes 138272 | tf_op jit(solution)/shard_map/ppermute | solution.py:606
  85.4 0.8 collective-permute-done.21
  86.2 0.7 add_convert_fusion
  (41 shorter events, 2.3 us)
Async XLA Ops:
  0.6 16.2 %copy-start = (bf16[24,2880]{1,0:T(8,128)(2,1)S(1)}, bf16[24,2880]{1,0:T(8,128)(2,1)}, u32[]{:S(2)}) copy-start(bf16[24,2880]{1,0:T(8,128)(2,1)} %hidden.1) | copy-start | bytes 414724
  0.6 8.2 %copy-start.5 = (s32[1,24]{1,0:T(1,128)S(1)}, s32[1,24]{1,0:T(1,128)}, u32[]{:S(2)}) copy-start(s32[1,24]{1,0:T(1,128)} %param.24) | copy-start | bytes 292
  0.7 16.2 %copy-start.2 = (f32[2880]{0:T(1024)S(1)}, f32[2880]{0:T(1024)}, u32[]{:S(2)}) copy-start(f32[2880]{0:T(1024)} %refs_4_.1) | copy-start | bytes 34564
  0.7 16.2 %collective-permute-start.3 = (bf16[2880,512]{1,0:T(8,128)(2,1)}, bf16[2880,512]{1,0:T(8,128)(2,1)S(1)}, u32[]{:S(2)}, u32[]{:S(2)}) collective-permute-start(bf16[2880,512]{1,0:T(8,128)(2,1)} %refs_0_.1), channel_id=1, source_target_pairs={{0,1},{1,0},{2,3},{3,2},{4,5},{5,4},{6,7},{7,6},{8,9},{9,8},{10,11... | collective-permute-start | bytes 8847368 | tf_op jit(solution)/shard_map/ppermute | solution.py:606
  1.2 15.7 %collective-permute-start.4 = (bf16[2880,128]{1,0:T(8,128)(2,1)}, bf16[2880,128]{1,0:T(8,128)(2,1)S(1)}, u32[]{:S(2)}, u32[]{:S(2)}) collective-permute-start(bf16[2880,128]{1,0:T(8,128)(2,1)} %refs_1_.2), channel_id=1, source_target_pairs={{0,1},{1,0},{2,3},{3,2},{4,5},{5,4},{6,7},{7,6},{8,9},{9,8},{10,11... | collective-permute-start | bytes 2211848 | tf_op jit(solution)/shard_map/ppermute | solution.py:606
  1.3 14.8 %collective-permute-start.2 = (bf16[24,2880]{1,0:T(8,128)(2,1)}, bf16[24,2880]{1,0:T(8,128)(2,1)S(1)}, u32[]{:S(2)}, u32[]{:S(2)}) collective-permute-start(bf16[24,2880]{1,0:T(8,128)(2,1)} %hidden.1), channel_id=1, source_target_pairs={{0,4},{1,5},{2,6},{3,7},{4,0},{5,1},{6,2},{7,3},{8,12},{9,13},{10,... | collective-permute-start | bytes 414728 | tf_op jit(solution)/shard_map/ppermute | solution.py:606
  5.3 10.8 %collective-permute-start.1 = (bf16[24,2880]{1,0:T(8,128)(2,1)}, bf16[24,2880]{1,0:T(8,128)(2,1)S(1)}, u32[]{:S(2)}, u32[]{:S(2)}) collective-permute-start(bf16[24,2880]{1,0:T(8,128)(2,1)} %hidden.1), channel_id=1, source_target_pairs={{0,6},{1,7},{2,4},{3,5},{4,2},{5,3},{6,0},{7,1},{8,14},{9,15},{10,... | collective-permute-start | bytes 414728 | tf_op jit(solution)/shard_map/ppermute | solution.py:606
  6.6 10.2 %collective-permute-start = (bf16[24,2880]{1,0:T(8,128)(2,1)}, bf16[24,2880]{1,0:T(8,128)(2,1)S(1)}, u32[]{:S(2)}, u32[]{:S(2)}) collective-permute-start(bf16[24,2880]{1,0:T(8,128)(2,1)} %hidden.1), channel_id=1, source_target_pairs={{0,2},{1,3},{2,0},{3,1},{4,6},{5,7},{6,4},{7,5},{8,10},{9,11},{10,... | collective-permute-start | bytes 414728 | tf_op jit(solution)/shard_map/ppermute | solution.py:606
  18.5 10.3 %copy-start.4 = (s32[192,4]{0,1:T(4,128)S(1)}, s32[192,4]{0,1:T(4,128)}, u32[]{:S(2)}) copy-start(s32[192,4]{0,1:T(4,128)} %param.28) | copy-start | bytes 9220
  18.5 15.4 %collective-permute-start.5 = (bf16[512,2880]{0,1:T(8,128)(2,1)}, bf16[512,2880]{0,1:T(8,128)(2,1)}, u32[]{:S(2)}, u32[]{:S(2)}) collective-permute-start(bf16[512,2880]{0,1:T(8,128)(2,1)} %param.20), channel_id=1, source_target_pairs={{0,1},{1,0},{2,3},{3,2},{4,5},{5,4},{6,7},{7,6},{8,9},{9,8},{10,11... | collective-permute-start | bytes 8847368 | tf_op jit(solution)/shard_map/ppermute | solution.py:606
  18.6 11.1 %collective-permute-start.6 = (bf16[24,1280]{1,0:T(8,128)(2,1)S(1)}, bf16[24,1280]{1,0:T(8,128)(2,1)S(1)}, u32[]{:S(2)}, u32[]{:S(2)}) collective-permute-start(bf16[24,1280]{1,0:T(8,128)(2,1)S(1)} %get-tuple-element.114), channel_id=1, source_target_pairs={{0,4},{1,5},{2,6},{3,7},{4,0},{5,1},{6,2},{7,3},{8,12},{9,13},{10,... | collective-permute-start | bytes 184328 | tf_op jit(solution)/shard_map/ppermute | solution.py:606
  23.0 6.7 %collective-permute-start.7 = (bf16[24,1280]{1,0:T(8,128)(2,1)S(1)}, bf16[24,1280]{1,0:T(8,128)(2,1)S(1)}, u32[]{:S(2)}, u32[]{:S(2)}) collective-permute-start(bf16[24,1280]{1,0:T(8,128)(2,1)S(1)} %get-tuple-element.115), channel_id=1, source_target_pairs={{0,2},{1,3},{2,0},{3,1},{4,6},{5,7},{6,4},{7,5},{8,10},{9,11},{10,... | collective-permute-start | bytes 184328 | tf_op jit(solution)/shard_map/ppermute | solution.py:606
  23.0 6.7 %collective-permute-start.8 = (bf16[24,1280]{1,0:T(8,128)(2,1)S(1)}, bf16[24,1280]{1,0:T(8,128)(2,1)S(1)}, u32[]{:S(2)}, u32[]{:S(2)}) collective-permute-start(bf16[24,1280]{1,0:T(8,128)(2,1)S(1)} %get-tuple-element.116), channel_id=1, source_target_pairs={{0,6},{1,7},{2,4},{3,5},{4,2},{5,3},{6,0},{7,1},{8,14},{9,15},{10,... | collective-permute-start | bytes 184328 | tf_op jit(solution)/shard_map/ppermute | solution.py:606
  29.7 4.2 %collective-permute-start.9 = (bf16[24,2880]{1,0:T(8,128)(2,1)S(1)}, bf16[24,2880]{1,0:T(8,128)(2,1)S(1)}, u32[]{:S(2)}, u32[]{:S(2)}) collective-permute-start(bf16[24,2880]{1,0:T(8,128)(2,1)S(1)} %get-tuple-element.149), channel_id=1, source_target_pairs={{0,1},{1,0},{2,3},{3,2},{4,5},{5,4},{6,7},{7,6},{8,9},{9,8},{10,11... | collective-permute-start | bytes 414728 | tf_op jit(solution)/shard_map/ppermute | solution.py:606
  33.9 8.8 %collective-permute-start.10 = (bf16[24,1024]{1,0:T(8,128)(2,1)S(1)}, bf16[24,1024]{1,0:T(8,128)(2,1)S(1)}, u32[]{:S(2)}, u32[]{:S(2)}) collective-permute-start(bf16[24,1024]{1,0:T(8,128)(2,1)S(1)} %get-tuple-element.153), channel_id=1, source_target_pairs={{0,4},{1,5},{2,6},{3,7},{4,0},{5,1},{6,2},{7,3},{8,12},{9,13},{10,... | collective-permute-start | bytes 147464 | tf_op jit(solution)/shard_map/ppermute | solution.py:606
  36.1 6.7 %collective-permute-start.11 = (bf16[24,1024]{1,0:T(8,128)(2,1)S(1)}, bf16[24,1024]{1,0:T(8,128)(2,1)S(1)}, u32[]{:S(2)}, u32[]{:S(2)}) collective-permute-start(bf16[24,1024]{1,0:T(8,128)(2,1)S(1)} %get-tuple-element.154), channel_id=1, source_target_pairs={{0,6},{1,7},{2,4},{3,5},{4,2},{5,3},{6,0},{7,1},{8,14},{9,15},{10,... | collective-permute-start | bytes 147464 | tf_op jit(solution)/shard_map/ppermute | solution.py:606
  36.8 5.9 %collective-permute-start.12 = (bf16[24,1024]{1,0:T(8,128)(2,1)S(1)}, bf16[24,1024]{1,0:T(8,128)(2,1)S(1)}, u32[]{:S(2)}, u32[]{:S(2)}) collective-permute-start(bf16[24,1024]{1,0:T(8,128)(2,1)S(1)} %get-tuple-element.155), channel_id=1, source_target_pairs={{0,2},{1,3},{2,0},{3,1},{4,6},{5,7},{6,4},{7,5},{8,10},{9,11},{10,... | collective-permute-start | bytes 147464 | tf_op jit(solution)/shard_map/ppermute | solution.py:606
  43.1 1.5 %collective-permute-start.13 = (bf16[96,1024]{1,0:T(8,128)(2,1)S(1)}, bf16[96,1024]{1,0:T(8,128)(2,1)S(1)}, u32[]{:S(2)}, u32[]{:S(2)}) collective-permute-start(bf16[96,1024]{1,0:T(8,128)(2,1)S(1)} %get-tuple-element.166), channel_id=1, source_target_pairs={{0,1},{1,0},{2,3},{3,2},{4,5},{5,4},{6,7},{7,6},{8,9},{9,8},{10,11... | collective-permute-start | bytes 589832 | tf_op jit(solution)/shard_map/ppermute | solution.py:606
  46.5 14.0 %collective-permute-start.14 = (bf16[24,2880]{1,0:T(8,128)(2,1)S(1)}, bf16[24,2880]{1,0:T(8,128)(2,1)S(1)}, u32[]{:S(2)}, u32[]{:S(2)}) collective-permute-start(bf16[24,2880]{1,0:T(8,128)(2,1)S(1)} %get-tuple-element.170), channel_id=1, source_target_pairs={{0,4},{1,5},{2,6},{3,7},{4,0},{5,1},{6,2},{7,3},{8,12},{9,13},{10,... | collective-permute-start | bytes 414728 | tf_op jit(solution)/shard_map/ppermute | solution.py:606
  49.5 11.0 %collective-permute-start.15 = (bf16[24,2880]{1,0:T(8,128)(2,1)S(1)}, bf16[24,2880]{1,0:T(8,128)(2,1)S(1)}, u32[]{:S(2)}, u32[]{:S(2)}) collective-permute-start(bf16[24,2880]{1,0:T(8,128)(2,1)S(1)} %get-tuple-element.171), channel_id=1, source_target_pairs={{0,6},{1,7},{2,4},{3,5},{4,2},{5,3},{6,0},{7,1},{8,14},{9,15},{10,... | collective-permute-start | bytes 414728 | tf_op jit(solution)/shard_map/ppermute | solution.py:606
  50.3 10.7 %collective-permute-start.16 = (bf16[24,2880]{1,0:T(8,128)(2,1)S(1)}, bf16[24,2880]{1,0:T(8,128)(2,1)S(1)}, u32[]{:S(2)}, u32[]{:S(2)}) collective-permute-start(bf16[24,2880]{1,0:T(8,128)(2,1)S(1)} %get-tuple-element.172), channel_id=1, source_target_pairs={{0,2},{1,3},{2,0},{3,1},{4,6},{5,7},{6,4},{7,5},{8,10},{9,11},{10,... | collective-permute-start | bytes 414728 | tf_op jit(solution)/shard_map/ppermute | solution.py:606
  58.6 3.9 %copy-start.1 = (bf16[2880,32]{0,1:T(8,128)(2,1)S(1)}, bf16[2880,32]{0,1:T(8,128)(2,1)}, u32[]{:S(2)}) copy-start(bf16[2880,32]{0,1:T(8,128)(2,1)} %param.27) | copy-start | bytes 552964
  58.6 3.9 %copy-start.3 = (f32[2880]{0:T(1024)S(1)}, f32[2880]{0:T(1024)}, u32[]{:S(2)}) copy-start(f32[2880]{0:T(1024)} %gain.1) | copy-start | bytes 34564
  61.1 1.4 %collective-permute-start.17 = (bf16[24,2880]{1,0:T(8,128)(2,1)S(1)}, bf16[24,2880]{1,0:T(8,128)(2,1)S(1)}, u32[]{:S(2)}, u32[]{:S(2)}) collective-permute-start(bf16[24,2880]{1,0:T(8,128)(2,1)S(1)} %add_convert_fusion.1.mine), channel_id=1, source_target_pairs={{0,1},{1,0},{2,3},{3,2},{4,5},{5,4},{6,7},{7,6},{8,9},{9,8},{10,11... | collective-permute-start | bytes 414728 | tf_op jit(solution)/shard_map/ppermute | solution.py:606
  69.2 1.6 %collective-permute-start.18 = (bf16[48,2880]{1,0:T(8,128)(2,1)S(1)}, bf16[48,2880]{1,0:T(8,128)(2,1)S(1)}, u32[]{:S(2)}, u32[]{:S(2)}) collective-permute-start(bf16[48,2880]{1,0:T(8,128)(2,1)S(1)} %shard_map.179.mine), channel_id=1, source_target_pairs={{0,1},{1,0},{2,3},{3,2},{4,5},{5,4},{6,7},{7,6},{8,9},{9,8},{10,11... | collective-permute-start | bytes 829448 | tf_op jit(solution)/shard_map/ppermute | solution.py:606
  71.5 13.8 %collective-permute-start.19 = (bf16[24,2880]{1,0:T(8,128)(2,1)S(1)}, bf16[24,2880]{1,0:T(8,128)(2,1)S(1)}, u32[]{:S(2)}, u32[]{:S(2)}) collective-permute-start(bf16[24,2880]{1,0:T(8,128)(2,1)S(1)} %get-tuple-element.194), channel_id=1, source_target_pairs={{0,4},{1,5},{2,6},{3,7},{4,0},{5,1},{6,2},{7,3},{8,12},{9,13},{10,... | collective-permute-start | bytes 414728 | tf_op jit(solution)/shard_map/ppermute | solution.py:606
  74.7 10.6 %collective-permute-start.20 = (bf16[24,2880]{1,0:T(8,128)(2,1)S(1)}, bf16[24,2880]{1,0:T(8,128)(2,1)S(1)}, u32[]{:S(2)}, u32[]{:S(2)}) collective-permute-start(bf16[24,2880]{1,0:T(8,128)(2,1)S(1)} %get-tuple-element.195), channel_id=1, source_target_pairs={{0,6},{1,7},{2,4},{3,5},{4,2},{5,3},{6,0},{7,1},{8,14},{9,15},{10,... | collective-permute-start | bytes 414728 | tf_op jit(solution)/shard_map/ppermute | solution.py:606
  76.2 10.0 %collective-permute-start.21 = (bf16[24,2880]{1,0:T(8,128)(2,1)S(1)}, bf16[24,2880]{1,0:T(8,128)(2,1)S(1)}, u32[]{:S(2)}, u32[]{:S(2)}) collective-permute-start(bf16[24,2880]{1,0:T(8,128)(2,1)S(1)} %get-tuple-element.196), channel_id=1, source_target_pairs={{0,2},{1,3},{2,0},{3,1},{4,6},{5,7},{6,4},{7,5},{8,10},{9,11},{10,... | collective-permute-start | bytes 414728 | tf_op jit(solution)/shard_map/ppermute | solution.py:606

commit v6 on v5

--- a/solution.py
+++ b/solution.py
@@ -353,7 +353,7 @@
     arrived = refs[2:6]
     cos, sin, bias, pick, keys, values = refs[6:12]
     outs, rest = refs[12 : 12 + len(ways)], list(refs[12 + len(ways) :])
-    accepted_out = rest.pop(0) if accept else None
+    accepted_out, fresh_rows = (rest.pop(0), rest.pop()) if accept else (None, None)
     blocks, queries, new_keys, new_values, held = rest
     draft = cos.shape[0]
     lanes = 2 * HEAD_DIM
@@ -446,14 +446,13 @@
                 col = p * q_cols + t * lanes
                 out[:, col : col + lanes] = tile.astype(jnp.bfloat16)
     if accept:
-        picked = pick[...].astype(jnp.bfloat16)
+        fresh_rows[...] = jnp.zeros_like(fresh_rows)
         for pair in range(4):
-            new_keys[0, :draft, :] = rope(blocks[pair, :, q_cols:])
-            new_values[0, :draft, :] = blocks[4 + pair, :, q_cols:]
-            for half, fresh in enumerate((new_keys, new_values)):
-                at = (4 * half + pair) * lanes
-                rows = dot_nn(picked, fresh[0].astype(jnp.bfloat16))
-                accepted_out[:, at : at + lanes] = rows.astype(jnp.bfloat16)
+            at = pair * lanes
+            fresh_rows[:draft, at : at + lanes] = rope(blocks[pair, :, q_cols:])
+            fresh_rows[:draft, 4 * lanes + at : 5 * lanes + at] = blocks[4 + pair, :, q_cols:]
+        rows = dot_nn(pick[...].astype(jnp.bfloat16), fresh_rows[...].astype(jnp.bfloat16))
+        accepted_out[...] = rows.astype(jnp.bfloat16)
 
 
 def slot_order(routes, expert):
@@ -688,6 +687,7 @@
                 pltpu.VMEM((len(ways), lanes, lanes), f32),
                 pltpu.VMEM((len(ways), lanes, lanes), f32),
                 pltpu.VMEM((min(len(ways), 2), per_way, slots), f32),
+                *([pltpu.VMEM((lanes, 2 * kv_cols), f32)] * accept),
             ],
             limit=16 * MIB,
             flops=len(ways) * rows * HEADS * slots * HEAD_DIM,

time: 87.1 us -> 87.1 us (level)
  no operation moved by 1% of the time
where the time goes in v6:
time: 87.1 us; the launch traced here: 86.9 us
  Pallas kernels  36.5 us (42%)
  starting transfers between devices  24.7 us (28%)
  waiting for transfers between devices  22.6 us (26%)
  between operations  2.19 us (3%)
    ppermute x22, starting transfers between devices, swap(): return lax.ppermute(values, 'tp', [(i, i ^ offset) for i in range(devices)])  24.7 us
    ppermute x22, waiting for transfers between devices, swap(): return lax.ppermute(values, 'tp', [(i, i ^ offset) for i in range(devices)])  22.6 us
    pallas_call x10, Pallas kernels, run(): pl.pallas_call(kernel, out_shape=tuple((jax.ShapeDtypeStruct(s, t) for s,...  21.2 us
    pallas_call x4, Pallas kernels, load(): pl.pallas_call(kernel, out_shape=tuple((pltpu.VMEM(a.shape, a.dtype) for...  15.3 us
  transfers between devices with their start and end apart: 22, of which 8 were waited for; matrix products, arithmetic and copies ran while one was open for 0% of the time, Pallas kernels for 29%

profile of v6, /device:TPU:0, one launch (start us, length us, event | category | flops | bytes accessed | tf_op | source)
XLA Modules:
  0.0 86.9 jit_solution(6152164353924901374)
XLA Ops:
  1.3 4.0 %collective-permute-start.2 = (bf16[24,2880]{1,0:T(8,128)(2,1)}, bf16[24,2880]{1,0:T(8,128)(2,1)S(1)}, u32[]{:S(2)}, u32[]{:S(2)}) collective-permute-start(bf16[24,2880]{1,0:T(8,128)(2,1)} %hidden.1), channel_id=1, source_target_pairs={{0,4},{1,5},{2,6},{3,7},{4,0},{5,1},{6,2},{7,3},{8,12},{9,13},{10,... | collective-permute-start | bytes 414728 | tf_op jit(solution)/shard_map/ppermute | solution.py:605
  5.3 1.3 %collective-permute-start.1 = (bf16[24,2880]{1,0:T(8,128)(2,1)}, bf16[24,2880]{1,0:T(8,128)(2,1)S(1)}, u32[]{:S(2)}, u32[]{:S(2)}) collective-permute-start(bf16[24,2880]{1,0:T(8,128)(2,1)} %hidden.1), channel_id=1, source_target_pairs={{0,6},{1,7},{2,4},{3,5},{4,2},{5,3},{6,0},{7,1},{8,14},{9,15},{10,... | collective-permute-start | bytes 414728 | tf_op jit(solution)/shard_map/ppermute | solution.py:605
  6.9 2.0 %shard_map.167 = (bf16[2880,512]{1,0:T(8,128)(2,1)S(1)}, bf16[2880,128]{1,0:T(8,128)(2,1)S(1)}) custom-call(bf16[2880,512]{1,0:T(8,128)(2,1)} %refs_0_.1, bf16[2880,128]{1,0:T(8,128)(2,1)} %refs_1_.2), custom_call_target="tpu_custom_call" | custom-call | bytes 7372800 | tf_op jit(solution)/shard_map/pallas_call | solution.py:273
  8.9 7.2 %collective-permute-done.2.refs_2_.refs_3_ = bf16[24,2880]{1,0:T(8,128)(2,1)S(1)} collective-permute-done((bf16[24,2880]{1,0:T(8,128)(2,1)}, bf16[24,2880]{1,0:T(8,128)(2,1)S(1)}, u32[]{:S(2)}, u32[]{:S(2)}) %collective-permute-start.2) | collective-permute-done | bytes 138272 | tf_op jit(solution)/shard_map/ppermute | solution.py:605
  16.1 0.8 collective-permute-done.refs_1_.refs_2_
  16.9 1.6 %shard_map.168 = (bf16[24,1280]{1,0:T(8,128)(2,1)S(1)}, bf16[24,1280]{1,0:T(8,128)(2,1)S(1)}, bf16[24,1280]{1,0:T(8,128)(2,1)S(1)}, bf16[24,1280]{1,0:T(8,128)(2,1)S(1)}) custom-call(bf16[24,2880]{1,0:T(8,128)(2,1)S(1)} %copy-done, bf16[24,2880]{1,0:T(8,128)(2,1)S(1)} %collective-permute-done.refs_1_.refs_2_, ...), custom_call_target="tpu_custom_call" | custom-call | flops 707788800 | bytes 3686400 | tf_op jit(solution)/shard_map/pallas_call | solution.py:240
  18.6 4.4 %collective-permute-start.6 = (bf16[24,1280]{1,0:T(8,128)(2,1)S(1)}, bf16[24,1280]{1,0:T(8,128)(2,1)S(1)}, u32[]{:S(2)}, u32[]{:S(2)}) collective-permute-start(bf16[24,1280]{1,0:T(8,128)(2,1)S(1)} %get-tuple-element.114), channel_id=1, source_target_pairs={{0,4},{1,5},{2,6},{3,7},{4,0},{5,1},{6,2},{7,3},{8,12},{9,13},{10,... | collective-permute-start | bytes 184328 | tf_op jit(solution)/shard_map/ppermute | solution.py:605
  23.0 1.5 %collective-permute-start.8 = (bf16[24,1280]{1,0:T(8,128)(2,1)S(1)}, bf16[24,1280]{1,0:T(8,128)(2,1)S(1)}, u32[]{:S(2)}, u32[]{:S(2)}) collective-permute-start(bf16[24,1280]{1,0:T(8,128)(2,1)S(1)} %get-tuple-element.116), channel_id=1, source_target_pairs={{0,6},{1,7},{2,4},{3,5},{4,2},{5,3},{6,0},{7,1},{8,14},{9,15},{10,... | collective-permute-start | bytes 184328 | tf_op jit(solution)/shard_map/ppermute | solution.py:605
  25.9 0.7 shard_map.169
  26.6 2.2 %shard_map.170 = (bf16[2048,512]{1,0:T(8,128)(2,1)S(1)}, bf16[2048,512]{1,0:T(8,128)(2,1)S(1)}) custom-call(bf16[2048,512]{1,0:T(8,128)(2,1)} %bitcast.10, bf16[2048,512]{1,0:T(8,128)(2,1)} %bitcast.11), custom_call_target="tpu_custom_call" | custom-call | bytes 8388608 | tf_op jit(solution)/shard_map/pallas_call | solution.py:273
  28.8 0.9 shard_map.171
  29.8 4.1 %shard_map.172 = (bf16[24,1024]{1,0:T(8,128)(2,1)S(1)}, bf16[24,1024]{1,0:T(8,128)(2,1)S(1)}, bf16[24,1024]{1,0:T(8,128)(2,1)S(1)}) custom-call(s32[1]{0:T(128)} %bitcast.refs_0_.me_ref, s32[1]{0:T(128)S(6)} %copy.18.lens.refs_1_, bf16[24,1280]{1,0:T(8,128)(2,1)S(1)} %get-tuple-element.136.refs_2_, bf16[24,1280]{1,0:T(8,128)(2,1)S(1)} %collective-permute-done.7.refs_3_, ...), custom_call_target="tpu_custom_call" | custom-call | flops 603979776 | bytes 3145728 | tf_op jit(solution)/shard_map/pallas_call | solution.py:240
  33.9 2.2 %collective-permute-start.10 = (bf16[24,1024]{1,0:T(8,128)(2,1)S(1)}, bf16[24,1024]{1,0:T(8,128)(2,1)S(1)}, u32[]{:S(2)}, u32[]{:S(2)}) collective-permute-start(bf16[24,1024]{1,0:T(8,128)(2,1)S(1)} %get-tuple-element.153), channel_id=1, source_target_pairs={{0,4},{1,5},{2,6},{3,7},{4,0},{5,1},{6,2},{7,3},{8,12},{9,13},{10,... | collective-permute-start | bytes 147464 | tf_op jit(solution)/shard_map/ppermute | solution.py:605
  36.1 0.8 collective-permute-start.11
  36.8 0.6 collective-permute-start.12
  37.5 2.7 %shard_map.174 = (bf16[2880,512]{1,0:T(8,128)(2,1)S(1)}, bf16[2880,512]{1,0:T(8,128)(2,1)S(1)}) custom-call(bf16[2880,512]{1,0:T(8,128)(2,1)} %bitcast.4.refs_0_, bf16[2880,512]{1,0:T(8,128)(2,1)} %bitcast.5.refs_1_), custom_call_target="tpu_custom_call" | custom-call | bytes 11796480 | tf_op jit(solution)/shard_map/pallas_call | solution.py:273
  40.2 2.5 %shard_map.173 = (bf16[24,1024]{1,0:T(8,128)(2,1)S(1)}, bf16[8,1024]{1,0:T(8,128)(2,1)}) custom-call(s32[1]{0:T(128)} %bitcast.refs_0_.me_ref, s32[1]{0:T(128)S(6)} %copy.18.lens.refs_1_, bf16[24,1280]{1,0:T(8,128)(2,1)S(1)} %get-tuple-element.136.refs_2_, bf16[24,1280]{1,0:T(8,128)(2,1)S(1)} %collective-permute-done.7.refs_3_, ...), custom_call_target="tpu_custom_call" | custom-call | flops 201326592 | bytes 1048576 | tf_op jit(solution)/shard_map/pallas_call | solution.py:240
  43.2 1.4 %collective-permute-done.13.taken = bf16[96,1024]{1,0:T(8,128)(2,1)S(1)} collective-permute-done((bf16[96,1024]{1,0:T(8,128)(2,1)S(1)}, bf16[96,1024]{1,0:T(8,128)(2,1)S(1)}, u32[]{:S(2)}, u32[]{:S(2)}) %collective-permute-start.13) | collective-permute-done | bytes 196640 | tf_op jit(solution)/shard_map/ppermute | solution.py:605
  44.6 1.9 %shard_map.176 = (f32[24,2880]{1,0:T(8,128)S(1)}, bf16[24,2880]{1,0:T(8,128)(2,1)S(1)}, bf16[24,2880]{1,0:T(8,128)(2,1)S(1)}, bf16[24,2880]{1,0:T(8,128)(2,1)S(1)}) custom-call(s32[1]{0:T(128)} %bitcast.refs_0_.me_ref, bf16[96,1024]{1,0:T(8,128)(2,1)S(1)} %get-tuple-element.165.kept, bf16[96,1024]{1,0:T(8,128)(2,1)S(1)} %collective-permute-done.13.taken, ...), custom_call_target="tpu_custom_call" | custom-call | flops 566231040 | bytes 5898240 | tf_op jit(solution)/shard_map/pallas_call | solution.py:240
  46.5 3.0 %collective-permute-start.14 = (bf16[24,2880]{1,0:T(8,128)(2,1)S(1)}, bf16[24,2880]{1,0:T(8,128)(2,1)S(1)}, u32[]{:S(2)}, u32[]{:S(2)}) collective-permute-start(bf16[24,2880]{1,0:T(8,128)(2,1)S(1)} %get-tuple-element.170), channel_id=1, source_target_pairs={{0,4},{1,5},{2,6},{3,7},{4,0},{5,1},{6,2},{7,3},{8,12},{9,13},{10,... | collective-permute-start | bytes 414728 | tf_op jit(solution)/shard_map/ppermute | solution.py:605
  49.5 0.8 collective-permute-start.15
  50.3 8.3 %shard_map.178 = (bf16[1440,2880]{1,0:T(8,128)(2,1)S(1)}, bf16[1440,2880]{1,0:T(8,128)(2,1)S(1)}, bf16[1440,2880]{1,0:T(8,128)(2,1)S(1)}) custom-call(bf16[1440,2880]{1,0:T(8,128)(2,1)} %refs_0_.3, bf16[1440,2880]{1,0:T(8,128)(2,1)} %refs_1_.4, bf16[1440,2880]{1,0:T(8,128)(2,1)} %refs_2_), custom_call_target="tpu_custom_call" | custom-call | bytes 49766400 | tf_op jit(solution)/shard_map/pallas_call | solution.py:273
  58.6 1.9 %shard_map.177.sums = f32[96,2880]{1,0:T(8,128)S(1)} custom-call(s32[1]{0:T(128)} %bitcast.refs_0_.me_ref, bf16[24,1024]{1,0:T(8,128)(2,1)S(1)} %get-tuple-element.160.refs_1_, bf16[24,1024]{1,0:T(8,128)(2,1)S(1)} %collective-permute-done.12.refs_2_, bf16[24,1024]{1,0:T(8,128)(2,1)S(1)} %collective-permute-done.10.refs_3_, ...), custom_call_target="tpu_custom_call" | custom-call | flops 566231040 | bytes 5898240 | tf_op jit(solution)/shard_map/pallas_call | solution.py:240
  61.2 1.3 %collective-permute-done.17.theirs = bf16[24,2880]{1,0:T(8,128)(2,1)S(1)} collective-permute-done((bf16[24,2880]{1,0:T(8,128)(2,1)S(1)}, bf16[24,2880]{1,0:T(8,128)(2,1)S(1)}, u32[]{:S(2)}, u32[]{:S(2)}) %collective-permute-start.17) | collective-permute-done | bytes 138272 | tf_op jit(solution)/shard_map/ppermute | solution.py:605
  62.5 6.7 %shard_map.179.mine = bf16[48,2880]{1,0:T(8,128)(2,1)S(1)} custom-call(s32[1]{0:T(128)} %bitcast.refs_0_.me_ref, bf16[24,2880]{1,0:T(8,128)(2,1)S(1)} %add_convert_fusion.1.mine, bf16[24,2880]{1,0:T(8,128)(2,1)S(1)} %collective-permute-done.17.theirs, f32[2880]{0:T(1024)S(1)} %copy-done.3, bf16[32,2880]{1,0:T(8,128)(2,1)S(1)} %bitcast.8, ...), custom_call_target="tpu_custom_call" | custom-call | flops 1194393600 | bytes 24883200 | tf_op jit(solution)/shard_map/pallas_call | solution.py:240
  69.4 1.4 %collective-permute-done.18.theirs = bf16[48,2880]{1,0:T(8,128)(2,1)S(1)} collective-permute-done((bf16[48,2880]{1,0:T(8,128)(2,1)S(1)}, bf16[48,2880]{1,0:T(8,128)(2,1)S(1)}, u32[]{:S(2)}, u32[]{:S(2)}) %collective-permute-start.18) | collective-permute-done | bytes 276512 | tf_op jit(solution)/shard_map/ppermute | solution.py:605
  70.8 0.6 shard_map.180
  71.5 3.2 %collective-permute-start.19 = (bf16[24,2880]{1,0:T(8,128)(2,1)S(1)}, bf16[24,2880]{1,0:T(8,128)(2,1)S(1)}, u32[]{:S(2)}, u32[]{:S(2)}) collective-permute-start(bf16[24,2880]{1,0:T(8,128)(2,1)S(1)} %get-tuple-element.194), channel_id=1, source_target_pairs={{0,4},{1,5},{2,6},{3,7},{4,0},{5,1},{6,2},{7,3},{8,12},{9,13},{10,... | collective-permute-start | bytes 414728 | tf_op jit(solution)/shard_map/ppermute | solution.py:605
  74.7 1.5 %collective-permute-start.20 = (bf16[24,2880]{1,0:T(8,128)(2,1)S(1)}, bf16[24,2880]{1,0:T(8,128)(2,1)S(1)}, u32[]{:S(2)}, u32[]{:S(2)}) collective-permute-start(bf16[24,2880]{1,0:T(8,128)(2,1)S(1)} %get-tuple-element.195), channel_id=1, source_target_pairs={{0,6},{1,7},{2,4},{3,5},{4,2},{5,3},{6,0},{7,1},{8,14},{9,15},{10,... | collective-permute-start | bytes 414728 | tf_op jit(solution)/shard_map/ppermute | solution.py:605
  76.2 9.1 %collective-permute-done.19 = bf16[24,2880]{1,0:T(8,128)(2,1)S(1)} collective-permute-done((bf16[24,2880]{1,0:T(8,128)(2,1)S(1)}, bf16[24,2880]{1,0:T(8,128)(2,1)S(1)}, u32[]{:S(2)}, u32[]{:S(2)}) %collective-permute-start.19) | collective-permute-done | bytes 138272 | tf_op jit(solution)/shard_map/ppermute | solution.py:605
  85.3 0.8 collective-permute-done.21
  86.2 0.7 add_convert_fusion
  (41 shorter events, 2.3 us)
Async XLA Ops:
  0.6 16.2 %copy-start = (bf16[24,2880]{1,0:T(8,128)(2,1)S(1)}, bf16[24,2880]{1,0:T(8,128)(2,1)}, u32[]{:S(2)}) copy-start(bf16[24,2880]{1,0:T(8,128)(2,1)} %hidden.1) | copy-start | bytes 414724
  0.6 8.2 %copy-start.5 = (s32[1,24]{1,0:T(1,128)S(1)}, s32[1,24]{1,0:T(1,128)}, u32[]{:S(2)}) copy-start(s32[1,24]{1,0:T(1,128)} %param.24) | copy-start | bytes 292
  0.7 16.2 %copy-start.2 = (f32[2880]{0:T(1024)S(1)}, f32[2880]{0:T(1024)}, u32[]{:S(2)}) copy-start(f32[2880]{0:T(1024)} %refs_4_.1) | copy-start | bytes 34564
  0.7 16.2 %collective-permute-start.3 = (bf16[2880,512]{1,0:T(8,128)(2,1)}, bf16[2880,512]{1,0:T(8,128)(2,1)S(1)}, u32[]{:S(2)}, u32[]{:S(2)}) collective-permute-start(bf16[2880,512]{1,0:T(8,128)(2,1)} %refs_0_.1), channel_id=1, source_target_pairs={{0,1},{1,0},{2,3},{3,2},{4,5},{5,4},{6,7},{7,6},{8,9},{9,8},{10,11... | collective-permute-start | bytes 8847368 | tf_op jit(solution)/shard_map/ppermute | solution.py:605
  1.2 15.7 %collective-permute-start.4 = (bf16[2880,128]{1,0:T(8,128)(2,1)}, bf16[2880,128]{1,0:T(8,128)(2,1)S(1)}, u32[]{:S(2)}, u32[]{:S(2)}) collective-permute-start(bf16[2880,128]{1,0:T(8,128)(2,1)} %refs_1_.2), channel_id=1, source_target_pairs={{0,1},{1,0},{2,3},{3,2},{4,5},{5,4},{6,7},{7,6},{8,9},{9,8},{10,11... | collective-permute-start | bytes 2211848 | tf_op jit(solution)/shard_map/ppermute | solution.py:605
  1.3 14.8 %collective-permute-start.2 = (bf16[24,2880]{1,0:T(8,128)(2,1)}, bf16[24,2880]{1,0:T(8,128)(2,1)S(1)}, u32[]{:S(2)}, u32[]{:S(2)}) collective-permute-start(bf16[24,2880]{1,0:T(8,128)(2,1)} %hidden.1), channel_id=1, source_target_pairs={{0,4},{1,5},{2,6},{3,7},{4,0},{5,1},{6,2},{7,3},{8,12},{9,13},{10,... | collective-permute-start | bytes 414728 | tf_op jit(solution)/shard_map/ppermute | solution.py:605
  5.3 10.8 %collective-permute-start.1 = (bf16[24,2880]{1,0:T(8,128)(2,1)}, bf16[24,2880]{1,0:T(8,128)(2,1)S(1)}, u32[]{:S(2)}, u32[]{:S(2)}) collective-permute-start(bf16[24,2880]{1,0:T(8,128)(2,1)} %hidden.1), channel_id=1, source_target_pairs={{0,6},{1,7},{2,4},{3,5},{4,2},{5,3},{6,0},{7,1},{8,14},{9,15},{10,... | collective-permute-start | bytes 414728 | tf_op jit(solution)/shard_map/ppermute | solution.py:605
  6.6 10.2 %collective-permute-start = (bf16[24,2880]{1,0:T(8,128)(2,1)}, bf16[24,2880]{1,0:T(8,128)(2,1)S(1)}, u32[]{:S(2)}, u32[]{:S(2)}) collective-permute-start(bf16[24,2880]{1,0:T(8,128)(2,1)} %hidden.1), channel_id=1, source_target_pairs={{0,2},{1,3},{2,0},{3,1},{4,6},{5,7},{6,4},{7,5},{8,10},{9,11},{10,... | collective-permute-start | bytes 414728 | tf_op jit(solution)/shard_map/ppermute | solution.py:605
  18.5 10.3 %copy-start.4 = (s32[192,4]{0,1:T(4,128)S(1)}, s32[192,4]{0,1:T(4,128)}, u32[]{:S(2)}) copy-start(s32[192,4]{0,1:T(4,128)} %param.28) | copy-start | bytes 9220
  18.5 15.4 %collective-permute-start.5 = (bf16[512,2880]{0,1:T(8,128)(2,1)}, bf16[512,2880]{0,1:T(8,128)(2,1)}, u32[]{:S(2)}, u32[]{:S(2)}) collective-permute-start(bf16[512,2880]{0,1:T(8,128)(2,1)} %param.20), channel_id=1, source_target_pairs={{0,1},{1,0},{2,3},{3,2},{4,5},{5,4},{6,7},{7,6},{8,9},{9,8},{10,11... | collective-permute-start | bytes 8847368 | tf_op jit(solution)/shard_map/ppermute | solution.py:605
  18.6 11.1 %collective-permute-start.6 = (bf16[24,1280]{1,0:T(8,128)(2,1)S(1)}, bf16[24,1280]{1,0:T(8,128)(2,1)S(1)}, u32[]{:S(2)}, u32[]{:S(2)}) collective-permute-start(bf16[24,1280]{1,0:T(8,128)(2,1)S(1)} %get-tuple-element.114), channel_id=1, source_target_pairs={{0,4},{1,5},{2,6},{3,7},{4,0},{5,1},{6,2},{7,3},{8,12},{9,13},{10,... | collective-permute-start | bytes 184328 | tf_op jit(solution)/shard_map/ppermute | solution.py:605
  23.0 6.7 %collective-permute-start.7 = (bf16[24,1280]{1,0:T(8,128)(2,1)S(1)}, bf16[24,1280]{1,0:T(8,128)(2,1)S(1)}, u32[]{:S(2)}, u32[]{:S(2)}) collective-permute-start(bf16[24,1280]{1,0:T(8,128)(2,1)S(1)} %get-tuple-element.115), channel_id=1, source_target_pairs={{0,2},{1,3},{2,0},{3,1},{4,6},{5,7},{6,4},{7,5},{8,10},{9,11},{10,... | collective-permute-start | bytes 184328 | tf_op jit(solution)/shard_map/ppermute | solution.py:605
  23.0 6.7 %collective-permute-start.8 = (bf16[24,1280]{1,0:T(8,128)(2,1)S(1)}, bf16[24,1280]{1,0:T(8,128)(2,1)S(1)}, u32[]{:S(2)}, u32[]{:S(2)}) collective-permute-start(bf16[24,1280]{1,0:T(8,128)(2,1)S(1)} %get-tuple-element.116), channel_id=1, source_target_pairs={{0,6},{1,7},{2,4},{3,5},{4,2},{5,3},{6,0},{7,1},{8,14},{9,15},{10,... | collective-permute-start | bytes 184328 | tf_op jit(solution)/shard_map/ppermute | solution.py:605
  29.7 4.2 %collective-permute-start.9 = (bf16[24,2880]{1,0:T(8,128)(2,1)S(1)}, bf16[24,2880]{1,0:T(8,128)(2,1)S(1)}, u32[]{:S(2)}, u32[]{:S(2)}) collective-permute-start(bf16[24,2880]{1,0:T(8,128)(2,1)S(1)} %get-tuple-element.149), channel_id=1, source_target_pairs={{0,1},{1,0},{2,3},{3,2},{4,5},{5,4},{6,7},{7,6},{8,9},{9,8},{10,11... | collective-permute-start | bytes 414728 | tf_op jit(solution)/shard_map/ppermute | solution.py:605
  33.9 8.8 %collective-permute-start.10 = (bf16[24,1024]{1,0:T(8,128)(2,1)S(1)}, bf16[24,1024]{1,0:T(8,128)(2,1)S(1)}, u32[]{:S(2)}, u32[]{:S(2)}) collective-permute-start(bf16[24,1024]{1,0:T(8,128)(2,1)S(1)} %get-tuple-element.153), channel_id=1, source_target_pairs={{0,4},{1,5},{2,6},{3,7},{4,0},{5,1},{6,2},{7,3},{8,12},{9,13},{10,... | collective-permute-start | bytes 147464 | tf_op jit(solution)/shard_map/ppermute | solution.py:605
  36.1 6.6 %collective-permute-start.11 = (bf16[24,1024]{1,0:T(8,128)(2,1)S(1)}, bf16[24,1024]{1,0:T(8,128)(2,1)S(1)}, u32[]{:S(2)}, u32[]{:S(2)}) collective-permute-start(bf16[24,1024]{1,0:T(8,128)(2,1)S(1)} %get-tuple-element.154), channel_id=1, source_target_pairs={{0,6},{1,7},{2,4},{3,5},{4,2},{5,3},{6,0},{7,1},{8,14},{9,15},{10,... | collective-permute-start | bytes 147464 | tf_op jit(solution)/shard_map/ppermute | solution.py:605
  36.8 5.9 %collective-permute-start.12 = (bf16[24,1024]{1,0:T(8,128)(2,1)S(1)}, bf16[24,1024]{1,0:T(8,128)(2,1)S(1)}, u32[]{:S(2)}, u32[]{:S(2)}) collective-permute-start(bf16[24,1024]{1,0:T(8,128)(2,1)S(1)} %get-tuple-element.155), channel_id=1, source_target_pairs={{0,2},{1,3},{2,0},{3,1},{4,6},{5,7},{6,4},{7,5},{8,10},{9,11},{10,... | collective-permute-start | bytes 147464 | tf_op jit(solution)/shard_map/ppermute | solution.py:605
  43.1 1.5 %collective-permute-start.13 = (bf16[96,1024]{1,0:T(8,128)(2,1)S(1)}, bf16[96,1024]{1,0:T(8,128)(2,1)S(1)}, u32[]{:S(2)}, u32[]{:S(2)}) collective-permute-start(bf16[96,1024]{1,0:T(8,128)(2,1)S(1)} %get-tuple-element.166), channel_id=1, source_target_pairs={{0,1},{1,0},{2,3},{3,2},{4,5},{5,4},{6,7},{7,6},{8,9},{9,8},{10,11... | collective-permute-start | bytes 589832 | tf_op jit(solution)/shard_map/ppermute | solution.py:605
  46.5 14.0 %collective-permute-start.14 = (bf16[24,2880]{1,0:T(8,128)(2,1)S(1)}, bf16[24,2880]{1,0:T(8,128)(2,1)S(1)}, u32[]{:S(2)}, u32[]{:S(2)}) collective-permute-start(bf16[24,2880]{1,0:T(8,128)(2,1)S(1)} %get-tuple-element.170), channel_id=1, source_target_pairs={{0,4},{1,5},{2,6},{3,7},{4,0},{5,1},{6,2},{7,3},{8,12},{9,13},{10,... | collective-permute-start | bytes 414728 | tf_op jit(solution)/shard_map/ppermute | solution.py:605
  49.5 11.0 %collective-permute-start.15 = (bf16[24,2880]{1,0:T(8,128)(2,1)S(1)}, bf16[24,2880]{1,0:T(8,128)(2,1)S(1)}, u32[]{:S(2)}, u32[]{:S(2)}) collective-permute-start(bf16[24,2880]{1,0:T(8,128)(2,1)S(1)} %get-tuple-element.171), channel_id=1, source_target_pairs={{0,6},{1,7},{2,4},{3,5},{4,2},{5,3},{6,0},{7,1},{8,14},{9,15},{10,... | collective-permute-start | bytes 414728 | tf_op jit(solution)/shard_map/ppermute | solution.py:605
  50.3 10.7 %collective-permute-start.16 = (bf16[24,2880]{1,0:T(8,128)(2,1)S(1)}, bf16[24,2880]{1,0:T(8,128)(2,1)S(1)}, u32[]{:S(2)}, u32[]{:S(2)}) collective-permute-start(bf16[24,2880]{1,0:T(8,128)(2,1)S(1)} %get-tuple-element.172), channel_id=1, source_target_pairs={{0,2},{1,3},{2,0},{3,1},{4,6},{5,7},{6,4},{7,5},{8,10},{9,11},{10,... | collective-permute-start | bytes 414728 | tf_op jit(solution)/shard_map/ppermute | solution.py:605
  58.6 3.9 %copy-start.1 = (bf16[2880,32]{0,1:T(8,128)(2,1)S(1)}, bf16[2880,32]{0,1:T(8,128)(2,1)}, u32[]{:S(2)}) copy-start(bf16[2880,32]{0,1:T(8,128)(2,1)} %param.27) | copy-start | bytes 552964
  58.6 3.9 %copy-start.3 = (f32[2880]{0:T(1024)S(1)}, f32[2880]{0:T(1024)}, u32[]{:S(2)}) copy-start(f32[2880]{0:T(1024)} %gain.1) | copy-start | bytes 34564
  61.1 1.4 %collective-permute-start.17 = (bf16[24,2880]{1,0:T(8,128)(2,1)S(1)}, bf16[24,2880]{1,0:T(8,128)(2,1)S(1)}, u32[]{:S(2)}, u32[]{:S(2)}) collective-permute-start(bf16[24,2880]{1,0:T(8,128)(2,1)S(1)} %add_convert_fusion.1.mine), channel_id=1, source_target_pairs={{0,1},{1,0},{2,3},{3,2},{4,5},{5,4},{6,7},{7,6},{8,9},{9,8},{10,11... | collective-permute-start | bytes 414728 | tf_op jit(solution)/shard_map/ppermute | solution.py:605
  69.2 1.6 %collective-permute-start.18 = (bf16[48,2880]{1,0:T(8,128)(2,1)S(1)}, bf16[48,2880]{1,0:T(8,128)(2,1)S(1)}, u32[]{:S(2)}, u32[]{:S(2)}) collective-permute-start(bf16[48,2880]{1,0:T(8,128)(2,1)S(1)} %shard_map.179.mine), channel_id=1, source_target_pairs={{0,1},{1,0},{2,3},{3,2},{4,5},{5,4},{6,7},{7,6},{8,9},{9,8},{10,11... | collective-permute-start | bytes 829448 | tf_op jit(solution)/shard_map/ppermute | solution.py:605
  71.5 13.8 %collective-permute-start.19 = (bf16[24,2880]{1,0:T(8,128)(2,1)S(1)}, bf16[24,2880]{1,0:T(8,128)(2,1)S(1)}, u32[]{:S(2)}, u32[]{:S(2)}) collective-permute-start(bf16[24,2880]{1,0:T(8,128)(2,1)S(1)} %get-tuple-element.194), channel_id=1, source_target_pairs={{0,4},{1,5},{2,6},{3,7},{4,0},{5,1},{6,2},{7,3},{8,12},{9,13},{10,... | collective-permute-start | bytes 414728 | tf_op jit(solution)/shard_map/ppermute | solution.py:605
  74.7 10.6 %collective-permute-start.20 = (bf16[24,2880]{1,0:T(8,128)(2,1)S(1)}, bf16[24,2880]{1,0:T(8,128)(2,1)S(1)}, u32[]{:S(2)}, u32[]{:S(2)}) collective-permute-start(bf16[24,2880]{1,0:T(8,128)(2,1)S(1)} %get-tuple-element.195), channel_id=1, source_target_pairs={{0,6},{1,7},{2,4},{3,5},{4,2},{5,3},{6,0},{7,1},{8,14},{9,15},{10,... | collective-permute-start | bytes 414728 | tf_op jit(solution)/shard_map/ppermute | solution.py:605
  76.2 10.0 %collective-permute-start.21 = (bf16[24,2880]{1,0:T(8,128)(2,1)S(1)}, bf16[24,2880]{1,0:T(8,128)(2,1)S(1)}, u32[]{:S(2)}, u32[]{:S(2)}) collective-permute-start(bf16[24,2880]{1,0:T(8,128)(2,1)S(1)} %get-tuple-element.196), channel_id=1, source_target_pairs={{0,2},{1,3},{2,0},{3,1},{4,6},{5,7},{6,4},{7,5},{8,10},{9,11},{10,... | collective-permute-start | bytes 414728 | tf_op jit(solution)/shard_map/ppermute | solution.py:605
